TPU v7x, 32 devices: a whole 2x2x4 slice. The times are simulated.
32 devices in a mesh: hap: 4 (over z), pos: 8 (over y, x, core).
Axes of the slice: x: 2, y: 2, z: 4, core: 2. Of those that a mesh axis runs over, the one named last changes fastest.
Arguments:
- haplo_rows: bfloat16 [12, 2048, 1024], P('hap', 'pos'), may hold values from -6 to 6
- norm_gain: float32 [1024], replicated, may hold values from 0.25 to 1.75
- query_row: bfloat16 [1024, 1024], replicated, may hold values from -0.1875 to 0.1875
- key_row: bfloat16 [1024, 1024], replicated, may hold values from -0.1875 to 0.1875
- value_row: bfloat16 [1024, 1024], replicated, may hold values from -0.1875 to 0.1875
- out_row: bfloat16 [1024, 1024], replicated, may hold values from -0.1875 to 0.1875
- head_gain: float32 [1024], replicated, may hold values from 0.25 to 1.75
- query_col: bfloat16 [1024, 1024], replicated, may hold values from -0.1875 to 0.1875
- key_col: bfloat16 [1024, 1024], replicated, may hold values from -0.1875 to 0.1875
- value_col: bfloat16 [1024, 1024], replicated, may hold values from -0.1875 to 0.1875
- out_col: bfloat16 [1024, 1024], replicated, may hold values from -0.1875 to 0.1875
- temper: float32 [16], replicated, may hold values from 4 to 16
Outputs:
- updated: bfloat16 [12, 2048, 1024], P('hap', 'pos')
All inputs are finite; a program needn't handle non-finite values.
Results may differ from a plain program's by a relative error of at most 0.01.
Values may be sent and summed in bfloat16 or wider, within the bound.
No kernel may reach another device: no remote copies, remote signals or barrier semaphores. Data moves between devices by JAX's collectives and lax.ppermute only.
A program may use at most 128 MiB of HBM per device.

v0:
```python
import jax
import jax.numpy as jnp
from jax import lax
from jax.sharding import PartitionSpec as P


def head_matrix(width, heads):
    head_dim = width // heads
    rows = lax.broadcasted_iota(jnp.int32, (width, heads), 0) // head_dim
    cols = lax.broadcasted_iota(jnp.int32, (width, heads), 1)
    return (rows == cols).astype(jnp.float32)


def head_sums(values, summing):
    shape = values.shape
    flat_values = values.reshape(-1, shape[-1])
    return jnp.dot(flat_values, summing, precision=lax.Precision.HIGHEST).reshape(
        shape[:-1] + (summing.shape[1],)
    )


def head_spread(values, summing):
    shape = values.shape
    flat_values = values.reshape(-1, shape[-1])
    return jnp.dot(flat_values, summing.T, precision=lax.Precision.HIGHEST).reshape(
        shape[:-1] + (summing.shape[0],)
    )


def project_flat(source, weight):
    count_a, count_b, width = source.shape
    flat_rows = source.reshape(count_a * count_b, width)
    return (
        jnp.dot(flat_rows, weight, preferred_element_type=jnp.float32)
        .astype(jnp.bfloat16)
        .reshape(count_a, count_b, weight.shape[1])
    )


def unit_flat(values, summing):
    widened = values.astype(jnp.float32)
    scales = lax.rsqrt(head_sums(widened * widened, summing) + 1e-06)
    return widened * head_spread(scales, summing)


def column_inputs(source, query_col, key_col, value_col, temper, summing):
    q_col = project_flat(source, query_col)
    k_col = project_flat(source, key_col)
    v_col = project_flat(source, value_col)
    temper_wide = jnp.dot(temper[None, :], summing.T, precision=lax.Precision.HIGHEST)[0]
    qn = (unit_flat(q_col, summing) * temper_wide).astype(jnp.bfloat16)
    kn = unit_flat(k_col, summing).astype(jnp.bfloat16)
    return (qn, kn, v_col)


def attend_flat(query_all, key_rows, value_rows, carry, summing):
    spread_bf = summing.T.astype(jnp.bfloat16)
    query_wide = query_all.astype(jnp.float32)

    def one_key(state, pair):
        key_one, value_one = pair
        product = query_wide * key_one.astype(jnp.float32)[None]
        scores = head_sums(product, summing)
        weight = jnp.exp(scores).astype(jnp.bfloat16)
        count_a, count_p, heads = weight.shape
        wide = jnp.dot(
            weight.reshape(count_a * count_p, heads), spread_bf, preferred_element_type=jnp.float32
        )
        wide = wide.reshape(count_a, count_p, summing.shape[0])
        summed = state[0] + wide * value_one.astype(jnp.float32)[None]
        total = state[1] + weight.astype(jnp.float32)
        return ((summed, total), None)

    result, _unused = lax.scan(one_key, carry, (key_rows, value_rows))
    return result


def finish_column(summed, total, summing):
    return (summed / head_spread(total, summing)).astype(jnp.bfloat16)


def local(
    haplo_rows,
    norm_gain,
    query_row,
    key_row,
    value_row,
    out_row,
    head_gain,
    query_col,
    key_col,
    value_col,
    out_col,
    temper,
):
    local_haps, local_pos, width = haplo_rows.shape
    heads = temper.shape[0]
    head_dim = width // heads
    summing = head_matrix(width, heads)
    inputs = haplo_rows.astype(jnp.float32)
    normed = (
        inputs * lax.rsqrt(jnp.mean(inputs * inputs, axis=-1, keepdims=True) + 1e-06) * norm_gain
    ).astype(jnp.bfloat16)
    q_row = project_flat(normed, query_row).astype(jnp.float32)
    k_row = project_flat(normed, key_row).astype(jnp.float32)
    v_row = project_flat(normed, value_row)
    query_plus = (jax.nn.elu(q_row) + 1.0).astype(jnp.bfloat16)
    query_minus = (jax.nn.elu(-q_row) + 1.0).astype(jnp.bfloat16)
    key_plus = (jax.nn.elu(k_row) + 1.0).astype(jnp.bfloat16)
    key_minus = (jax.nn.elu(-k_row) + 1.0).astype(jnp.bfloat16)
    partials = []
    for head in range(heads):
        lower = head * head_dim
        upper = lower + head_dim
        value_head = v_row[:, :, lower:upper]
        upper_state = jnp.einsum(
            "rpf,rpe->rfe",
            key_plus[:, :, lower:upper],
            value_head,
            preferred_element_type=jnp.float32,
        )
        lower_state = jnp.einsum(
            "rpf,rpe->rfe",
            key_minus[:, :, lower:upper],
            value_head,
            preferred_element_type=jnp.float32,
        )
        partials.append(jnp.concatenate([upper_state, lower_state], axis=1))
    partial_state = jnp.stack(partials, axis=1)
    state = lax.psum(
        partial_state.reshape(local_haps, heads * 2 * head_dim * head_dim).astype(jnp.bfloat16),
        "pos",
    ).astype(jnp.float32)
    state = state.reshape(local_haps, heads, 2 * head_dim, head_dim)
    pieces = []
    for head in range(heads):
        lower = head * head_dim
        upper = lower + head_dim
        head_state = state[:, head]
        along_head = jnp.einsum(
            "rpf,rfe->rpe",
            query_plus[:, :, lower:upper].astype(jnp.float32),
            head_state[:, :head_dim],
            precision=lax.Precision.HIGHEST,
        )
        along_head = along_head + jnp.einsum(
            "rpf,rfe->rpe",
            query_minus[:, :, lower:upper].astype(jnp.float32),
            head_state[:, head_dim:],
            precision=lax.Precision.HIGHEST,
        )
        pieces.append(
            along_head
            * lax.rsqrt(jnp.mean(along_head * along_head, axis=-1, keepdims=True) + 1e-06)
        )
    along = jnp.concatenate(pieces, axis=-1)
    row_mixed = (along * head_gain).astype(jnp.bfloat16)
    row_out = jnp.dot(
        row_mixed.reshape(local_haps * local_pos, width),
        out_row,
        preferred_element_type=jnp.float32,
    )
    moved_normed = lax.all_to_all(normed, "hap", split_axis=1, concat_axis=0, tiled=True)
    all_haps, pos_block, _unused = moved_normed.shape
    query_all, key_all, value_all = column_inputs(
        moved_normed, query_col, key_col, value_col, temper, summing
    )
    empty_sum = jnp.zeros((all_haps, pos_block, width), jnp.float32)
    empty_total = jnp.zeros((all_haps, pos_block, heads), jnp.float32)
    summed, total = attend_flat(query_all, key_all, value_all, (empty_sum, empty_total), summing)
    block_mixed = finish_column(summed, total, summing)
    returned = lax.all_to_all(block_mixed, "hap", split_axis=0, concat_axis=1, tiled=True)
    col_mixed = returned.reshape(local_haps * local_pos, width)
    col_out = jnp.dot(col_mixed, out_col, preferred_element_type=jnp.float32)
    merged = inputs.reshape(local_haps * local_pos, width) + row_out + col_out
    return merged.reshape(local_haps, local_pos, width).astype(jnp.bfloat16)


def solution(mesh):
    return jax.shard_map(
        local,
        mesh=mesh,
        in_specs=(P("hap", "pos", None), P(), P(), P(), P(), P(), P(), P(), P(), P(), P(), P()),
        out_specs=P("hap", "pos", None),
        check_vma=False,
    )
```

profile of v0, /device:TPU:0, one launch (start us, length us, event | category | flops | bytes accessed | tf_op | source)
XLA Modules:
  0.0 355.4 jit_solution(2688465623605317789)
XLA Ops:
  6.5 1.9 multiply_reduce_fusion
  10.1 2.7 copy.206
  12.9 6.3 %all-to-all-start = ((bf16[3,256,1024]{2,0,1:T(4,128)(2,1)}), bf16[3,256,1024]{2,0,1:T(4,128)(2,1)}, u32[]{:S(2)}, u32[]{:S(2)}) async-start(bf16[3,256,1024]{2,0,1:T(4,128)(2,1)} %copy.206), calls=%async_computation | async-start | bytes 4194304 | tf_op jit(solution)/shard_map/all_to_all | solution.py:163
  19.2 5.2 %convolution_convert_fusion.3 = bf16[768,1024]{1,0:T(8,128)(2,1)} fusion(bf16[768,1024]{1,0:T(8,128)(2,1)} %bitcast.224, bf16[1024,1024]{1,0:T(8,128)(2,1)} %param.18), kind=kOutput, calls=%fused_computation.58 | convolution fusion | flops 1611399168 | bytes 5242880 | tf_op jit(solution)/shard_map/dot_general | solution.py:34
  24.4 3.0 convolution_convert_fusion.4
  27.3 3.2 copy.169
  30.5 4.7 %fusion.28 = (bf16[3,256,1024]{1,2,0:T(8,128)(2,1)S(1)}, bf16[3,256,1024]{1,2,0:T(8,128)(2,1)S(1)}) fusion(f32[3,256,1024]{1,2,0:T(8,128)} %copy.169), kind=kLoop, calls=%fused_computation.36 | loop fusion | flops 8650752 | bytes 6291456 | tf_op jit(solution)/shard_map/convert_element_type | solution.py:109
  46.8 5.0 %convolution_convert_fusion.5 = bf16[768,1024]{1,0:T(8,128)(2,1)} fusion(bf16[768,1024]{1,0:T(8,128)(2,1)} %bitcast.225, bf16[1024,1024]{1,0:T(8,128)(2,1)} %param.16), kind=kOutput, calls=%fused_computation.60 | convolution fusion | flops 1611399168 | bytes 5242880 | tf_op jit(solution)/shard_map/dot_general | solution.py:34
  51.8 3.3 copy.166
  55.3 6.3 %fusion.34 = (bf16[3,256,1024]{1,2,0:T(8,128)(2,1)}, bf16[3,256,1024]{1,2,0:T(8,128)(2,1)}) fusion(f32[3,256,1024]{1,2,0:T(8,128)} %copy.166), kind=kLoop, calls=%fused_computation.42 | loop fusion | flops 8650752 | bytes 6291456 | tf_op jit(solution)/shard_map/convert_element_type | solution.py:108
  61.5 42.4 %all-reduce.2.cloned.1.call-done = bf16[3,16,128,64]{2,3,0,1:T(8,128)(2,1)} async-done(((bf16[3,16,128,64]{2,3,0,1:T(8,128)(2,1)}), bf16[3,16,128,64]{2,3,0,1:T(8,128)(2,1)}) %all-reduce.2.cloned.1.call-update) | async-done | bytes 786448 | tf_op jit(solution)/shard_map/psum | solution.py:130
  151.8 2.2 copy.207
  154.1 1.8 fusion.203
  155.9 2.0 fusion.42
  157.9 1.8 fusion.202
  159.7 2.4 fusion.43
  162.1 3.0 convolution_convert_fusion
  165.1 2.7 multiply_convert_fusion.1
  169.5 126.4 %while.15 = (s32[]{:T(128)}, f32[12,64,1024]{2,1,0:T(8,128)}, f32[12,64,16]{1,2,0:T(8,128)S(1)}, bf16[12,64,1024]{2,1,0:T(8,128)(2,1)}, f32[12,64,1024]{2,1,0:T(...) while((s32[]{:T(128)}, f32[12,64,1024]{2,1,0:T(8,128)}, ...), condition=%wide.region_19.20_spmd.clone.clone.clone, body=%wide.region_18.19_spmd.clone.clone.clone.sunk | while | flops 179601408 | bytes 10913916 | solution.py:74
  171.2 4.8 %select_add_fusion.4 = (f32[12,64,16]{1,2,0:T(8,128)S(1)}, bf16[12,64,16]{1,2,0:T(8,128)(2,1)S(1)}) fusion(f32[12,64,16]{1,2,0:T(8,128)S(1)} %get-tuple-element.308, pred[]{:T(512)S(6)} %compare.8, s32[1024]{0:T(1024)S(1)} %get-tuple-element.323, s32[1024]{0:T(1024)S(1)} %get-tuple-element.324, pred[1024]{0:T(1024)(128)(4,1)S(1)} %get-tuple-element.325, ...), kind=kOutput, calls=%fused_computation.10.clone.1 | convolution fusion | flops 151879680 | bytes 3539969 | tf_op jit(solution)/shard_map/while/body/eval_jaxpr/dot_general | solution.py:17
  176.1 2.2 select_add_fusion.5
  180.0 4.8 %select_add_fusion.4 = (f32[12,64,16]{1,2,0:T(8,128)S(1)}, bf16[12,64,16]{1,2,0:T(8,128)(2,1)S(1)}) fusion(f32[12,64,16]{1,2,0:T(8,128)S(1)} %get-tuple-element.308, pred[]{:T(512)S(6)} %compare.8, s32[1024]{0:T(1024)S(1)} %get-tuple-element.323, s32[1024]{0:T(1024)S(1)} %get-tuple-element.324, pred[1024]{0:T(1024)(128)(4,1)S(1)} %get-tuple-element.325, ...), kind=kOutput, calls=%fused_computation.10.clone.1 | convolution fusion | flops 151879680 | bytes 3539969 | tf_op jit(solution)/shard_map/while/body/eval_jaxpr/dot_general | solution.py:17
  184.9 4.1 %select_add_fusion.5 = f32[12,64,1024]{2,1,0:T(8,128)} fusion(f32[12,64,1024]{2,1,0:T(8,128)} %get-tuple-element.307, bf16[12,64,16]{1,2,0:T(8,128)(2,1)S(1)} %get-tuple-element.292, f32[64,1024]{1,0:T(8,128)S(1)} %get-tuple-element.293, pred[]{:T(512)S(6)} %compare.8, s32[1024]{0:T(1024)S(1)} %get-tuple-element.323, ...), kind=kOutput, calls=%fused_computation.2.clone.1 | convolution fusion | flops 27590656 | bytes 6587393 | tf_op jit(solution)/shard_map/while/body/eval_jaxpr/dot_general | solution.py:66
  190.7 4.8 %select_add_fusion.4 = (f32[12,64,16]{1,2,0:T(8,128)S(1)}, bf16[12,64,16]{1,2,0:T(8,128)(2,1)S(1)}) fusion(f32[12,64,16]{1,2,0:T(8,128)S(1)} %get-tuple-element.308, pred[]{:T(512)S(6)} %compare.8, s32[1024]{0:T(1024)S(1)} %get-tuple-element.323, s32[1024]{0:T(1024)S(1)} %get-tuple-element.324, pred[1024]{0:T(1024)(128)(4,1)S(1)} %get-tuple-element.325, ...), kind=kOutput, calls=%fused_computation.10.clone.1 | convolution fusion | flops 151879680 | bytes 3539969 | tf_op jit(solution)/shard_map/while/body/eval_jaxpr/dot_general | solution.py:17
  195.6 4.1 %select_add_fusion.5 = f32[12,64,1024]{2,1,0:T(8,128)} fusion(f32[12,64,1024]{2,1,0:T(8,128)} %get-tuple-element.307, bf16[12,64,16]{1,2,0:T(8,128)(2,1)S(1)} %get-tuple-element.292, f32[64,1024]{1,0:T(8,128)S(1)} %get-tuple-element.293, pred[]{:T(512)S(6)} %compare.8, s32[1024]{0:T(1024)S(1)} %get-tuple-element.323, ...), kind=kOutput, calls=%fused_computation.2.clone.1 | convolution fusion | flops 27590656 | bytes 6587393 | tf_op jit(solution)/shard_map/while/body/eval_jaxpr/dot_general | solution.py:66
  201.4 4.8 %select_add_fusion.4 = (f32[12,64,16]{1,2,0:T(8,128)S(1)}, bf16[12,64,16]{1,2,0:T(8,128)(2,1)S(1)}) fusion(f32[12,64,16]{1,2,0:T(8,128)S(1)} %get-tuple-element.308, pred[]{:T(512)S(6)} %compare.8, s32[1024]{0:T(1024)S(1)} %get-tuple-element.323, s32[1024]{0:T(1024)S(1)} %get-tuple-element.324, pred[1024]{0:T(1024)(128)(4,1)S(1)} %get-tuple-element.325, ...), kind=kOutput, calls=%fused_computation.10.clone.1 | convolution fusion | flops 151879680 | bytes 3539969 | tf_op jit(solution)/shard_map/while/body/eval_jaxpr/dot_general | solution.py:17
  206.2 4.1 %select_add_fusion.5 = f32[12,64,1024]{2,1,0:T(8,128)} fusion(f32[12,64,1024]{2,1,0:T(8,128)} %get-tuple-element.307, bf16[12,64,16]{1,2,0:T(8,128)(2,1)S(1)} %get-tuple-element.292, f32[64,1024]{1,0:T(8,128)S(1)} %get-tuple-element.293, pred[]{:T(512)S(6)} %compare.8, s32[1024]{0:T(1024)S(1)} %get-tuple-element.323, ...), kind=kOutput, calls=%fused_computation.2.clone.1 | convolution fusion | flops 27590656 | bytes 6587393 | tf_op jit(solution)/shard_map/while/body/eval_jaxpr/dot_general | solution.py:66
  212.1 4.8 %select_add_fusion.4 = (f32[12,64,16]{1,2,0:T(8,128)S(1)}, bf16[12,64,16]{1,2,0:T(8,128)(2,1)S(1)}) fusion(f32[12,64,16]{1,2,0:T(8,128)S(1)} %get-tuple-element.308, pred[]{:T(512)S(6)} %compare.8, s32[1024]{0:T(1024)S(1)} %get-tuple-element.323, s32[1024]{0:T(1024)S(1)} %get-tuple-element.324, pred[1024]{0:T(1024)(128)(4,1)S(1)} %get-tuple-element.325, ...), kind=kOutput, calls=%fused_computation.10.clone.1 | convolution fusion | flops 151879680 | bytes 3539969 | tf_op jit(solution)/shard_map/while/body/eval_jaxpr/dot_general | solution.py:17
  216.9 4.1 %select_add_fusion.5 = f32[12,64,1024]{2,1,0:T(8,128)} fusion(f32[12,64,1024]{2,1,0:T(8,128)} %get-tuple-element.307, bf16[12,64,16]{1,2,0:T(8,128)(2,1)S(1)} %get-tuple-element.292, f32[64,1024]{1,0:T(8,128)S(1)} %get-tuple-element.293, pred[]{:T(512)S(6)} %compare.8, s32[1024]{0:T(1024)S(1)} %get-tuple-element.323, ...), kind=kOutput, calls=%fused_computation.2.clone.1 | convolution fusion | flops 27590656 | bytes 6587393 | tf_op jit(solution)/shard_map/while/body/eval_jaxpr/dot_general | solution.py:66
  222.8 4.8 %select_add_fusion.4 = (f32[12,64,16]{1,2,0:T(8,128)S(1)}, bf16[12,64,16]{1,2,0:T(8,128)(2,1)S(1)}) fusion(f32[12,64,16]{1,2,0:T(8,128)S(1)} %get-tuple-element.308, pred[]{:T(512)S(6)} %compare.8, s32[1024]{0:T(1024)S(1)} %get-tuple-element.323, s32[1024]{0:T(1024)S(1)} %get-tuple-element.324, pred[1024]{0:T(1024)(128)(4,1)S(1)} %get-tuple-element.325, ...), kind=kOutput, calls=%fused_computation.10.clone.1 | convolution fusion | flops 151879680 | bytes 3539969 | tf_op jit(solution)/shard_map/while/body/eval_jaxpr/dot_general | solution.py:17
  227.6 4.1 %select_add_fusion.5 = f32[12,64,1024]{2,1,0:T(8,128)} fusion(f32[12,64,1024]{2,1,0:T(8,128)} %get-tuple-element.307, bf16[12,64,16]{1,2,0:T(8,128)(2,1)S(1)} %get-tuple-element.292, f32[64,1024]{1,0:T(8,128)S(1)} %get-tuple-element.293, pred[]{:T(512)S(6)} %compare.8, s32[1024]{0:T(1024)S(1)} %get-tuple-element.323, ...), kind=kOutput, calls=%fused_computation.2.clone.1 | convolution fusion | flops 27590656 | bytes 6587393 | tf_op jit(solution)/shard_map/while/body/eval_jaxpr/dot_general | solution.py:66
  233.5 4.8 %select_add_fusion.4 = (f32[12,64,16]{1,2,0:T(8,128)S(1)}, bf16[12,64,16]{1,2,0:T(8,128)(2,1)S(1)}) fusion(f32[12,64,16]{1,2,0:T(8,128)S(1)} %get-tuple-element.308, pred[]{:T(512)S(6)} %compare.8, s32[1024]{0:T(1024)S(1)} %get-tuple-element.323, s32[1024]{0:T(1024)S(1)} %get-tuple-element.324, pred[1024]{0:T(1024)(128)(4,1)S(1)} %get-tuple-element.325, ...), kind=kOutput, calls=%fused_computation.10.clone.1 | convolution fusion | flops 151879680 | bytes 3539969 | tf_op jit(solution)/shard_map/while/body/eval_jaxpr/dot_general | solution.py:17
  238.3 4.1 %select_add_fusion.5 = f32[12,64,1024]{2,1,0:T(8,128)} fusion(f32[12,64,1024]{2,1,0:T(8,128)} %get-tuple-element.307, bf16[12,64,16]{1,2,0:T(8,128)(2,1)S(1)} %get-tuple-element.292, f32[64,1024]{1,0:T(8,128)S(1)} %get-tuple-element.293, pred[]{:T(512)S(6)} %compare.8, s32[1024]{0:T(1024)S(1)} %get-tuple-element.323, ...), kind=kOutput, calls=%fused_computation.2.clone.1 | convolution fusion | flops 27590656 | bytes 6587393 | tf_op jit(solution)/shard_map/while/body/eval_jaxpr/dot_general | solution.py:66
  244.1 4.8 %select_add_fusion.4 = (f32[12,64,16]{1,2,0:T(8,128)S(1)}, bf16[12,64,16]{1,2,0:T(8,128)(2,1)S(1)}) fusion(f32[12,64,16]{1,2,0:T(8,128)S(1)} %get-tuple-element.308, pred[]{:T(512)S(6)} %compare.8, s32[1024]{0:T(1024)S(1)} %get-tuple-element.323, s32[1024]{0:T(1024)S(1)} %get-tuple-element.324, pred[1024]{0:T(1024)(128)(4,1)S(1)} %get-tuple-element.325, ...), kind=kOutput, calls=%fused_computation.10.clone.1 | convolution fusion | flops 151879680 | bytes 3539969 | tf_op jit(solution)/shard_map/while/body/eval_jaxpr/dot_general | solution.py:17
  249.0 4.1 %select_add_fusion.5 = f32[12,64,1024]{2,1,0:T(8,128)} fusion(f32[12,64,1024]{2,1,0:T(8,128)} %get-tuple-element.307, bf16[12,64,16]{1,2,0:T(8,128)(2,1)S(1)} %get-tuple-element.292, f32[64,1024]{1,0:T(8,128)S(1)} %get-tuple-element.293, pred[]{:T(512)S(6)} %compare.8, s32[1024]{0:T(1024)S(1)} %get-tuple-element.323, ...), kind=kOutput, calls=%fused_computation.2.clone.1 | convolution fusion | flops 27590656 | bytes 6587393 | tf_op jit(solution)/shard_map/while/body/eval_jaxpr/dot_general | solution.py:66
  254.8 4.8 %select_add_fusion.4 = (f32[12,64,16]{1,2,0:T(8,128)S(1)}, bf16[12,64,16]{1,2,0:T(8,128)(2,1)S(1)}) fusion(f32[12,64,16]{1,2,0:T(8,128)S(1)} %get-tuple-element.308, pred[]{:T(512)S(6)} %compare.8, s32[1024]{0:T(1024)S(1)} %get-tuple-element.323, s32[1024]{0:T(1024)S(1)} %get-tuple-element.324, pred[1024]{0:T(1024)(128)(4,1)S(1)} %get-tuple-element.325, ...), kind=kOutput, calls=%fused_computation.10.clone.1 | convolution fusion | flops 151879680 | bytes 3539969 | tf_op jit(solution)/shard_map/while/body/eval_jaxpr/dot_general | solution.py:17
  259.7 4.1 %select_add_fusion.5 = f32[12,64,1024]{2,1,0:T(8,128)} fusion(f32[12,64,1024]{2,1,0:T(8,128)} %get-tuple-element.307, bf16[12,64,16]{1,2,0:T(8,128)(2,1)S(1)} %get-tuple-element.292, f32[64,1024]{1,0:T(8,128)S(1)} %get-tuple-element.293, pred[]{:T(512)S(6)} %compare.8, s32[1024]{0:T(1024)S(1)} %get-tuple-element.323, ...), kind=kOutput, calls=%fused_computation.2.clone.1 | convolution fusion | flops 27590656 | bytes 6587393 | tf_op jit(solution)/shard_map/while/body/eval_jaxpr/dot_general | solution.py:66
  265.5 4.8 %select_add_fusion.4 = (f32[12,64,16]{1,2,0:T(8,128)S(1)}, bf16[12,64,16]{1,2,0:T(8,128)(2,1)S(1)}) fusion(f32[12,64,16]{1,2,0:T(8,128)S(1)} %get-tuple-element.308, pred[]{:T(512)S(6)} %compare.8, s32[1024]{0:T(1024)S(1)} %get-tuple-element.323, s32[1024]{0:T(1024)S(1)} %get-tuple-element.324, pred[1024]{0:T(1024)(128)(4,1)S(1)} %get-tuple-element.325, ...), kind=kOutput, calls=%fused_computation.10.clone.1 | convolution fusion | flops 151879680 | bytes 3539969 | tf_op jit(solution)/shard_map/while/body/eval_jaxpr/dot_general | solution.py:17
  270.4 4.1 %select_add_fusion.5 = f32[12,64,1024]{2,1,0:T(8,128)} fusion(f32[12,64,1024]{2,1,0:T(8,128)} %get-tuple-element.307, bf16[12,64,16]{1,2,0:T(8,128)(2,1)S(1)} %get-tuple-element.292, f32[64,1024]{1,0:T(8,128)S(1)} %get-tuple-element.293, pred[]{:T(512)S(6)} %compare.8, s32[1024]{0:T(1024)S(1)} %get-tuple-element.323, ...), kind=kOutput, calls=%fused_computation.2.clone.1 | convolution fusion | flops 27590656 | bytes 6587393 | tf_op jit(solution)/shard_map/while/body/eval_jaxpr/dot_general | solution.py:66
  276.2 4.8 %select_add_fusion.4 = (f32[12,64,16]{1,2,0:T(8,128)S(1)}, bf16[12,64,16]{1,2,0:T(8,128)(2,1)S(1)}) fusion(f32[12,64,16]{1,2,0:T(8,128)S(1)} %get-tuple-element.308, pred[]{:T(512)S(6)} %compare.8, s32[1024]{0:T(1024)S(1)} %get-tuple-element.323, s32[1024]{0:T(1024)S(1)} %get-tuple-element.324, pred[1024]{0:T(1024)(128)(4,1)S(1)} %get-tuple-element.325, ...), kind=kOutput, calls=%fused_computation.10.clone.1 | convolution fusion | flops 151879680 | bytes 3539969 | tf_op jit(solution)/shard_map/while/body/eval_jaxpr/dot_general | solution.py:17
  281.0 4.1 %select_add_fusion.5 = f32[12,64,1024]{2,1,0:T(8,128)} fusion(f32[12,64,1024]{2,1,0:T(8,128)} %get-tuple-element.307, bf16[12,64,16]{1,2,0:T(8,128)(2,1)S(1)} %get-tuple-element.292, f32[64,1024]{1,0:T(8,128)S(1)} %get-tuple-element.293, pred[]{:T(512)S(6)} %compare.8, s32[1024]{0:T(1024)S(1)} %get-tuple-element.323, ...), kind=kOutput, calls=%fused_computation.2.clone.1 | convolution fusion | flops 27590656 | bytes 6587393 | tf_op jit(solution)/shard_map/while/body/eval_jaxpr/dot_general | solution.py:66
  286.9 4.8 %select_add_fusion.4 = (f32[12,64,16]{1,2,0:T(8,128)S(1)}, bf16[12,64,16]{1,2,0:T(8,128)(2,1)S(1)}) fusion(f32[12,64,16]{1,2,0:T(8,128)S(1)} %get-tuple-element.308, pred[]{:T(512)S(6)} %compare.8, s32[1024]{0:T(1024)S(1)} %get-tuple-element.323, s32[1024]{0:T(1024)S(1)} %get-tuple-element.324, pred[1024]{0:T(1024)(128)(4,1)S(1)} %get-tuple-element.325, ...), kind=kOutput, calls=%fused_computation.10.clone.1 | convolution fusion | flops 151879680 | bytes 3539969 | tf_op jit(solution)/shard_map/while/body/eval_jaxpr/dot_general | solution.py:17
  291.7 4.1 %select_add_fusion.5 = f32[12,64,1024]{2,1,0:T(8,128)} fusion(f32[12,64,1024]{2,1,0:T(8,128)} %get-tuple-element.307, bf16[12,64,16]{1,2,0:T(8,128)(2,1)S(1)} %get-tuple-element.292, f32[64,1024]{1,0:T(8,128)S(1)} %get-tuple-element.293, pred[]{:T(512)S(6)} %compare.8, s32[1024]{0:T(1024)S(1)} %get-tuple-element.323, ...), kind=kOutput, calls=%fused_computation.2.clone.1 | convolution fusion | flops 27590656 | bytes 6587393 | tf_op jit(solution)/shard_map/while/body/eval_jaxpr/dot_general | solution.py:66
  295.9 4.6 %divide_convert_fusion = bf16[12,64,1024]{2,1,0:T(8,128)(2,1)} fusion(f32[12,64,1024]{2,1,0:T(8,128)} %get-tuple-element.48, f32[12,64,16]{1,2,0:T(8,128)S(1)} %get-tuple-element.49, s32[1024]{0:T(1024)S(1)} %get-tuple-element.332, s32[1024]{0:T(1024)S(1)} %get-tuple-element.333, pred[1024]{0:T(1024)(128)(4,1)S(1)} %get-tuple-element.337), kind=kOutput, calls=%fused_computation.46 | convolution fusion | flops 152600576 | bytes 4776960 | tf_op jit(solution)/shard_map/dot_general | solution.py:25
  300.4 4.8 %all-to-all-start.1 = ((bf16[12,64,1024]{2,1,0:T(8,128)(2,1)}), bf16[12,64,1024]{2,1,0:T(8,128)(2,1)S(1)}, u32[]{:S(2)}, u32[]{:S(2)}) async-start(bf16[12,64,1024]{2,1,0:T(8,128)(2,1)} %divide_convert_fusion), calls=%async_computation.1 | async-start | bytes 3145728 | tf_op jit(solution)/shard_map/all_to_all | solution.py:172
  308.2 3.6 %fusion.40 = f32[768,1024]{1,0:T(8,128)} fusion(bf16[1024,1024]{1,0:T(8,128)(2,1)S(1)} %copy-done.27, f32[768,1024]{0,1:T(8,128)S(1)} %constant_dynamic-update-slice_fusion.16, f32[1024]{0:T(1024)S(1)} %copy-done.28), kind=kOutput, calls=%fused_computation.61 | convolution fusion | flops 1612185600 | bytes 8392704 | tf_op jit(solution)/shard_map/dot_general | solution.py:158
  311.8 29.5 %all-to-all-done.1 = bf16[12,64,1024]{2,1,0:T(8,128)(2,1)S(1)} async-done(((bf16[12,64,1024]{2,1,0:T(8,128)(2,1)}), bf16[12,64,1024]{2,1,0:T(8,128)(2,1)S(1)}, u32[]{:S(2)}, u32[]{:S(2)}) %all-to-all-start.1) | async-done | bytes 1572896 | tf_op jit(solution)/shard_map/all_to_all | solution.py:172
  342.7 5.7 %fusion.36 = bf16[768,1024]{1,0:T(8,128)(2,1)} fusion(f32[768,1024]{1,0:T(8,128)} %fusion.40, bf16[768,1024]{1,0:T(8,128)(2,1)S(1)} %bitcast.236, bf16[1024,1024]{1,0:T(8,128)(2,1)} %param.24, bf16[3,256,1024]{2,1,0:T(8,128)(2,1)S(1)} %copy-done.3), kind=kOutput, calls=%fused_computation.45 | convolution fusion | flops 1613758464 | bytes 9961472 | tf_op jit(solution)/shard_map/dot_general | solution.py:174
  (232 shorter events, 87.3 us)
Async XLA Ops:
  6.5 147.6 %copy-start = (bf16[1024,1024]{1,0:T(8,128)(2,1)S(1)}, bf16[1024,1024]{1,0:T(8,128)(2,1)}, u32[]{:S(2)}) copy-start(bf16[1024,1024]{1,0:T(8,128)(2,1)} %param.21) | copy-start | bytes 6291460
  6.5 2.0 copy-start.2
  6.5 2.0 copy-start.23
  9.0 1.1 copy-start.4
  12.9 138.9 %all-to-all-start = ((bf16[3,256,1024]{2,0,1:T(4,128)(2,1)}), bf16[3,256,1024]{2,0,1:T(4,128)(2,1)}, u32[]{:S(2)}, u32[]{:S(2)}) async-start(bf16[3,256,1024]{2,0,1:T(4,128)(2,1)} %copy.206), calls=%async_computation | async-start | bytes 4194304 | tf_op jit(solution)/shard_map/all_to_all | solution.py:163
  19.2 84.8 %all-reduce.2.cloned.1.call-start = ((), (), s32[]{:S(2)}) async-start(), calls=%async_computation.2 | async-start | bytes 1572864 | tf_op jit(solution)/shard_map/psum | solution.py:130
  19.2 5.2 %copy-start.5 = (bf16[3,256,1024]{2,1,0:T(8,128)(2,1)S(1)}, bf16[3,256,1024]{2,1,0:T(8,128)(2,1)}, u32[]{:S(2)}) copy-start(bf16[3,256,1024]{2,1,0:T(8,128)(2,1)} %copy-done.4) | copy-start | bytes 4718596
  19.2 5.2 %copy-start.24 = (bf16[1024,1024]{1,0:T(8,128)(2,1)S(1)}, bf16[1024,1024]{1,0:T(8,128)(2,1)}, u32[]{:S(2)}) copy-start(bf16[1024,1024]{1,0:T(8,128)(2,1)} %param.17) | copy-start | bytes 6291460
  30.5 4.7 %copy-start.30 = (bf16[768,1024]{1,0:T(8,128)(2,1)S(1)}, bf16[768,1024]{1,0:T(8,128)(2,1)}, u32[]{:S(2)}) copy-start(bf16[768,1024]{1,0:T(8,128)(2,1)} %convolution_convert_fusion.3) | copy-start | bytes 4718596
  45.8 0.9 copy-start.6
  51.8 3.3 copy-start.29
  155.9 2.0 copy-start.25
  159.7 2.4 copy-start.26
  300.4 4.8 %copy-start.22 = (f32[3,8,8,256]{3,2,0,1:T(8,128)S(1)}, f32[3,8,8,256]{3,2,0,1:T(8,128)}, u32[]{:S(2)}) copy-start(f32[3,8,8,256]{3,2,0,1:T(8,128)} %copy.226) | copy-start | bytes 589828
  300.4 4.9 %copy-start.21 = (f32[3,8,8,256]{3,2,0,1:T(8,128)S(1)}, f32[3,8,8,256]{3,2,0,1:T(8,128)}, u32[]{:S(2)}) copy-start(f32[3,8,8,256]{3,2,0,1:T(8,128)} %copy.227) | copy-start | bytes 589828
  300.4 4.9 %copy-start.20 = (f32[3,8,8,256]{3,2,0,1:T(8,128)S(1)}, f32[3,8,8,256]{3,2,0,1:T(8,128)}, u32[]{:S(2)}) copy-start(f32[3,8,8,256]{3,2,0,1:T(8,128)} %copy.228) | copy-start | bytes 589828
  300.4 4.9 %copy-start.19 = (f32[3,8,8,256]{3,2,0,1:T(8,128)S(1)}, f32[3,8,8,256]{3,2,0,1:T(8,128)}, u32[]{:S(2)}) copy-start(f32[3,8,8,256]{3,2,0,1:T(8,128)} %copy.229) | copy-start | bytes 589828
  300.4 40.9 %all-to-all-start.1 = ((bf16[12,64,1024]{2,1,0:T(8,128)(2,1)}), bf16[12,64,1024]{2,1,0:T(8,128)(2,1)S(1)}, u32[]{:S(2)}, u32[]{:S(2)}) async-start(bf16[12,64,1024]{2,1,0:T(8,128)(2,1)} %divide_convert_fusion), calls=%async_computation.1 | async-start | bytes 3145728 | tf_op jit(solution)/shard_map/all_to_all | solution.py:172
  305.2 0.9 copy-start.18
  305.2 1.0 copy-start.17
  305.2 1.1 copy-start.16
  305.2 1.2 copy-start.15
  305.2 1.2 copy-start.14
  305.3 1.3 copy-start.13
  305.3 1.3 copy-start.12
  305.4 1.3 copy-start.11
  306.1 1.0 copy-start.10
  306.2 1.0 copy-start.9
  306.3 1.0 copy-start.8
  306.4 1.0 copy-start.7
  306.5 1.7 copy-start.27
  306.5 1.7 copy-start.28
  341.3 1.4 copy-start.3
  342.7 5.7 %copy-start.1 = (bf16[1024,1024]{1,0:T(8,128)(2,1)S(1)}, bf16[1024,1024]{1,0:T(8,128)(2,1)}, u32[]{:S(2)}) copy-start(bf16[1024,1024]{1,0:T(8,128)(2,1)} %param.21) | copy-start | bytes 6291460
Sparse Core Ops, SparseCore 0:
  46.9 57.0 all-reduce.1
where the time goes:
time: 362 us; the launch traced here: 355 us
  matrix products  192 us (53%)
  waiting for transfers between devices  71.9 us (20%)
  other arithmetic  36 us (10%)
  local copies, waits for them, and re-layouts  30.1 us (8%)
  between operations  14.5 us (4%)
  starting transfers between devices  11.1 us (3%)
    dot_general x14, matrix products, head_sums(): jnp.dot(flat_values, summing, precision=lax.Precision.HIGHEST)  62.3 us
    dot_general x12, matrix products, one_key(): jnp.dot(weight.reshape(count_a * count_p, heads), spread_bf, preferred_el...  47.6 us
    psum x1, waiting for transfers between devices, local(): lax.psum(partial_state.reshape(local_haps, heads * 2 * head_dim * head_di...  42.4 us
    all_to_all x1, waiting for transfers between devices, local(): lax.all_to_all(block_mixed, 'hap', split_axis=0, concat_axis=1, tiled=True)  29.5 us
    mul x12, other arithmetic, one_key(): summed = state[0] + wide * value_one.astype(jnp.float32)[None]  20.7 us
    dot_general x6, matrix products, project_flat(): jnp.dot(flat_rows, weight, preferred_element_type=jnp.float32)  19.7 us
    dot_general x16, matrix products, local(): jnp.einsum('rpf,rfe->rpe', query_minus[:, :, lower:upper].astype(jnp.floa...  18.2 us
    dot_general x16, matrix products, local(): jnp.einsum('rpf,rfe->rpe', query_plus[:, :, lower:upper].astype(jnp.float...  16.6 us
  transfers between devices with their start and end apart: 3, of which 2 were waited for; matrix products, arithmetic and copies ran while one was open for 26% of the time, Pallas kernels for 0%

commit v1 on v0

v1 whole, which is shorter than its diff:
```python
import functools

import jax
import jax.numpy as jnp
from jax import lax
from jax.experimental import pallas as pl
from jax.experimental.pallas import tpu as pltpu
from jax.sharding import PartitionSpec as P

EPS = 1e-06
LANES = 128
TILE = 16
F32 = jnp.float32
BF16 = jnp.bfloat16
VMEM_LIMIT = 40 * 1024 * 1024
COLUMN_COSTS = (200, 30)
FINISH_COSTS = (30, 0)


def last_dims(left, right):
    return lax.dot_general(left, right, (((1,), (1,)), ((), ())), preferred_element_type=F32)


def first_dims(left, right):
    return lax.dot_general(left, right, (((0,), (0,)), ((), ())), preferred_element_type=F32)


def plain(left, right):
    return jnp.dot(left, right, preferred_element_type=F32)


def lane_of(shape):
    return lax.broadcasted_iota(jnp.int32, shape, len(shape) - 1)


def group_ones(size, head_dim):
    rows = lax.broadcasted_iota(jnp.int32, (size, size), 0) // head_dim
    cols = lax.broadcasted_iota(jnp.int32, (size, size), 1) // head_dim
    return jnp.where(rows == cols, 1.0, 0.0).astype(BF16)


def head_square_sums(values, ones):
    size = ones.shape[0]
    parts = []
    for start in range(0, values.shape[1], size):
        piece = values[:, start : start + size]
        square = piece * piece
        high = square.astype(BF16)
        low = (square - high.astype(F32)).astype(BF16)
        parts.append(plain(high, ones) + plain(low, ones))
    return jnp.concatenate(parts, axis=1) if len(parts) > 1 else parts[0]


def feature_pair(values):
    small = jnp.exp(-jnp.abs(values))
    up = values > 0
    plus = jnp.where(up, values + 1.0, small).astype(BF16)
    minus = jnp.where(up, small, 1.0 - values).astype(BF16)
    return plus, minus


def pack_kernel(places, place_ref, rows_ref, gain_ref, *outs):
    z = place_ref[0]
    gain = gain_ref[...]
    for (c, k), (index, slot) in places.items():
        block = rows_ref[0, z ^ k, c].astype(F32)
        scale = lax.rsqrt(jnp.mean(block * block, axis=-1, keepdims=True) + EPS)
        outs[index][slot, 0] = (block * scale * gain).astype(BF16)


def row_kernel(head_dim, places, *refs):
    wq_ref, wk_ref, wv_ref, q_ref, state_ref = refs[-5:]
    rows = jnp.concatenate([refs[index][slot, 0] for index, slot in places.values()], axis=0)
    keys = plain(rows, wk_ref[...]).astype(BF16)
    values = plain(rows, wv_ref[...]).astype(BF16)
    first_head = lane_of((head_dim, 2 * LANES)) % LANES < head_dim
    for pair in range(keys.shape[1] // LANES):
        lower = pair * LANES
        plus, minus = feature_pair(keys[:, lower : lower + LANES].astype(F32))
        features = jnp.concatenate([plus, minus], axis=1)
        state = first_dims(values[:, lower : lower + LANES], features)
        folded = jnp.where(first_head, state[:head_dim], state[head_dim:])
        state_ref[pair, 0] = folded.astype(BF16)
    q_ref[0] = plain(rows, wq_ref[...]).astype(BF16)


def along_kernel(head_dim, order, place_ref, rows_ref, q_ref, state_ref, gain_ref, wo_ref, out_ref, mixed):
    z = place_ref[0]
    first_head = lane_of((head_dim, 2 * LANES)) % LANES < head_dim
    ones = group_ones(2 * LANES, head_dim)
    alongs = []
    for pair in range(state_ref.shape[0]):
        lower = pair * LANES
        plus, minus = feature_pair(q_ref[0, :, lower : lower + LANES].astype(F32))
        features = jnp.concatenate([plus, minus], axis=1)
        folded = state_ref[pair, 0]
        none = jnp.zeros_like(folded)
        state = jnp.concatenate(
            [jnp.where(first_head, folded, none), jnp.where(first_head, none, folded)], axis=0
        )
        alongs.append(last_dims(features, state))
        if pair % 2 == 1:
            lower -= LANES
            wide = jnp.concatenate(alongs[-2:], axis=1)
            mean = head_square_sums(wide, ones) * (1.0 / head_dim)
            scaled = wide * lax.rsqrt(mean + EPS) * gain_ref[:, lower : lower + 2 * LANES]
            mixed[:, lower : lower + 2 * LANES] = scaled.astype(BF16)
    row_out = plain(mixed[...], wo_ref[...])
    depth = rows_ref.shape[3]
    for i, (c, k) in enumerate(order):
        out_ref[0, i] = rows_ref[0, z ^ k, c].astype(F32) + row_out[i * depth : (i + 1) * depth]


def column_kernel(head_dim, count, temper_ref, wq_ref, wk_ref, wv_ref, *refs):
    blocks = refs[:count]
    outs = refs[-3 - count : -3]
    q_all, k_all, v_all = refs[-3:]
    _one, haps, depth, width = blocks[0].shape
    rows = jnp.concatenate([block[0, r] for block in blocks for r in range(haps)], axis=0)
    shape = q_all.shape
    ones = group_ones(2 * LANES, head_dim)
    q = plain(rows, wq_ref[...]).astype(BF16).astype(F32)
    q = q * lax.rsqrt(head_square_sums(q, ones) + EPS) * temper_ref[...]
    q_all[...] = q.astype(BF16).reshape(shape)
    k = plain(rows, wk_ref[...]).astype(BF16).astype(F32)
    k = k * lax.rsqrt(head_square_sums(k, ones) + EPS)
    k_all[...] = k.astype(BF16).reshape(shape)
    v_all[...] = plain(rows, wv_ref[...]).astype(BF16).reshape(shape)
    all_haps = shape[0]
    many = all_haps * TILE
    same = (
        lax.broadcasted_iota(jnp.int32, (many, many), 0) % TILE
        == lax.broadcasted_iota(jnp.int32, (many, many), 1) % TILE
    )
    first_head = lane_of((many, LANES)) < head_dim
    none = jnp.zeros((many, LANES), BF16)
    one = jnp.ones((many, LANES), BF16)
    for start in range(0, depth, TILE):
        for lower in range(0, width, LANES):
            at = (slice(None), slice(start, start + TILE), slice(lower, lower + LANES))
            query = q_all[at].reshape(many, LANES)
            key = k_all[at].reshape(many, LANES)
            value = v_all[at].reshape(many, LANES)
            score_a = last_dims(jnp.where(first_head, query, none), key)
            score_b = last_dims(jnp.where(first_head, none, query), key)
            weight_a = jnp.where(same, jnp.exp(score_a), 0.0).astype(BF16)
            weight_b = jnp.where(same, jnp.exp(score_b), 0.0).astype(BF16)
            sum_a = plain(weight_a, jnp.where(first_head, value, one))
            sum_b = plain(weight_b, jnp.where(first_head, one, value))
            summed = jnp.where(first_head, sum_a, sum_b)
            total = pltpu.roll(jnp.where(first_head, sum_b, sum_a), head_dim, 1)
            result = (summed / total).astype(BF16).reshape(all_haps, TILE, LANES)
            for k in range(count):
                outs[k][0, :, start : start + TILE, lower : lower + LANES] = result[
                    k * haps : (k + 1) * haps
                ]


def finish_kernel(pieces, order, place_ref, acc_ref, wo_ref, *refs):
    mixed = refs[: len(pieces)]
    out_ref, acc, result, acc_sems, out_sems = refs[-5:]
    z = place_ref[0]
    _one, haps, depth, _width = mixed[0].shape
    loads = [
        pltpu.make_async_copy(acc_ref.at[:, order.index(piece)], acc.at[i], acc_sems.at[i])
        for i, piece in enumerate(pieces)
    ]
    for load in loads:
        load.start()
    flat = jnp.concatenate([block[0, r] for block in mixed for r in range(haps)], axis=0)
    col_out = plain(flat, wo_ref[...])
    stores = []
    for i, (c, k) in enumerate(pieces):
        loads[i].wait()
        for r in range(haps):
            lower = (i * haps + r) * depth
            result[i, r] = (acc[i, r] + col_out[lower : lower + depth]).astype(BF16)
        store = pltpu.make_async_copy(result.at[i], out_ref.at[:, z ^ k, c], out_sems.at[i])
        store.start()
        stores.append(store)
    for store in stores:
        store.wait()


def whole(array):
    zeros = (0,) * array.ndim
    return pl.BlockSpec(array.shape, lambda *_: zeros)


def once(array):
    zeros = (0,) * array.ndim
    return pl.BlockSpec(array.shape, lambda *_: zeros, pipeline_mode=pl.Buffered(1))


SCALARS = pl.BlockSpec(memory_space=pltpu.SMEM)
PARAMS = pltpu.CompilerParams(vmem_limit_bytes=VMEM_LIMIT)


def cost(micros):
    return pl.CostEstimate(flops=int(micros * 1e9), bytes_accessed=1, transcendentals=0)


def local(
    sizes,
    haplo_rows,
    norm_gain,
    query_row,
    key_row,
    value_row,
    out_row,
    head_gain,
    query_col,
    key_col,
    value_col,
    out_col,
    temper,
):
    n, m = sizes
    haps, length, width = haplo_rows.shape
    heads = temper.shape[0]
    head_dim = width // heads
    owned = length // n
    chunks = 2 if owned % (2 * TILE) == 0 else 1
    depth = owned // chunks
    pairs = width // LANES
    place = lax.axis_index("hap").astype(jnp.int32)[None]
    rows5 = haplo_rows.reshape(haps, n, chunks, depth, width)
    gain_flat = norm_gain[None, :]
    head_gain_flat = head_gain[None, :]
    temper_flat = jnp.repeat(temper, head_dim)[None, :]
    anywhere = pl.BlockSpec(memory_space=pl.ANY)

    def exchange(array, k):
        return lax.ppermute(array, "hap", [(i, i ^ k) for i in range(n)])

    order = [(c, k) for c in range(chunks) for k in range(n)]
    places, lengths = {}, []
    for c, k in order:
        if k == 1 and c > 0:
            places[c, k] = (places[0, 1][0], c)
        else:
            places[c, k] = (len(lengths), 0)
            lengths.append(chunks if k == 1 else 1)
    shapes = [jax.ShapeDtypeStruct((many, haps, depth, width), BF16) for many in lengths]
    hap_specs = [
        pl.BlockSpec((many, 1, depth, width), lambda r: (0, r, 0, 0)) for many in lengths
    ]
    rows_spec = pl.BlockSpec((1, n, chunks, depth, width), lambda r: (r, 0, 0, 0, 0))

    def piece_spec(c, k):
        slot = places[c, k][1]
        return pl.BlockSpec((1, haps, depth, width), lambda *_: (slot, 0, 0, 0))

    normed = pl.pallas_call(
        functools.partial(pack_kernel, places),
        grid=(haps,),
        in_specs=[SCALARS, rows_spec, whole(gain_flat)],
        out_specs=hap_specs,
        out_shape=shapes,
        compiler_params=PARAMS,
        cost_estimate=cost(0),
        name="pack",
    )(place, rows5, gain_flat)

    def send_all(arrays):
        got = {}
        sent = list(arrays)
        for c, k in order[1:] if n > 1 else []:
            index, slot = places[c, k]
            if k > 0 and slot == 0:
                sent[index] = exchange(arrays[index], k)
        return sent

    arrived = send_all(normed)

    full_rows = jax.ShapeDtypeStruct((haps, length, width), BF16)
    row_spec = pl.BlockSpec((1, length, width), lambda r: (r, 0, 0))
    state_spec = pl.BlockSpec((pairs, 1, head_dim, 2 * LANES), lambda r: (0, r, 0, 0))
    state_shape = (pairs, haps, head_dim, 2 * LANES)
    q_row, state = pl.pallas_call(
        functools.partial(row_kernel, head_dim, places),
        grid=(haps,),
        in_specs=hap_specs + [once(query_row)] * 3,
        out_specs=[row_spec, state_spec],
        out_shape=[full_rows, jax.ShapeDtypeStruct(state_shape, BF16)],
        compiler_params=PARAMS,
        cost_estimate=cost(0),
        name="row",
    )(*normed, query_row, key_row, value_row)

    shares = state.reshape(m, -1, 2 * LANES)
    shares = lax.all_to_all(shares, "pos", split_axis=0, concat_axis=0, tiled=True)
    share = jnp.sum(shares.astype(F32), axis=0).astype(BF16)

    column_outs = None
    for c in range(chunks):
        blocks = [arrived[places[c, k][0]] for k in range(n)]
        extra = []
        if c > 0:
            blocks, _unused = lax.optimization_barrier((blocks, share))
            extra = [column_outs[places[0, 1][0]]] if n > 1 else []
        every = pltpu.VMEM((haps * n, depth, width), BF16)
        results = pl.pallas_call(
            functools.partial(column_kernel, head_dim, n),
            grid=(1,),
            in_specs=[whole(temper_flat)]
            + [once(query_col)] * 3
            + [piece_spec(c, k) for k in range(n)]
            + [anywhere] * len(extra),
            out_specs=[piece_spec(c, k) for k in range(n)],
            out_shape=[shapes[places[c, k][0]] for k in range(n)],
            scratch_shapes=[every] * 3,
            input_output_aliases={4 + n: 1} if extra else {},
            compiler_params=PARAMS,
            cost_estimate=cost(COLUMN_COSTS[c]),
            name="column",
        )(temper_flat, query_col, key_col, value_col, *blocks, *extra)
        if column_outs is None:
            column_outs = [None] * len(shapes)
        for k in range(n):
            column_outs[places[c, k][0]] = results[k]
    returned = send_all(column_outs)

    state = lax.all_gather(share, "pos", axis=0, tiled=True).reshape(state_shape)
    acc = pl.pallas_call(
        functools.partial(along_kernel, head_dim, order),
        grid=(haps,),
        in_specs=[SCALARS, rows_spec, row_spec, state_spec, whole(head_gain_flat), once(out_row)],
        out_specs=pl.BlockSpec((1, len(order), depth, width), lambda r: (r, 0, 0, 0)),
        out_shape=jax.ShapeDtypeStruct((haps, len(order), depth, width), F32),
        scratch_shapes=[pltpu.VMEM((length, width), BF16)],
        compiler_params=PARAMS,
        cost_estimate=cost(0),
        name="along",
    )(place, rows5, q_row, state, head_gain_flat, out_row)

    early = [(0, k) for k in range(n) if k != 1] if chunks > 1 else []
    late = [piece for piece in order if piece not in early]
    updated = None
    for pieces in [early, late] if early else [late]:
        extra = [] if updated is None else [updated]
        count = len(pieces)
        updated = pl.pallas_call(
            functools.partial(finish_kernel, pieces, order),
            grid=(1,),
            in_specs=[SCALARS, anywhere, once(out_col)]
            + [piece_spec(c, k) for c, k in pieces]
            + [anywhere] * len(extra),
            out_specs=anywhere,
            out_shape=jax.ShapeDtypeStruct(rows5.shape, BF16),
            scratch_shapes=[
                pltpu.VMEM((count, haps, depth, width), F32),
                pltpu.VMEM((count, haps, depth, width), BF16),
                pltpu.SemaphoreType.DMA((count,)),
                pltpu.SemaphoreType.DMA((count,)),
            ],
            input_output_aliases={3 + count: 0} if extra else {},
            compiler_params=PARAMS,
            cost_estimate=cost(FINISH_COSTS[0 if pieces is early else 1]),
            name="finish",
        )(place, acc, out_col, *[returned[places[c, k][0]] for c, k in pieces], *extra)
    return updated.reshape(haps, length, width)


def solution(mesh):
    sizes = (mesh.shape["hap"], mesh.shape["pos"])
    return jax.shard_map(
        functools.partial(local, sizes),
        mesh=mesh,
        in_specs=(P("hap", "pos", None), P(), P(), P(), P(), P(), P(), P(), P(), P(), P(), P()),
        out_specs=P("hap", "pos", None),
        check_vma=False,
    )
```

time: 362 us -> 90.4 us (0.25); the launches traced: 355 us -> 89.8 us
  matrix products: 192 us -> 0 us
  waiting for transfers between devices: 71.9 us -> 0.03 us
  other arithmetic: 36 us -> 1.24 us
  Pallas kernels: 0 us -> 33.9 us
  starting transfers between devices: 11.1 us -> 26.4 us
  between operations: 14.5 us -> 0.39 us
  local copies, waits for them, and re-layouts: 30.1 us -> 17.2 us
  blocking collectives: 0 us -> 10.6 us
    dot_general x102 -> x0, matrix products: 192 us -> none  [the longest x14 62.3 us: head_sums(): jnp.dot(flat_values, summing, precision=lax.Precision.HIGHEST)]
    psum x1 -> x0, waiting for transfers between devices: 42.4 us -> none  [local(): lax.psum(partial_state.reshape(local_haps, heads * 2 * head_dim * head_di...]
    pallas_call x0 -> x7, Pallas kernels: none -> 33.9 us  [the longest x2 15.1 us: local(): pl.pallas_call(functools.partial(column_kernel, head_dim, n), grid=(1,),...]
    all_to_all x2 -> x1, waiting for transfers between devices: 29.5 us -> 0.01 us  [local(): lax.all_to_all(shares, 'pos', split_axis=0, concat_axis=0, tiled=True)]
    ppermute x0 -> x10, starting transfers between devices: none -> 22 us  [exchange(): return lax.ppermute(array, 'hap', [(i, i ^ k) for i in range(n)])]
    mul x12 -> x0, other arithmetic: 20.7 us -> none  [one_key(): summed = state[0] + wide * value_one.astype(jnp.float32)[None]]
    convert_element_type x3 -> x0, other arithmetic: 11.4 us -> none  [the longest x1 6.25 us: local(): query_minus = (jax.nn.elu(-q_row) + 1.0).astype(jnp.bfloat16)]
    concatenate x17 -> x0, local copies, waits for them, and re-layouts: 11.1 us -> none  [local(): along = jnp.concatenate(pieces, axis=-1)]
  transfers between devices with their start and end apart: 3 -> 11, of which waited for: 2 -> 0; matrix products, arithmetic and copies ran while one was open for 26% -> 2% of each run, Pallas kernels for 0% -> 33%
where the time goes in v1:
time: 90.4 us; the launch traced here: 89.8 us
  Pallas kernels  33.9 us (38%)
  starting transfers between devices  26.4 us (29%)
  local copies, waits for them, and re-layouts  17.2 us (19%)
  blocking collectives  10.6 us (12%)
  other arithmetic  1.24 us (1%)
    ppermute x10, starting transfers between devices, exchange(): return lax.ppermute(array, 'hap', [(i, i ^ k) for i in range(n)])  22 us
    unnamed x40, local copies, waits for them, and re-layouts  17.1 us
    pallas_call x2, Pallas kernels, local(): pl.pallas_call(functools.partial(column_kernel, head_dim, n), grid=(1,),...  15.1 us
    all_gather x1, blocking collectives, local(): lax.all_gather(share, 'pos', axis=0, tiled=True).reshape(state_shape)  10.6 us
    pallas_call x1, Pallas kernels, local(): pl.pallas_call(functools.partial(row_kernel, head_dim, places), grid=(hap...  7.91 us
    pallas_call x1, Pallas kernels, local(): pl.pallas_call(functools.partial(along_kernel, head_dim, order), grid=(ha...  4.7 us
    pallas_call x2, Pallas kernels, local(): pl.pallas_call(functools.partial(finish_kernel, pieces, order), grid=(1,)...  4.43 us
    all_to_all x1, starting transfers between devices, local(): lax.all_to_all(shares, 'pos', split_axis=0, concat_axis=0, tiled=True)  4.39 us
  transfers between devices with their start and end apart: 11, of which 0 were waited for; matrix products, arithmetic and copies ran while one was open for 2% of the time, Pallas kernels for 33%

profile of v1, /device:TPU:0, one launch (start us, length us, event | category | flops | bytes accessed | tf_op | source)
XLA Modules:
  0.0 89.8 jit_solution(4600000423106726735)
XLA Ops:
  0.0 1.4 %copy-done = bf16[3,256,1024]{2,1,0:T(8,128)(2,1)S(1)} copy-done((bf16[3,256,1024]{2,1,0:T(8,128)(2,1)S(1)}, bf16[3,256,1024]{2,1,0:T(8,128)(2,1)}, u32[]{:S(2)}) %copy-start) | copy-done | bytes 1572888
  1.4 0.7 copy-done.9
  2.1 1.7 %pack.1 = (bf16[1,3,32,1024]{3,2,1,0:T(8,128)(2,1)S(1)}, bf16[2,3,32,1024]{3,2,1,0:T(8,128)(2,1)S(1)}, bf16[1,3,32,1024]{3,2,1,0:T(8,128)(2,1)S(1)}, bf16[1,3,32...) custom-call(s32[1]{0:T(128)} %bitcast.place_ref, ...), custom_call_target="tpu_custom_call" | custom-call | bytes 1 | tf_op jit(solution)/shard_map/pack/pallas_call | solution.py:254
  3.8 3.0 %collective-permute-start = (bf16[2,3,32,1024]{3,2,1,0:T(8,128)(2,1)S(1)}, bf16[2,3,32,1024]{3,2,1,0:T(8,128)(2,1)S(1)}, u32[]{:S(2)}, u32[]{:S(2)}) collective-permute-start(bf16[2,3,32,1024]{3,2,1,0:T(8,128)(2,1)S(1)} %get-tuple-element.27.refs_1_), channel_id=1, source_target_pairs={{0,8},{8,0},{16,24},{24,16},{1,9},{9,1},{17,25},{25,17},{2,10},{10... | collective-permute-start | bytes 1179656 | tf_op jit(solution)/shard_map/ppermute | solution.py:234
  6.9 2.6 %collective-permute-start.3 = (bf16[1,3,32,1024]{3,2,1,0:T(8,128)(2,1)S(1)}, bf16[1,3,32,1024]{3,2,1,0:T(8,128)(2,1)S(1)}, u32[]{:S(2)}, u32[]{:S(2)}) collective-permute-start(bf16[1,3,32,1024]{3,2,1,0:T(8,128)(2,1)S(1)} %get-tuple-element.28.refs_2_), channel_id=1, source_target_pairs={{0,16},{8,24},{16,0},{24,8},{1,17},{9,25},{17,1},{25,9},{2,18},{10... | collective-permute-start | bytes 589832 | tf_op jit(solution)/shard_map/ppermute | solution.py:234
  9.4 0.0 collective-permute-start.4
  9.5 1.9 %collective-permute-start.1 = (bf16[1,3,32,1024]{3,2,1,0:T(8,128)(2,1)}, bf16[1,3,32,1024]{3,2,1,0:T(8,128)(2,1)}, u32[]{:S(2)}, u32[]{:S(2)}) collective-permute-start(bf16[1,3,32,1024]{3,2,1,0:T(8,128)(2,1)} %get-tuple-element.31.refs_5_), channel_id=1, source_target_pairs={{0,16},{8,24},{16,0},{24,8},{1,17},{9,25},{17,1},{25,9},{2,18},{10... | collective-permute-start | bytes 589832 | tf_op jit(solution)/shard_map/ppermute | solution.py:234
  11.4 1.9 %collective-permute-start.2 = (bf16[1,3,32,1024]{3,2,1,0:T(8,128)(2,1)}, bf16[1,3,32,1024]{3,2,1,0:T(8,128)(2,1)}, u32[]{:S(2)}, u32[]{:S(2)}) collective-permute-start(bf16[1,3,32,1024]{3,2,1,0:T(8,128)(2,1)} %get-tuple-element.32.refs_6_), channel_id=1, source_target_pairs={{0,24},{8,16},{16,8},{24,0},{1,25},{9,17},{17,9},{25,1},{2,26},{10... | collective-permute-start | bytes 589832 | tf_op jit(solution)/shard_map/ppermute | solution.py:234
  13.3 1.6 %copy-done.3 = bf16[1024,1024]{1,0:T(8,128)(2,1)S(1)} copy-done((bf16[1024,1024]{1,0:T(8,128)(2,1)S(1)}, bf16[1024,1024]{1,0:T(8,128)(2,1)}, u32[]{:S(2)}) %copy-start.3) | copy-done | bytes 2097176
  14.9 1.6 %copy-done.4 = bf16[1024,1024]{1,0:T(8,128)(2,1)S(1)} copy-done((bf16[1024,1024]{1,0:T(8,128)(2,1)S(1)}, bf16[1024,1024]{1,0:T(8,128)(2,1)}, u32[]{:S(2)}) %copy-start.4) | copy-done | bytes 2097176
  16.5 1.6 %copy-done.5 = bf16[1024,1024]{1,0:T(8,128)(2,1)S(1)} copy-done((bf16[1024,1024]{1,0:T(8,128)(2,1)S(1)}, bf16[1024,1024]{1,0:T(8,128)(2,1)}, u32[]{:S(2)}) %copy-start.5) | copy-done | bytes 2097176
  18.1 7.9 %row.1 = (bf16[3,256,1024]{2,1,0:T(8,128)(2,1)S(1)}, bf16[8,3,64,256]{3,2,1,0:T(8,128)(2,1)}) custom-call(bf16[1,3,32,1024]{3,2,1,0:T(8,128)(2,1)S(1)} %get-tuple-element.26.refs_0_, bf16[2,3,32,1024]{3,2,1,0:T(8,128)(2,1)S(1)} %get-tuple-element.27.refs_1_, bf16[1,3,32,1024]{3,2,1,0:T(8,128)(2,1)S(1)} %get-tuple-element.28.refs_2_, ...), custom_call_target="tpu_custom_call" | custom-call | bytes 1 | tf_op jit(solution)/shard_map/row/pallas_call | solution.py:280
  26.0 4.4 %all-to-all-start = ((bf16[8,192,256]{2,1,0:T(8,128)(2,1)}), bf16[8,192,256]{2,1,0:T(8,128)(2,1)}, u32[]{:S(2)}, u32[]{:S(2)}) async-start(bf16[8,192,256]{2,1,0:T(8,128)(2,1)} %bitcast.3), calls=%async_computation | async-start | bytes 1572864 | tf_op jit(solution)/shard_map/all_to_all | solution.py:292
  30.4 0.1 broadcast_in_dim.15
  30.4 0.1 broadcast_in_dim_reshape.3.temper_ref
  30.5 0.0 collective-permute-done.3.refs_2_
  30.5 0.0 collective-permute-done.4.refs_3_
  30.5 0.0 collective-permute-done.refs_1_
  30.5 0.0 copy-start.11
  30.6 1.6 %copy-done.11 = bf16[1024,1024]{1,0:T(8,128)(2,1)S(1)} copy-done((bf16[1024,1024]{1,0:T(8,128)(2,1)S(1)}, bf16[1024,1024]{1,0:T(8,128)(2,1)}, u32[]{:S(2)}) %copy-start.11) | copy-done | bytes 2097176
  32.1 1.6 %copy-done.13 = bf16[1024,1024]{1,0:T(8,128)(2,1)S(1)} copy-done((bf16[1024,1024]{1,0:T(8,128)(2,1)S(1)}, bf16[1024,1024]{1,0:T(8,128)(2,1)}, u32[]{:S(2)}) %copy-start.13) | copy-done | bytes 2097176
  33.7 1.6 %copy-done.15 = bf16[1024,1024]{1,0:T(8,128)(2,1)S(1)} copy-done((bf16[1024,1024]{1,0:T(8,128)(2,1)S(1)}, bf16[1024,1024]{1,0:T(8,128)(2,1)}, u32[]{:S(2)}) %copy-start.15) | copy-done | bytes 2097176
  35.3 6.9 %column.2 = (bf16[1,3,32,1024]{3,2,1,0:T(8,128)(2,1)S(1)}, bf16[2,3,32,1024]{3,2,1,0:T(8,128)(2,1)S(1)}, bf16[1,3,32,1024]{3,2,1,0:T(8,128)(2,1)S(1)}, bf16[1,3,32,1024]{3,2,1,0:T(8,128)(2,1)S(1)}) custom-call(f32[1,1024]{1,0:T(1,128)S(1)} %broadcast_in_dim_reshape.3.temper_ref, bf16[1024,1024]{1,0:T(8,128)(2,1)S(1)} %copy-done.11, ...), custom_call_target="tpu_custom_call" | custom-call | flops 199999995904 | bytes 1 | tf_op jit(solution)/shard_map/column/pallas_call | solution.py:303
  42.3 0.7 copy-done.17
  42.9 7.7 %collective-permute-start.8 = (bf16[1,3,32,1024]{3,2,1,0:T(8,128)(2,1)S(1)}, bf16[1,3,32,1024]{3,2,1,0:T(8,128)(2,1)S(1)}, u32[]{:S(2)}, u32[]{:S(2)}) collective-permute-start(bf16[1,3,32,1024]{3,2,1,0:T(8,128)(2,1)S(1)} %get-tuple-element.45), channel_id=1, source_target_pairs={{0,16},{8,24},{16,0},{24,8},{1,17},{9,25},{17,1},{25,9},{2,18},{10... | collective-permute-start | bytes 589832 | tf_op jit(solution)/shard_map/ppermute | solution.py:234
  50.6 1.3 %collective-permute-start.9 = (bf16[1,3,32,1024]{3,2,1,0:T(8,128)(2,1)S(1)}, bf16[1,3,32,1024]{3,2,1,0:T(8,128)(2,1)S(1)}, u32[]{:S(2)}, u32[]{:S(2)}) collective-permute-start(bf16[1,3,32,1024]{3,2,1,0:T(8,128)(2,1)S(1)} %get-tuple-element.46), channel_id=1, source_target_pairs={{0,24},{8,16},{16,8},{24,0},{1,25},{9,17},{17,9},{25,1},{2,26},{10... | collective-permute-start | bytes 589832 | tf_op jit(solution)/shard_map/ppermute | solution.py:234
  52.0 0.0 all-to-all-done
  52.0 1.2 %reduce_sum.12 = bf16[192,256]{1,0:T(8,128)(2,1)S(1)} reduce(bf16[8,192,256]{2,1,0:T(8,128)(2,1)} %all-to-all-done, bf16[]{:T(256)} %constant.7.clone.1), dimensions={0}, to_apply=%region_0.0 | reduce | flops 344064 | bytes 884738 | tf_op jit(solution)/shard_map/reduce_sum | solution.py:293
  53.2 0.0 collective-permute-done.1.refs_2_
  53.2 0.0 collective-permute-done.2.refs_3_
  53.2 0.0 copy-start.12
  53.3 1.6 %copy-done.12 = bf16[1024,1024]{1,0:T(8,128)(2,1)S(1)} copy-done((bf16[1024,1024]{1,0:T(8,128)(2,1)S(1)}, bf16[1024,1024]{1,0:T(8,128)(2,1)}, u32[]{:S(2)}) %copy-start.12) | copy-done | bytes 2097176
  54.8 1.6 %copy-done.14 = bf16[1024,1024]{1,0:T(8,128)(2,1)S(1)} copy-done((bf16[1024,1024]{1,0:T(8,128)(2,1)S(1)}, bf16[1024,1024]{1,0:T(8,128)(2,1)}, u32[]{:S(2)}) %copy-start.14) | copy-done | bytes 2097176
  56.4 1.6 %copy-done.16 = bf16[1024,1024]{1,0:T(8,128)(2,1)S(1)} copy-done((bf16[1024,1024]{1,0:T(8,128)(2,1)S(1)}, bf16[1024,1024]{1,0:T(8,128)(2,1)}, u32[]{:S(2)}) %copy-start.16) | copy-done | bytes 2097176
  58.0 8.2 %column.3 = (bf16[1,3,32,1024]{3,2,1,0:T(8,128)(2,1)S(1)}, bf16[2,3,32,1024]{3,2,1,0:T(8,128)(2,1)S(1)}, bf16[1,3,32,1024]{3,2,1,0:T(8,128)(2,1)S(1)}, bf16[1,3,32,1024]{3,2,1,0:T(8,128)(2,1)S(1)}) custom-call(f32[1,1024]{1,0:T(1,128)S(1)} %broadcast_in_dim_reshape.3.temper_ref, bf16[1024,1024]{1,0:T(8,128)(2,1)S(1)} %copy-done.12, ...), custom_call_target="tpu_custom_call", output_to_operand_aliasing={{1}: (8, {})} | custom-call | flops 30000001024 | bytes 1 | tf_op jit(solution)/shard_map/column/pallas_call | solution.py:303
  66.2 0.1 collective-permute-start.6
  66.3 2.6 %collective-permute-start.7 = (bf16[1,3,32,1024]{3,2,1,0:T(8,128)(2,1)S(1)}, bf16[1,3,32,1024]{3,2,1,0:T(8,128)(2,1)S(1)}, u32[]{:S(2)}, u32[]{:S(2)}) collective-permute-start(bf16[1,3,32,1024]{3,2,1,0:T(8,128)(2,1)S(1)} %get-tuple-element.43), channel_id=1, source_target_pairs={{0,24},{8,16},{16,8},{24,0},{1,25},{9,17},{17,9},{25,1},{2,26},{10... | collective-permute-start | bytes 589832 | tf_op jit(solution)/shard_map/ppermute | solution.py:234
  68.8 0.9 %collective-permute-start.5 = (bf16[2,3,32,1024]{3,2,1,0:T(8,128)(2,1)S(1)}, bf16[2,3,32,1024]{3,2,1,0:T(8,128)(2,1)S(1)}, u32[]{:S(2)}, u32[]{:S(2)}) collective-permute-start(bf16[2,3,32,1024]{3,2,1,0:T(8,128)(2,1)S(1)} %get-tuple-element.40), channel_id=1, source_target_pairs={{0,8},{8,0},{16,24},{24,16},{1,9},{9,1},{17,25},{25,17},{2,10},{10... | collective-permute-start | bytes 1179656 | tf_op jit(solution)/shard_map/ppermute | solution.py:234
  69.8 10.6 %all_gather.3 = bf16[1536,256]{1,0:T(8,128)(2,1)S(1)} all-gather(bf16[192,256]{1,0:T(8,128)(2,1)S(1)} %reduce_sum.12), channel_id=1, replica_groups=mesh['hap'=4,'pos'=8] {'pos'}, dimensions={0}, use_global_device_ids=true | all-gather | bytes 884736 | tf_op jit(solution)/shard_map/all_gather | solution.py:324
  80.4 0.0 copy-done.10
  80.4 4.7 %along.1.acc_ref = f32[3,8,32,1024]{3,2,1,0:T(8,128)S(1)} custom-call(s32[1]{0:T(128)} %bitcast.place_ref, bf16[3,4,2,32,1024]{4,3,2,1,0:T(8,128)(2,1)S(1)} %bitcast.8, bf16[3,256,1024]{2,1,0:T(8,128)(2,1)S(1)} %get-tuple-element.33.q_ref, bf16[8,3,64,256]{3,2,1,0:T(8,128)(2,1)S(1)} %bitcast.9, f32[1,1024]{1,0:T(1,128)S(1)} %bitcast.11, ...), custom_call_target="tpu_custom_call" | custom-call | bytes 1 | tf_op jit(solution)/shard_map/along/pallas_call | solution.py:325
  85.1 0.0 collective-permute-done.8.refs_1_
  85.1 0.0 collective-permute-done.9.refs_2_
  85.1 1.9 %finish.2.refs_5_ = bf16[3,4,2,32,1024]{4,3,2,1,0:T(8,128)(2,1)} custom-call(s32[1]{0:T(128)} %bitcast.place_ref, f32[3,8,32,1024]{3,2,1,0:T(8,128)S(1)} %along.1.acc_ref, bf16[1024,1024]{1,0:T(8,128)(2,1)S(1)} %copy-done.2, bf16[1,3,32,1024]{3,2,1,0:T(8,128)(2,1)S(1)} %copy-done.18, bf16[1,3,32,1024]{3,2,1,0:T(8,128)(2,1)S(1)} %collective-permute-done.8.refs_1_, ...), custom_call_target="tpu_custom_call" | custom-call | flops 30000001024 | bytes 1 | tf_op jit(solution)/shard_map/finish/pallas_call | solution.py:343
  87.0 0.0 collective-permute-done.6.refs_3_
  87.0 0.0 collective-permute-done.7.refs_4_
  87.0 0.0 collective-permute-done.5.refs_0_.refs_2_
  87.0 2.6 %finish.3 = bf16[3,4,2,32,1024]{4,3,2,1,0:T(8,128)(2,1)} custom-call(s32[1]{0:T(128)} %bitcast.place_ref, f32[3,8,32,1024]{3,2,1,0:T(8,128)S(1)} %along.1.acc_ref, bf16[1024,1024]{1,0:T(8,128)(2,1)S(1)} %copy-done.2, bf16[2,3,32,1024]{3,2,1,0:T(8,128)(2,1)S(1)} %collective-permute-done.5.refs_0_.refs_2_, ...), custom_call_target="tpu_custom_call", output_to_operand_aliasing={{}: (8, {})} | custom-call | bytes 1 | tf_op jit(solution)/shard_map/finish/pallas_call | solution.py:343
  (25 shorter events, 0.0 us)
Async XLA Ops:
  0.0 1.4 %copy-start = (bf16[3,256,1024]{2,1,0:T(8,128)(2,1)S(1)}, bf16[3,256,1024]{2,1,0:T(8,128)(2,1)}, u32[]{:S(2)}) copy-start(bf16[3,256,1024]{2,1,0:T(8,128)(2,1)} %param.12) | copy-start | bytes 4718596
  1.4 0.7 copy-start.9
  3.8 22.1 %copy-start.7 = (bf16[1,3,32,1024]{3,2,1,0:T(8,128)(2,1)}, bf16[1,3,32,1024]{3,2,1,0:T(8,128)(2,1)S(1)}, u32[]{:S(2)}) copy-start(bf16[1,3,32,1024]{3,2,1,0:T(8,128)(2,1)S(1)} %get-tuple-element.35.refs_4_.refs_0_) | copy-start | bytes 589828
  3.8 26.7 %collective-permute-start = (bf16[2,3,32,1024]{3,2,1,0:T(8,128)(2,1)S(1)}, bf16[2,3,32,1024]{3,2,1,0:T(8,128)(2,1)S(1)}, u32[]{:S(2)}, u32[]{:S(2)}) collective-permute-start(bf16[2,3,32,1024]{3,2,1,0:T(8,128)(2,1)S(1)} %get-tuple-element.27.refs_1_), channel_id=1, source_target_pairs={{0,8},{8,0},{16,24},{24,16},{1,9},{9,1},{17,25},{25,17},{2,10},{10... | collective-permute-start | bytes 1179656 | tf_op jit(solution)/shard_map/ppermute | solution.py:234
  6.9 23.7 %collective-permute-start.3 = (bf16[1,3,32,1024]{3,2,1,0:T(8,128)(2,1)S(1)}, bf16[1,3,32,1024]{3,2,1,0:T(8,128)(2,1)S(1)}, u32[]{:S(2)}, u32[]{:S(2)}) collective-permute-start(bf16[1,3,32,1024]{3,2,1,0:T(8,128)(2,1)S(1)} %get-tuple-element.28.refs_2_), channel_id=1, source_target_pairs={{0,16},{8,24},{16,0},{24,8},{1,17},{9,25},{17,1},{25,9},{2,18},{10... | collective-permute-start | bytes 589832 | tf_op jit(solution)/shard_map/ppermute | solution.py:234
  9.4 21.1 %collective-permute-start.4 = (bf16[1,3,32,1024]{3,2,1,0:T(8,128)(2,1)S(1)}, bf16[1,3,32,1024]{3,2,1,0:T(8,128)(2,1)S(1)}, u32[]{:S(2)}, u32[]{:S(2)}) collective-permute-start(bf16[1,3,32,1024]{3,2,1,0:T(8,128)(2,1)S(1)} %get-tuple-element.29.refs_3_), channel_id=1, source_target_pairs={{0,24},{8,16},{16,8},{24,0},{1,25},{9,17},{17,9},{25,1},{2,26},{10... | collective-permute-start | bytes 589832 | tf_op jit(solution)/shard_map/ppermute | solution.py:234
  9.5 43.8 %collective-permute-start.1 = (bf16[1,3,32,1024]{3,2,1,0:T(8,128)(2,1)}, bf16[1,3,32,1024]{3,2,1,0:T(8,128)(2,1)}, u32[]{:S(2)}, u32[]{:S(2)}) collective-permute-start(bf16[1,3,32,1024]{3,2,1,0:T(8,128)(2,1)} %get-tuple-element.31.refs_5_), channel_id=1, source_target_pairs={{0,16},{8,24},{16,0},{24,8},{1,17},{9,25},{17,1},{25,9},{2,18},{10... | collective-permute-start | bytes 589832 | tf_op jit(solution)/shard_map/ppermute | solution.py:234
  11.4 41.9 %collective-permute-start.2 = (bf16[1,3,32,1024]{3,2,1,0:T(8,128)(2,1)}, bf16[1,3,32,1024]{3,2,1,0:T(8,128)(2,1)}, u32[]{:S(2)}, u32[]{:S(2)}) collective-permute-start(bf16[1,3,32,1024]{3,2,1,0:T(8,128)(2,1)} %get-tuple-element.32.refs_6_), channel_id=1, source_target_pairs={{0,24},{8,16},{16,8},{24,0},{1,25},{9,17},{17,9},{25,1},{2,26},{10... | collective-permute-start | bytes 589832 | tf_op jit(solution)/shard_map/ppermute | solution.py:234
  13.3 1.6 %copy-start.3 = (bf16[1024,1024]{1,0:T(8,128)(2,1)S(1)}, bf16[1024,1024]{1,0:T(8,128)(2,1)}, u32[]{:S(2)}) copy-start(bf16[1024,1024]{1,0:T(8,128)(2,1)} %refs_7_.1) | copy-start | bytes 6291460
  14.9 1.6 %copy-start.4 = (bf16[1024,1024]{1,0:T(8,128)(2,1)S(1)}, bf16[1024,1024]{1,0:T(8,128)(2,1)}, u32[]{:S(2)}) copy-start(bf16[1024,1024]{1,0:T(8,128)(2,1)} %refs_8_.1) | copy-start | bytes 6291460
  16.5 1.6 %copy-start.5 = (bf16[1024,1024]{1,0:T(8,128)(2,1)S(1)}, bf16[1024,1024]{1,0:T(8,128)(2,1)}, u32[]{:S(2)}) copy-start(bf16[1024,1024]{1,0:T(8,128)(2,1)} %refs_9_.1) | copy-start | bytes 6291460
  18.1 12.3 %copy-start.19 = (f32[16]{0:T(128)S(1)}, f32[16]{0:T(128)}, u32[]{:S(2)}) copy-start(f32[16]{0:T(128)} %param.23) | copy-start | bytes 196
  26.0 26.0 %all-to-all-start = ((bf16[8,192,256]{2,1,0:T(8,128)(2,1)}), bf16[8,192,256]{2,1,0:T(8,128)(2,1)}, u32[]{:S(2)}, u32[]{:S(2)}) async-start(bf16[8,192,256]{2,1,0:T(8,128)(2,1)} %bitcast.3), calls=%async_computation | async-start | bytes 1572864 | tf_op jit(solution)/shard_map/all_to_all | solution.py:292
  30.5 1.6 %copy-start.11 = (bf16[1024,1024]{1,0:T(8,128)(2,1)S(1)}, bf16[1024,1024]{1,0:T(8,128)(2,1)}, u32[]{:S(2)}) copy-start(bf16[1024,1024]{1,0:T(8,128)(2,1)} %wq_ref.3) | copy-start | bytes 6291460
  32.1 1.6 %copy-start.13 = (bf16[1024,1024]{1,0:T(8,128)(2,1)S(1)}, bf16[1024,1024]{1,0:T(8,128)(2,1)}, u32[]{:S(2)}) copy-start(bf16[1024,1024]{1,0:T(8,128)(2,1)} %wk_ref.3) | copy-start | bytes 6291460
  33.7 1.6 %copy-start.15 = (bf16[1024,1024]{1,0:T(8,128)(2,1)S(1)}, bf16[1024,1024]{1,0:T(8,128)(2,1)}, u32[]{:S(2)}) copy-start(bf16[1024,1024]{1,0:T(8,128)(2,1)} %wv_ref.3) | copy-start | bytes 6291460
  35.3 17.9 %copy-start.8 = (bf16[1,3,32,1024]{3,2,1,0:T(8,128)(2,1)S(1)}, bf16[1,3,32,1024]{3,2,1,0:T(8,128)(2,1)}, u32[]{:S(2)}) copy-start(bf16[1,3,32,1024]{3,2,1,0:T(8,128)(2,1)} %copy-done.7) | copy-start | bytes 589828
  42.3 0.7 copy-start.17
  42.9 42.2 %collective-permute-start.8 = (bf16[1,3,32,1024]{3,2,1,0:T(8,128)(2,1)S(1)}, bf16[1,3,32,1024]{3,2,1,0:T(8,128)(2,1)S(1)}, u32[]{:S(2)}, u32[]{:S(2)}) collective-permute-start(bf16[1,3,32,1024]{3,2,1,0:T(8,128)(2,1)S(1)} %get-tuple-element.45), channel_id=1, source_target_pairs={{0,16},{8,24},{16,0},{24,8},{1,17},{9,25},{17,1},{25,9},{2,18},{10... | collective-permute-start | bytes 589832 | tf_op jit(solution)/shard_map/ppermute | solution.py:234
  50.6 34.5 %collective-permute-start.9 = (bf16[1,3,32,1024]{3,2,1,0:T(8,128)(2,1)S(1)}, bf16[1,3,32,1024]{3,2,1,0:T(8,128)(2,1)S(1)}, u32[]{:S(2)}, u32[]{:S(2)}) collective-permute-start(bf16[1,3,32,1024]{3,2,1,0:T(8,128)(2,1)S(1)} %get-tuple-element.46), channel_id=1, source_target_pairs={{0,24},{8,16},{16,8},{24,0},{1,25},{9,17},{17,9},{25,1},{2,26},{10... | collective-permute-start | bytes 589832 | tf_op jit(solution)/shard_map/ppermute | solution.py:234
  53.2 1.6 %copy-start.12 = (bf16[1024,1024]{1,0:T(8,128)(2,1)S(1)}, bf16[1024,1024]{1,0:T(8,128)(2,1)}, u32[]{:S(2)}) copy-start(bf16[1024,1024]{1,0:T(8,128)(2,1)} %wq_ref.3) | copy-start | bytes 6291460
  54.8 1.6 %copy-start.14 = (bf16[1024,1024]{1,0:T(8,128)(2,1)S(1)}, bf16[1024,1024]{1,0:T(8,128)(2,1)}, u32[]{:S(2)}) copy-start(bf16[1024,1024]{1,0:T(8,128)(2,1)} %wk_ref.3) | copy-start | bytes 6291460
  56.4 1.6 %copy-start.16 = (bf16[1024,1024]{1,0:T(8,128)(2,1)S(1)}, bf16[1024,1024]{1,0:T(8,128)(2,1)}, u32[]{:S(2)}) copy-start(bf16[1024,1024]{1,0:T(8,128)(2,1)} %wv_ref.3) | copy-start | bytes 6291460
  58.0 22.3 %copy-start.1 = (bf16[3,256,1024]{2,1,0:T(8,128)(2,1)S(1)}, bf16[3,256,1024]{2,1,0:T(8,128)(2,1)}, u32[]{:S(2)}) copy-start(bf16[3,256,1024]{2,1,0:T(8,128)(2,1)} %param.12) | copy-start | bytes 4718596
  58.0 22.3 %copy-start.6 = (bf16[1024,1024]{1,0:T(8,128)(2,1)S(1)}, bf16[1024,1024]{1,0:T(8,128)(2,1)}, u32[]{:S(2)}) copy-start(bf16[1024,1024]{1,0:T(8,128)(2,1)} %wo_ref.3) | copy-start | bytes 6291460
  58.0 22.3 %copy-start.10 = (f32[1024]{0:T(1024)S(1)}, f32[1024]{0:T(1024)}, u32[]{:S(2)}) copy-start(f32[1024]{0:T(1024)} %param.18) | copy-start | bytes 12292
  66.2 20.8 %collective-permute-start.6 = (bf16[1,3,32,1024]{3,2,1,0:T(8,128)(2,1)S(1)}, bf16[1,3,32,1024]{3,2,1,0:T(8,128)(2,1)S(1)}, u32[]{:S(2)}, u32[]{:S(2)}) collective-permute-start(bf16[1,3,32,1024]{3,2,1,0:T(8,128)(2,1)S(1)} %get-tuple-element.42), channel_id=1, source_target_pairs={{0,16},{8,24},{16,0},{24,8},{1,17},{9,25},{17,1},{25,9},{2,18},{10... | collective-permute-start | bytes 589832 | tf_op jit(solution)/shard_map/ppermute | solution.py:234
  66.3 20.7 %collective-permute-start.7 = (bf16[1,3,32,1024]{3,2,1,0:T(8,128)(2,1)S(1)}, bf16[1,3,32,1024]{3,2,1,0:T(8,128)(2,1)S(1)}, u32[]{:S(2)}, u32[]{:S(2)}) collective-permute-start(bf16[1,3,32,1024]{3,2,1,0:T(8,128)(2,1)S(1)} %get-tuple-element.43), channel_id=1, source_target_pairs={{0,24},{8,16},{16,8},{24,0},{1,25},{9,17},{17,9},{25,1},{2,26},{10... | collective-permute-start | bytes 589832 | tf_op jit(solution)/shard_map/ppermute | solution.py:234
  68.8 18.2 %collective-permute-start.5 = (bf16[2,3,32,1024]{3,2,1,0:T(8,128)(2,1)S(1)}, bf16[2,3,32,1024]{3,2,1,0:T(8,128)(2,1)S(1)}, u32[]{:S(2)}, u32[]{:S(2)}) collective-permute-start(bf16[2,3,32,1024]{3,2,1,0:T(8,128)(2,1)S(1)} %get-tuple-element.40), channel_id=1, source_target_pairs={{0,8},{8,0},{16,24},{24,16},{1,9},{9,1},{17,25},{25,17},{2,10},{10... | collective-permute-start | bytes 1179656 | tf_op jit(solution)/shard_map/ppermute | solution.py:234
  80.4 4.8 %copy-start.2 = (bf16[1024,1024]{1,0:T(8,128)(2,1)S(1)}, bf16[1024,1024]{1,0:T(8,128)(2,1)}, u32[]{:S(2)}) copy-start(bf16[1024,1024]{1,0:T(8,128)(2,1)} %wo_ref.5) | copy-start | bytes 6291460
  80.4 4.8 %copy-start.18 = (bf16[1,3,32,1024]{3,2,1,0:T(8,128)(2,1)S(1)}, bf16[1,3,32,1024]{3,2,1,0:T(8,128)(2,1)}, u32[]{:S(2)}) copy-start(bf16[1,3,32,1024]{3,2,1,0:T(8,128)(2,1)} %copy-done.17) | copy-start | bytes 589828

commit v2 on v1

--- a/solution.py
+++ b/solution.py
@@ -12,7 +12,13 @@
 TILE = 16
 F32 = jnp.float32
 BF16 = jnp.bfloat16
-VMEM_LIMIT = 40 * 1024 * 1024
+VMEM_MIB = 24
+PACK_COST = 10
+ROW_COST = 20
+QUERY_COST = 5
+SHARE_COST = 5
+TIE_C1 = 'state'
+ALONG_COST = 0
 COLUMN_COSTS = (200, 30)
 FINISH_COSTS = (30, 0)
 
@@ -59,8 +65,13 @@
     return plus, minus
 
 
-def pack_kernel(places, place_ref, rows_ref, gain_ref, *outs):
+def pack_kernel(head_dim, places, place_ref, temper_ref, rows_ref, gain_ref, *outs):
     z = place_ref[0]
+    spread = outs[-1]
+    for head in range(temper_ref.shape[0]):
+        spread[:, head * head_dim : (head + 1) * head_dim] = jnp.full(
+            (1, head_dim), temper_ref[head], F32
+        )
     gain = gain_ref[...]
     for (c, k), (index, slot) in places.items():
         block = rows_ref[0, z ^ k, c].astype(F32)
@@ -68,8 +79,15 @@
         outs[index][slot, 0] = (block * scale * gain).astype(BF16)
 
 
+def share_kernel(shares_ref, out_ref):
+    total = shares_ref[0].astype(F32)
+    for i in range(1, shares_ref.shape[0]):
+        total = total + shares_ref[i].astype(F32)
+    out_ref[...] = total.astype(BF16)
+
+
 def row_kernel(head_dim, places, *refs):
-    wq_ref, wk_ref, wv_ref, q_ref, state_ref = refs[-5:]
+    wk_ref, wv_ref, state_ref = refs[-3:]
     rows = jnp.concatenate([refs[index][slot, 0] for index, slot in places.values()], axis=0)
     keys = plain(rows, wk_ref[...]).astype(BF16)
     values = plain(rows, wv_ref[...]).astype(BF16)
@@ -81,6 +99,11 @@
         state = first_dims(values[:, lower : lower + LANES], features)
         folded = jnp.where(first_head, state[:head_dim], state[head_dim:])
         state_ref[pair, 0] = folded.astype(BF16)
+
+
+def query_kernel(places, *refs):
+    wq_ref, q_ref = refs[-2:]
+    rows = jnp.concatenate([refs[index][slot, 0] for index, slot in places.values()], axis=0)
     q_ref[0] = plain(rows, wq_ref[...]).astype(BF16)
 
 
@@ -193,7 +216,7 @@
 
 
 SCALARS = pl.BlockSpec(memory_space=pltpu.SMEM)
-PARAMS = pltpu.CompilerParams(vmem_limit_bytes=VMEM_LIMIT)
+PARAMS = pltpu.CompilerParams(vmem_limit_bytes=VMEM_MIB * 1024 * 1024)
 
 
 def cost(micros):
@@ -227,7 +250,7 @@
     rows5 = haplo_rows.reshape(haps, n, chunks, depth, width)
     gain_flat = norm_gain[None, :]
     head_gain_flat = head_gain[None, :]
-    temper_flat = jnp.repeat(temper, head_dim)[None, :]
+    flat = jax.ShapeDtypeStruct((1, width), F32)
     anywhere = pl.BlockSpec(memory_space=pl.ANY)
 
     def exchange(array, k):
@@ -251,16 +274,16 @@
         slot = places[c, k][1]
         return pl.BlockSpec((1, haps, depth, width), lambda *_: (slot, 0, 0, 0))
 
-    normed = pl.pallas_call(
-        functools.partial(pack_kernel, places),
+    *normed, temper_flat = pl.pallas_call(
+        functools.partial(pack_kernel, head_dim, places),
         grid=(haps,),
-        in_specs=[SCALARS, rows_spec, whole(gain_flat)],
-        out_specs=hap_specs,
-        out_shape=shapes,
+        in_specs=[SCALARS, SCALARS, rows_spec, whole(gain_flat)],
+        out_specs=hap_specs + [whole(flat)],
+        out_shape=shapes + [flat],
         compiler_params=PARAMS,
-        cost_estimate=cost(0),
+        cost_estimate=cost(PACK_COST),
         name="pack",
-    )(place, rows5, gain_flat)
+    )(place, temper, rows5, gain_flat)
 
     def send_all(arrays):
         got = {}
@@ -271,33 +294,71 @@
                 sent[index] = exchange(arrays[index], k)
         return sent
 
-    arrived = send_all(normed)
-
     full_rows = jax.ShapeDtypeStruct((haps, length, width), BF16)
     row_spec = pl.BlockSpec((1, length, width), lambda r: (r, 0, 0))
     state_spec = pl.BlockSpec((pairs, 1, head_dim, 2 * LANES), lambda r: (0, r, 0, 0))
     state_shape = (pairs, haps, head_dim, 2 * LANES)
-    q_row, state = pl.pallas_call(
+    state = pl.pallas_call(
         functools.partial(row_kernel, head_dim, places),
         grid=(haps,),
-        in_specs=hap_specs + [once(query_row)] * 3,
-        out_specs=[row_spec, state_spec],
-        out_shape=[full_rows, jax.ShapeDtypeStruct(state_shape, BF16)],
+        in_specs=hap_specs + [once(key_row)] * 2,
+        out_specs=state_spec,
+        out_shape=jax.ShapeDtypeStruct(state_shape, BF16),
         compiler_params=PARAMS,
-        cost_estimate=cost(0),
+        cost_estimate=cost(ROW_COST),
         name="row",
-    )(*normed, query_row, key_row, value_row)
+    )(*normed, key_row, value_row)
+
+    q_row = pl.pallas_call(
+        functools.partial(query_kernel, places),
+        grid=(haps,),
+        in_specs=hap_specs + [once(query_row)],
+        out_specs=row_spec,
+        out_shape=full_rows,
+        compiler_params=PARAMS,
+        cost_estimate=cost(QUERY_COST),
+        name="query",
+    )(*normed, query_row)
+
+    waiting = [
+        index for index in range(len(lengths)) if any(places[c, k][0] == index for c, k in order if c > 0 and k > 1)
+    ]
+    held, state = lax.optimization_barrier(([normed[index] for index in waiting], state))
+    queue = list(normed)
+    for index, array in zip(waiting, held):
+        queue[index] = array
+    arrived = send_all(queue)
 
     shares = state.reshape(m, -1, 2 * LANES)
     shares = lax.all_to_all(shares, "pos", split_axis=0, concat_axis=0, tiled=True)
-    share = jnp.sum(shares.astype(F32), axis=0).astype(BF16)
+
+    state = None
+
+    def add_up(shares):
+        share = pl.pallas_call(
+            share_kernel,
+            grid=(1,),
+            in_specs=[whole(shares)],
+            out_specs=pl.BlockSpec(shares.shape[1:], lambda *_: (0, 0)),
+            out_shape=jax.ShapeDtypeStruct(shares.shape[1:], BF16),
+            compiler_params=PARAMS,
+            cost_estimate=cost(SHARE_COST),
+            name="share",
+        )(shares)
+        return lax.all_gather(share, "pos", axis=0, tiled=True).reshape(state_shape)
 
     column_outs = None
     for c in range(chunks):
         blocks = [arrived[places[c, k][0]] for k in range(n)]
         extra = []
+        if c == 0:
+            blocks, q_row = lax.optimization_barrier((blocks, q_row))
         if c > 0:
-            blocks, _unused = lax.optimization_barrier((blocks, share))
+            if TIE_C1 == "state":
+                state = add_up(shares)
+                blocks, state = lax.optimization_barrier((blocks, state))
+            elif TIE_C1 == "shares":
+                blocks, shares = lax.optimization_barrier((blocks, shares))
             extra = [column_outs[places[0, 1][0]]] if n > 1 else []
         every = pltpu.VMEM((haps * n, depth, width), BF16)
         results = pl.pallas_call(
@@ -321,7 +382,8 @@
             column_outs[places[c, k][0]] = results[k]
     returned = send_all(column_outs)
 
-    state = lax.all_gather(share, "pos", axis=0, tiled=True).reshape(state_shape)
+    if state is None:
+        state = add_up(shares)
     acc = pl.pallas_call(
         functools.partial(along_kernel, head_dim, order),
         grid=(haps,),
@@ -330,7 +392,7 @@
         out_shape=jax.ShapeDtypeStruct((haps, len(order), depth, width), F32),
         scratch_shapes=[pltpu.VMEM((length, width), BF16)],
         compiler_params=PARAMS,
-        cost_estimate=cost(0),
+        cost_estimate=cost(ALONG_COST),
         name="along",
     )(place, rows5, q_row, state, head_gain_flat, out_row)
 

time: 90.4 us -> 86.6 us (0.958)
  local copies, waits for them, and re-layouts: 17.2 us -> 5.09 us
  waiting for transfers between devices: 0.03 us -> 11.9 us
  starting transfers between devices: 26.4 us -> 20.1 us
  Pallas kernels: 33.9 us -> 37.7 us
  other arithmetic: 1.24 us -> 0 us
    unnamed x40 -> x36, local copies, waits for them, and re-layouts: 17.1 us -> 5.09 us
    ppermute x10, waiting for transfers between devices: 0.03 us -> 11.9 us  [exchange(): return lax.ppermute(array, 'hap', [(i, i ^ k) for i in range(n)])]
    ppermute x10, starting transfers between devices: 22 us -> 15.9 us  [exchange(): return lax.ppermute(array, 'hap', [(i, i ^ k) for i in range(n)])]
    pallas_call x1 -> x3, Pallas kernels: 1.74 us -> 7.26 us  [the longest x1 3.58 us: local(): pl.pallas_call(functools.partial(query_kernel, places), grid=(haps,), in_...]
    pallas_call x1, Pallas kernels: 7.91 us -> 6.3 us  [local(): pl.pallas_call(functools.partial(row_kernel, head_dim, places), grid=(hap...]
    reduce_sum x1 -> x0, other arithmetic: 1.24 us -> none  [local(): share = jnp.sum(shares.astype(F32), axis=0).astype(BF16)]
  transfers between devices with their start and end apart: 11 -> 11, of which waited for: 0 -> 2; matrix products, arithmetic and copies ran while one was open for 2% -> 0% of each run, Pallas kernels for 33% -> 38%
where the time goes in v2:
time: 86.6 us; the launch traced here: 86.3 us
  Pallas kernels  37.7 us (44%)
  starting transfers between devices  20.1 us (23%)
  waiting for transfers between devices  11.9 us (14%)
  blocking collectives  11.1 us (13%)
  local copies, waits for them, and re-layouts  5.09 us (6%)
    ppermute x10, starting transfers between devices, exchange(): return lax.ppermute(array, 'hap', [(i, i ^ k) for i in range(n)])  15.9 us
    pallas_call x2, Pallas kernels, local(): pl.pallas_call(functools.partial(column_kernel, head_dim, n), grid=(1,),...  15.1 us
    ppermute x10, waiting for transfers between devices, exchange(): return lax.ppermute(array, 'hap', [(i, i ^ k) for i in range(n)])  11.9 us
    all_gather x1, blocking collectives, add_up(): return lax.all_gather(share, 'pos', axis=0, tiled=True).reshape(state_shape)  11.1 us
    pallas_call x1, Pallas kernels, local(): pl.pallas_call(functools.partial(row_kernel, head_dim, places), grid=(hap...  6.3 us
    unnamed x36, local copies, waits for them, and re-layouts  5.09 us
    pallas_call x1, Pallas kernels, local(): pl.pallas_call(functools.partial(along_kernel, head_dim, order), grid=(ha...  4.7 us
    pallas_call x2, Pallas kernels, local(): pl.pallas_call(functools.partial(finish_kernel, pieces, order), grid=(1,)...  4.41 us
  transfers between devices with their start and end apart: 11, of which 2 were waited for; matrix products, arithmetic and copies ran while one was open for 0% of the time, Pallas kernels for 38%

profile of v2, /device:TPU:0, one launch (start us, length us, event | category | flops | bytes accessed | tf_op | source)
XLA Modules:
  0.0 86.3 jit_solution(3063648419880810156)
XLA Ops:
  0.0 1.4 %copy-done.2 = bf16[3,256,1024]{2,1,0:T(8,128)(2,1)S(1)} copy-done((bf16[3,256,1024]{2,1,0:T(8,128)(2,1)S(1)}, bf16[3,256,1024]{2,1,0:T(8,128)(2,1)}, u32[]{:S(2)}) %copy-start.2) | copy-done | bytes 1572888
  1.4 0.7 copy-done.14
  2.1 0.7 copy-done.15
  2.8 2.3 %pack.1 = (bf16[1,3,32,1024]{3,2,1,0:T(8,128)(2,1)S(1)}, bf16[2,3,32,1024]{3,2,1,0:T(8,128)(2,1)S(1)}, bf16[1,3,32,1024]{3,2,1,0:T(8,128)(2,1)S(1)}, bf16[1,3,32...) custom-call(s32[1]{0:T(128)} %bitcast.place_ref, ...), custom_call_target="tpu_custom_call" | custom-call | flops 10000000000 | bytes 1 | tf_op jit(solution)/shard_map/pack/pallas_call | solution.py:277
  5.0 4.0 %collective-permute-start.1 = (bf16[1,3,32,1024]{3,2,1,0:T(8,128)(2,1)S(1)}, bf16[1,3,32,1024]{3,2,1,0:T(8,128)(2,1)S(1)}, u32[]{:S(2)}, u32[]{:S(2)}) collective-permute-start(bf16[1,3,32,1024]{3,2,1,0:T(8,128)(2,1)S(1)} %get-tuple-element.36.refs_2_), channel_id=1, source_target_pairs={{0,16},{8,24},{16,0},{24,8},{1,17},{9,25},{17,1},{25,9},{2,18},{10... | collective-permute-start | bytes 589832 | tf_op jit(solution)/shard_map/ppermute | solution.py:257
  9.1 1.3 %collective-permute-start.2 = (bf16[1,3,32,1024]{3,2,1,0:T(8,128)(2,1)S(1)}, bf16[1,3,32,1024]{3,2,1,0:T(8,128)(2,1)S(1)}, u32[]{:S(2)}, u32[]{:S(2)}) collective-permute-start(bf16[1,3,32,1024]{3,2,1,0:T(8,128)(2,1)S(1)} %get-tuple-element.37.refs_3_), channel_id=1, source_target_pairs={{0,24},{8,16},{16,8},{24,0},{1,25},{9,17},{17,9},{25,1},{2,26},{10... | collective-permute-start | bytes 589832 | tf_op jit(solution)/shard_map/ppermute | solution.py:257
  10.4 0.2 collective-permute-start
  10.7 0.0 copy-done.5
  10.7 0.0 copy-done.6
  10.7 6.3 %row.1 = bf16[8,3,64,256]{3,2,1,0:T(8,128)(2,1)} custom-call(bf16[1,3,32,1024]{3,2,1,0:T(8,128)(2,1)S(1)} %get-tuple-element.51.refs_0_, bf16[2,3,32,1024]{3,2,1,0:T(8,128)(2,1)S(1)} %get-tuple-element.35.refs_1_, bf16[1,3,32,1024]{3,2,1,0:T(8,128)(2,1)S(1)} %get-tuple-element.36.refs_2_, bf16[1,3,32,1024]{3,2,1,0:T(8,128)(2,1)S(1)} %get-tuple-element.37.refs_3_, ...), custom_call_target="tpu_custom_call" | custom-call | flops 20000000000 | bytes 1 | tf_op jit(solution)/shard_map/row/pallas_call | solution.py:301
  17.0 4.2 %all-to-all-start = ((bf16[8,192,256]{2,1,0:T(8,128)(2,1)}), bf16[8,192,256]{2,1,0:T(8,128)(2,1)}, u32[]{:S(2)}, u32[]{:S(2)}) async-start(bf16[8,192,256]{2,1,0:T(8,128)(2,1)} %bitcast.3), calls=%async_computation | async-start | bytes 1572864 | tf_op jit(solution)/shard_map/all_to_all | solution.py:333
  21.2 2.9 %collective-permute-start.3 = (bf16[1,3,32,1024]{3,2,1,0:T(8,128)(2,1)}, bf16[1,3,32,1024]{3,2,1,0:T(8,128)(2,1)}, u32[]{:S(2)}, u32[]{:S(2)}) collective-permute-start(bf16[1,3,32,1024]{3,2,1,0:T(8,128)(2,1)} %get-tuple-element.42.refs_5_), channel_id=1, source_target_pairs={{0,16},{8,24},{16,0},{24,8},{1,17},{9,25},{17,1},{25,9},{2,18},{10... | collective-permute-start | bytes 589832 | tf_op jit(solution)/shard_map/ppermute | solution.py:257
  24.1 1.3 %collective-permute-start.4 = (bf16[1,3,32,1024]{3,2,1,0:T(8,128)(2,1)}, bf16[1,3,32,1024]{3,2,1,0:T(8,128)(2,1)}, u32[]{:S(2)}, u32[]{:S(2)}) collective-permute-start(bf16[1,3,32,1024]{3,2,1,0:T(8,128)(2,1)} %get-tuple-element.43.refs_6_), channel_id=1, source_target_pairs={{0,24},{8,16},{16,8},{24,0},{1,25},{9,17},{17,9},{25,1},{2,26},{10... | collective-permute-start | bytes 589832 | tf_op jit(solution)/shard_map/ppermute | solution.py:257
  25.4 1.6 %copy-done.7 = bf16[1024,1024]{1,0:T(8,128)(2,1)S(1)} copy-done((bf16[1024,1024]{1,0:T(8,128)(2,1)S(1)}, bf16[1024,1024]{1,0:T(8,128)(2,1)}, u32[]{:S(2)}) %copy-start.7) | copy-done | bytes 2097176
  27.0 3.6 %query.1.q_ref = bf16[3,256,1024]{2,1,0:T(8,128)(2,1)S(1)} custom-call(bf16[1,3,32,1024]{3,2,1,0:T(8,128)(2,1)S(1)} %get-tuple-element.51.refs_0_, bf16[2,3,32,1024]{3,2,1,0:T(8,128)(2,1)S(1)} %get-tuple-element.35.refs_1_, bf16[1,3,32,1024]{3,2,1,0:T(8,128)(2,1)S(1)} %get-tuple-element.36.refs_2_, bf16[1,3,32,1024]{3,2,1,0:T(8,128)(2,1)S(1)} %get-tuple-element.37.refs_3_, ...), custom_call_target="tpu_custom_call" | custom-call | flops 5000000000 | bytes 1 | tf_op jit(solution)/shard_map/query/pallas_call | solution.py:312
  30.6 0.0 collective-permute-done.1.refs_2_
  30.6 0.0 collective-permute-done.2.refs_3_
  30.6 0.0 collective-permute-done.refs_1_
  30.6 0.0 copy-done.8
  30.6 0.0 copy-done.10
  30.7 0.0 copy-done.12
  30.7 7.0 %column.2 = (bf16[1,3,32,1024]{3,2,1,0:T(8,128)(2,1)S(1)}, bf16[2,3,32,1024]{3,2,1,0:T(8,128)(2,1)S(1)}, bf16[1,3,32,1024]{3,2,1,0:T(8,128)(2,1)S(1)}, bf16[1,3,32,1024]{3,2,1,0:T(8,128)(2,1)S(1)}) custom-call(f32[1,1024]{1,0:T(1,128)S(1)} %get-tuple-element.46.temper_ref, bf16[1024,1024]{1,0:T(8,128)(2,1)S(1)} %copy-done.8, ...), custom_call_target="tpu_custom_call" | custom-call | flops 199999995904 | bytes 1 | tf_op jit(solution)/shard_map/column/pallas_call | solution.py:364
  37.6 0.0 copy-start.16
  37.6 0.7 copy-done.16
  38.3 0.8 collective-permute-start.8
  39.1 1.7 %collective-permute-start.9 = (bf16[1,3,32,1024]{3,2,1,0:T(8,128)(2,1)S(1)}, bf16[1,3,32,1024]{3,2,1,0:T(8,128)(2,1)S(1)}, u32[]{:S(2)}, u32[]{:S(2)}) collective-permute-start(bf16[1,3,32,1024]{3,2,1,0:T(8,128)(2,1)S(1)} %get-tuple-element.62), channel_id=1, source_target_pairs={{0,24},{8,16},{16,8},{24,0},{1,25},{9,17},{17,9},{25,1},{2,26},{10... | collective-permute-start | bytes 589832 | tf_op jit(solution)/shard_map/ppermute | solution.py:257
  40.8 0.0 all-to-all-done.shares_ref
  40.8 1.4 %share.1 = bf16[192,256]{1,0:T(8,128)(2,1)S(1)} custom-call(bf16[8,192,256]{2,1,0:T(8,128)(2,1)} %all-to-all-done.shares_ref), custom_call_target="tpu_custom_call" | custom-call | flops 5000000000 | bytes 1 | tf_op jit(solution)/shard_map/share/pallas_call | solution.py:338
  42.2 11.1 %all_gather.3 = bf16[1536,256]{1,0:T(8,128)(2,1)S(1)} all-gather(bf16[192,256]{1,0:T(8,128)(2,1)S(1)} %share.1), channel_id=1, replica_groups=mesh['hap'=4,'pos'=8] {'pos'}, dimensions={0}, use_global_device_ids=true | all-gather | bytes 884736 | tf_op jit(solution)/shard_map/all_gather | solution.py:348
  53.3 0.0 collective-permute-done.3.refs_2_
  53.3 0.0 collective-permute-done.4.refs_3_
  53.3 0.0 copy-done.9
  53.3 0.0 copy-start.1
  53.3 0.0 copy-start.3
  53.3 0.0 copy-start.4
  53.3 8.1 %column.3 = (bf16[1,3,32,1024]{3,2,1,0:T(8,128)(2,1)S(1)}, bf16[2,3,32,1024]{3,2,1,0:T(8,128)(2,1)S(1)}, bf16[1,3,32,1024]{3,2,1,0:T(8,128)(2,1)S(1)}, bf16[1,3,32,1024]{3,2,1,0:T(8,128)(2,1)S(1)}) custom-call(f32[1,1024]{1,0:T(1,128)S(1)} %get-tuple-element.46.temper_ref, bf16[1024,1024]{1,0:T(8,128)(2,1)S(1)} %copy-done.9, ...), custom_call_target="tpu_custom_call", output_to_operand_aliasing={{1}: (8, {})} | custom-call | flops 30000001024 | bytes 1 | tf_op jit(solution)/shard_map/column/pallas_call | solution.py:364
  61.4 2.1 %collective-permute-start.6 = (bf16[1,3,32,1024]{3,2,1,0:T(8,128)(2,1)S(1)}, bf16[1,3,32,1024]{3,2,1,0:T(8,128)(2,1)S(1)}, u32[]{:S(2)}, u32[]{:S(2)}) collective-permute-start(bf16[1,3,32,1024]{3,2,1,0:T(8,128)(2,1)S(1)} %get-tuple-element.58), channel_id=1, source_target_pairs={{0,16},{8,24},{16,0},{24,8},{1,17},{9,25},{17,1},{25,9},{2,18},{10... | collective-permute-start | bytes 589832 | tf_op jit(solution)/shard_map/ppermute | solution.py:257
  63.5 1.3 %collective-permute-start.7 = (bf16[1,3,32,1024]{3,2,1,0:T(8,128)(2,1)S(1)}, bf16[1,3,32,1024]{3,2,1,0:T(8,128)(2,1)S(1)}, u32[]{:S(2)}, u32[]{:S(2)}) collective-permute-start(bf16[1,3,32,1024]{3,2,1,0:T(8,128)(2,1)S(1)} %get-tuple-element.59), channel_id=1, source_target_pairs={{0,24},{8,16},{16,8},{24,0},{1,25},{9,17},{17,9},{25,1},{2,26},{10... | collective-permute-start | bytes 589832 | tf_op jit(solution)/shard_map/ppermute | solution.py:257
  64.9 0.1 collective-permute-start.5
  65.0 0.0 copy-done.3
  65.0 4.7 %along.1.acc_ref = f32[3,8,32,1024]{3,2,1,0:T(8,128)S(1)} custom-call(s32[1]{0:T(128)} %bitcast.place_ref, bf16[3,4,2,32,1024]{4,3,2,1,0:T(8,128)(2,1)S(1)} %bitcast.9, bf16[3,256,1024]{2,1,0:T(8,128)(2,1)S(1)} %query.1.q_ref, bf16[8,3,64,256]{3,2,1,0:T(8,128)(2,1)S(1)} %bitcast.7, f32[1,1024]{1,0:T(1,128)S(1)} %bitcast.10, bf16[1024,1024]{1,0:T(8,128)(2,1)S(1)} %copy-done.1), custom_call_target="tpu_custom_call" | custom-call | bytes 1 | tf_op jit(solution)/shard_map/along/pallas_call | solution.py:387
  69.8 0.0 collective-permute-done.8.refs_1_
  69.8 0.0 collective-permute-done.9.refs_2_
  69.8 1.9 %finish.2.refs_5_ = bf16[3,4,2,32,1024]{4,3,2,1,0:T(8,128)(2,1)} custom-call(s32[1]{0:T(128)} %bitcast.place_ref, f32[3,8,32,1024]{3,2,1,0:T(8,128)S(1)} %along.1.acc_ref, bf16[1024,1024]{1,0:T(8,128)(2,1)S(1)} %copy-done, bf16[1,3,32,1024]{3,2,1,0:T(8,128)(2,1)S(1)} %copy-done.17, bf16[1,3,32,1024]{3,2,1,0:T(8,128)(2,1)S(1)} %collective-permute-done.8.refs_1_, ...), custom_call_target="tpu_custom_call" | custom-call | flops 30000001024 | bytes 1 | tf_op jit(solution)/shard_map/finish/pallas_call | solution.py:405
  71.7 6.9 %collective-permute-done.6.refs_3_ = bf16[1,3,32,1024]{3,2,1,0:T(8,128)(2,1)S(1)} collective-permute-done((bf16[1,3,32,1024]{3,2,1,0:T(8,128)(2,1)S(1)}, bf16[1,3,32,1024]{3,2,1,0:T(8,128)(2,1)S(1)}, u32[]{:S(2)}, u32[]{:S(2)}) %collective-permute-start.6) | collective-permute-done | bytes 196640 | tf_op jit(solution)/shard_map/ppermute | solution.py:257
  78.5 0.0 collective-permute-done.7.refs_4_
  78.5 5.0 %collective-permute-done.5.refs_0_.refs_2_ = bf16[2,3,32,1024]{3,2,1,0:T(8,128)(2,1)S(1)} collective-permute-done((bf16[2,3,32,1024]{3,2,1,0:T(8,128)(2,1)S(1)}, bf16[2,3,32,1024]{3,2,1,0:T(8,128)(2,1)S(1)}, u32[]{:S(2)}, u32[]{:S(2)}) %collective-permute-start.5) | collective-permute-done | bytes 393248 | tf_op jit(solution)/shard_map/ppermute | solution.py:257
  83.6 2.5 %finish.3 = bf16[3,4,2,32,1024]{4,3,2,1,0:T(8,128)(2,1)} custom-call(s32[1]{0:T(128)} %bitcast.place_ref, f32[3,8,32,1024]{3,2,1,0:T(8,128)S(1)} %along.1.acc_ref, bf16[1024,1024]{1,0:T(8,128)(2,1)S(1)} %copy-done, bf16[2,3,32,1024]{3,2,1,0:T(8,128)(2,1)S(1)} %collective-permute-done.5.refs_0_.refs_2_, ...), custom_call_target="tpu_custom_call", output_to_operand_aliasing={{}: (8, {})} | custom-call | bytes 1 | tf_op jit(solution)/shard_map/finish/pallas_call | solution.py:405
  (20 shorter events, 0.0 us)
Async XLA Ops:
  0.0 1.4 %copy-start.2 = (bf16[3,256,1024]{2,1,0:T(8,128)(2,1)S(1)}, bf16[3,256,1024]{2,1,0:T(8,128)(2,1)}, u32[]{:S(2)}) copy-start(bf16[3,256,1024]{2,1,0:T(8,128)(2,1)} %param.12) | copy-start | bytes 4718596
  1.4 0.7 copy-start.14
  2.1 0.7 copy-start.15
  2.8 7.9 %copy-start.5 = (bf16[1024,1024]{1,0:T(8,128)(2,1)S(1)}, bf16[1024,1024]{1,0:T(8,128)(2,1)}, u32[]{:S(2)}) copy-start(bf16[1024,1024]{1,0:T(8,128)(2,1)} %refs_7_.3) | copy-start | bytes 6291460
  2.8 7.9 %copy-start.6 = (bf16[1024,1024]{1,0:T(8,128)(2,1)S(1)}, bf16[1024,1024]{1,0:T(8,128)(2,1)}, u32[]{:S(2)}) copy-start(bf16[1024,1024]{1,0:T(8,128)(2,1)} %refs_8_.1) | copy-start | bytes 6291460
  5.0 25.6 %collective-permute-start.1 = (bf16[1,3,32,1024]{3,2,1,0:T(8,128)(2,1)S(1)}, bf16[1,3,32,1024]{3,2,1,0:T(8,128)(2,1)S(1)}, u32[]{:S(2)}, u32[]{:S(2)}) collective-permute-start(bf16[1,3,32,1024]{3,2,1,0:T(8,128)(2,1)S(1)} %get-tuple-element.36.refs_2_), channel_id=1, source_target_pairs={{0,16},{8,24},{16,0},{24,8},{1,17},{9,25},{17,1},{25,9},{2,18},{10... | collective-permute-start | bytes 589832 | tf_op jit(solution)/shard_map/ppermute | solution.py:257
  9.1 21.5 %collective-permute-start.2 = (bf16[1,3,32,1024]{3,2,1,0:T(8,128)(2,1)S(1)}, bf16[1,3,32,1024]{3,2,1,0:T(8,128)(2,1)S(1)}, u32[]{:S(2)}, u32[]{:S(2)}) collective-permute-start(bf16[1,3,32,1024]{3,2,1,0:T(8,128)(2,1)S(1)} %get-tuple-element.37.refs_3_), channel_id=1, source_target_pairs={{0,24},{8,16},{16,8},{24,0},{1,25},{9,17},{17,9},{25,1},{2,26},{10... | collective-permute-start | bytes 589832 | tf_op jit(solution)/shard_map/ppermute | solution.py:257
  10.4 20.2 %collective-permute-start = (bf16[2,3,32,1024]{3,2,1,0:T(8,128)(2,1)S(1)}, bf16[2,3,32,1024]{3,2,1,0:T(8,128)(2,1)S(1)}, u32[]{:S(2)}, u32[]{:S(2)}) collective-permute-start(bf16[2,3,32,1024]{3,2,1,0:T(8,128)(2,1)S(1)} %get-tuple-element.35.refs_1_), channel_id=1, source_target_pairs={{0,8},{8,0},{16,24},{24,16},{1,9},{9,1},{17,25},{25,17},{2,10},{10... | collective-permute-start | bytes 1179656 | tf_op jit(solution)/shard_map/ppermute | solution.py:257
  17.0 23.8 %all-to-all-start = ((bf16[8,192,256]{2,1,0:T(8,128)(2,1)}), bf16[8,192,256]{2,1,0:T(8,128)(2,1)}, u32[]{:S(2)}, u32[]{:S(2)}) async-start(bf16[8,192,256]{2,1,0:T(8,128)(2,1)} %bitcast.3), calls=%async_computation | async-start | bytes 1572864 | tf_op jit(solution)/shard_map/all_to_all | solution.py:333
  21.2 32.1 %collective-permute-start.3 = (bf16[1,3,32,1024]{3,2,1,0:T(8,128)(2,1)}, bf16[1,3,32,1024]{3,2,1,0:T(8,128)(2,1)}, u32[]{:S(2)}, u32[]{:S(2)}) collective-permute-start(bf16[1,3,32,1024]{3,2,1,0:T(8,128)(2,1)} %get-tuple-element.42.refs_5_), channel_id=1, source_target_pairs={{0,16},{8,24},{16,0},{24,8},{1,17},{9,25},{17,1},{25,9},{2,18},{10... | collective-permute-start | bytes 589832 | tf_op jit(solution)/shard_map/ppermute | solution.py:257
  24.1 29.2 %collective-permute-start.4 = (bf16[1,3,32,1024]{3,2,1,0:T(8,128)(2,1)}, bf16[1,3,32,1024]{3,2,1,0:T(8,128)(2,1)}, u32[]{:S(2)}, u32[]{:S(2)}) collective-permute-start(bf16[1,3,32,1024]{3,2,1,0:T(8,128)(2,1)} %get-tuple-element.43.refs_6_), channel_id=1, source_target_pairs={{0,24},{8,16},{16,8},{24,0},{1,25},{9,17},{17,9},{25,1},{2,26},{10... | collective-permute-start | bytes 589832 | tf_op jit(solution)/shard_map/ppermute | solution.py:257
  25.4 1.6 %copy-start.7 = (bf16[1024,1024]{1,0:T(8,128)(2,1)S(1)}, bf16[1024,1024]{1,0:T(8,128)(2,1)}, u32[]{:S(2)}) copy-start(bf16[1024,1024]{1,0:T(8,128)(2,1)} %refs_7_.2) | copy-start | bytes 6291460
  27.0 3.6 %copy-start.8 = (bf16[1024,1024]{1,0:T(8,128)(2,1)S(1)}, bf16[1024,1024]{1,0:T(8,128)(2,1)}, u32[]{:S(2)}) copy-start(bf16[1024,1024]{1,0:T(8,128)(2,1)} %wq_ref.3) | copy-start | bytes 6291460
  27.0 3.6 %copy-start.10 = (bf16[1024,1024]{1,0:T(8,128)(2,1)S(1)}, bf16[1024,1024]{1,0:T(8,128)(2,1)}, u32[]{:S(2)}) copy-start(bf16[1024,1024]{1,0:T(8,128)(2,1)} %wk_ref.3) | copy-start | bytes 6291460
  27.0 3.6 %copy-start.12 = (bf16[1024,1024]{1,0:T(8,128)(2,1)S(1)}, bf16[1024,1024]{1,0:T(8,128)(2,1)}, u32[]{:S(2)}) copy-start(bf16[1024,1024]{1,0:T(8,128)(2,1)} %wv_ref.3) | copy-start | bytes 6291460
  37.6 0.7 copy-start.16
  38.3 31.4 %collective-permute-start.8 = (bf16[1,3,32,1024]{3,2,1,0:T(8,128)(2,1)S(1)}, bf16[1,3,32,1024]{3,2,1,0:T(8,128)(2,1)S(1)}, u32[]{:S(2)}, u32[]{:S(2)}) collective-permute-start(bf16[1,3,32,1024]{3,2,1,0:T(8,128)(2,1)S(1)} %get-tuple-element.61), channel_id=1, source_target_pairs={{0,16},{8,24},{16,0},{24,8},{1,17},{9,25},{17,1},{25,9},{2,18},{10... | collective-permute-start | bytes 589832 | tf_op jit(solution)/shard_map/ppermute | solution.py:257
  39.1 30.6 %collective-permute-start.9 = (bf16[1,3,32,1024]{3,2,1,0:T(8,128)(2,1)S(1)}, bf16[1,3,32,1024]{3,2,1,0:T(8,128)(2,1)S(1)}, u32[]{:S(2)}, u32[]{:S(2)}) collective-permute-start(bf16[1,3,32,1024]{3,2,1,0:T(8,128)(2,1)S(1)} %get-tuple-element.62), channel_id=1, source_target_pairs={{0,24},{8,16},{16,8},{24,0},{1,25},{9,17},{17,9},{25,1},{2,26},{10... | collective-permute-start | bytes 589832 | tf_op jit(solution)/shard_map/ppermute | solution.py:257
  40.8 12.5 %copy-start.9 = (bf16[1024,1024]{1,0:T(8,128)(2,1)S(1)}, bf16[1024,1024]{1,0:T(8,128)(2,1)}, u32[]{:S(2)}) copy-start(bf16[1024,1024]{1,0:T(8,128)(2,1)} %wq_ref.3) | copy-start | bytes 6291460
  40.8 12.5 %copy-start.11 = (bf16[1024,1024]{1,0:T(8,128)(2,1)S(1)}, bf16[1024,1024]{1,0:T(8,128)(2,1)}, u32[]{:S(2)}) copy-start(bf16[1024,1024]{1,0:T(8,128)(2,1)} %wk_ref.3) | copy-start | bytes 6291460
  40.8 12.5 %copy-start.13 = (bf16[1024,1024]{1,0:T(8,128)(2,1)S(1)}, bf16[1024,1024]{1,0:T(8,128)(2,1)}, u32[]{:S(2)}) copy-start(bf16[1024,1024]{1,0:T(8,128)(2,1)} %wv_ref.3) | copy-start | bytes 6291460
  53.3 11.7 %copy-start.1 = (bf16[1024,1024]{1,0:T(8,128)(2,1)S(1)}, bf16[1024,1024]{1,0:T(8,128)(2,1)}, u32[]{:S(2)}) copy-start(bf16[1024,1024]{1,0:T(8,128)(2,1)} %wo_ref.3) | copy-start | bytes 6291460
  53.3 11.7 %copy-start.3 = (bf16[3,256,1024]{2,1,0:T(8,128)(2,1)S(1)}, bf16[3,256,1024]{2,1,0:T(8,128)(2,1)}, u32[]{:S(2)}) copy-start(bf16[3,256,1024]{2,1,0:T(8,128)(2,1)} %param.12) | copy-start | bytes 4718596
  53.3 11.7 %copy-start.4 = (f32[1024]{0:T(1024)S(1)}, f32[1024]{0:T(1024)}, u32[]{:S(2)}) copy-start(f32[1024]{0:T(1024)} %param.18) | copy-start | bytes 12292
  61.4 17.1 %collective-permute-start.6 = (bf16[1,3,32,1024]{3,2,1,0:T(8,128)(2,1)S(1)}, bf16[1,3,32,1024]{3,2,1,0:T(8,128)(2,1)S(1)}, u32[]{:S(2)}, u32[]{:S(2)}) collective-permute-start(bf16[1,3,32,1024]{3,2,1,0:T(8,128)(2,1)S(1)} %get-tuple-element.58), channel_id=1, source_target_pairs={{0,16},{8,24},{16,0},{24,8},{1,17},{9,25},{17,1},{25,9},{2,18},{10... | collective-permute-start | bytes 589832 | tf_op jit(solution)/shard_map/ppermute | solution.py:257
  63.5 15.0 %collective-permute-start.7 = (bf16[1,3,32,1024]{3,2,1,0:T(8,128)(2,1)S(1)}, bf16[1,3,32,1024]{3,2,1,0:T(8,128)(2,1)S(1)}, u32[]{:S(2)}, u32[]{:S(2)}) collective-permute-start(bf16[1,3,32,1024]{3,2,1,0:T(8,128)(2,1)S(1)} %get-tuple-element.59), channel_id=1, source_target_pairs={{0,24},{8,16},{16,8},{24,0},{1,25},{9,17},{17,9},{25,1},{2,26},{10... | collective-permute-start | bytes 589832 | tf_op jit(solution)/shard_map/ppermute | solution.py:257
  64.9 18.7 %collective-permute-start.5 = (bf16[2,3,32,1024]{3,2,1,0:T(8,128)(2,1)S(1)}, bf16[2,3,32,1024]{3,2,1,0:T(8,128)(2,1)S(1)}, u32[]{:S(2)}, u32[]{:S(2)}) collective-permute-start(bf16[2,3,32,1024]{3,2,1,0:T(8,128)(2,1)S(1)} %get-tuple-element.56), channel_id=1, source_target_pairs={{0,8},{8,0},{16,24},{24,16},{1,9},{9,1},{17,25},{25,17},{2,10},{10... | collective-permute-start | bytes 1179656 | tf_op jit(solution)/shard_map/ppermute | solution.py:257
  65.0 4.8 %copy-start = (bf16[1024,1024]{1,0:T(8,128)(2,1)S(1)}, bf16[1024,1024]{1,0:T(8,128)(2,1)}, u32[]{:S(2)}) copy-start(bf16[1024,1024]{1,0:T(8,128)(2,1)} %wo_ref.5) | copy-start | bytes 6291460
  65.0 4.8 %copy-start.17 = (bf16[1,3,32,1024]{3,2,1,0:T(8,128)(2,1)S(1)}, bf16[1,3,32,1024]{3,2,1,0:T(8,128)(2,1)}, u32[]{:S(2)}) copy-start(bf16[1,3,32,1024]{3,2,1,0:T(8,128)(2,1)} %copy-done.16) | copy-start | bytes 589828

commit v3 on v2

--- a/solution.py
+++ b/solution.py
@@ -15,7 +15,8 @@
 VMEM_MIB = 24
 PACK_COST = 10
 ROW_COST = 20
-QUERY_COST = 5
+SPREAD_COST = 5
+RAW = True
 SHARE_COST = 5
 TIE_C1 = 'state'
 ALONG_COST = 0
@@ -65,18 +66,24 @@
     return plus, minus
 
 
-def pack_kernel(head_dim, places, place_ref, temper_ref, rows_ref, gain_ref, *outs):
-    z = place_ref[0]
-    spread = outs[-1]
+def normalise(rows, gain):
+    wide = rows.astype(F32)
+    scale = lax.rsqrt(jnp.mean(wide * wide, axis=-1, keepdims=True) + EPS)
+    return (wide * scale * gain).astype(BF16)
+
+
+def spread_kernel(head_dim, temper_ref, out_ref):
     for head in range(temper_ref.shape[0]):
-        spread[:, head * head_dim : (head + 1) * head_dim] = jnp.full(
+        out_ref[:, head * head_dim : (head + 1) * head_dim] = jnp.full(
             (1, head_dim), temper_ref[head], F32
         )
+
+
+def pack_kernel(places, place_ref, rows_ref, gain_ref, *outs):
+    z = place_ref[0]
     gain = gain_ref[...]
     for (c, k), (index, slot) in places.items():
-        block = rows_ref[0, z ^ k, c].astype(F32)
-        scale = lax.rsqrt(jnp.mean(block * block, axis=-1, keepdims=True) + EPS)
-        outs[index][slot, 0] = (block * scale * gain).astype(BF16)
+        outs[index][slot, 0] = normalise(rows_ref[0, z ^ k, c], gain)
 
 
 def share_kernel(shares_ref, out_ref):
@@ -101,20 +108,18 @@
         state_ref[pair, 0] = folded.astype(BF16)
 
 
-def query_kernel(places, *refs):
-    wq_ref, q_ref = refs[-2:]
-    rows = jnp.concatenate([refs[index][slot, 0] for index, slot in places.values()], axis=0)
-    q_ref[0] = plain(rows, wq_ref[...]).astype(BF16)
-
-
-def along_kernel(head_dim, order, place_ref, rows_ref, q_ref, state_ref, gain_ref, wo_ref, out_ref, mixed):
+def along_kernel(
+    head_dim, order, place_ref, rows_ref, norm_ref, wq_ref, state_ref, gain_ref, wo_ref, out_ref, mixed
+):
     z = place_ref[0]
+    rows = jnp.concatenate([rows_ref[0, z ^ k, c] for c, k in order], axis=0)
+    queries = plain(normalise(rows, norm_ref[...]), wq_ref[...]).astype(BF16)
     first_head = lane_of((head_dim, 2 * LANES)) % LANES < head_dim
     ones = group_ones(2 * LANES, head_dim)
     alongs = []
     for pair in range(state_ref.shape[0]):
         lower = pair * LANES
-        plus, minus = feature_pair(q_ref[0, :, lower : lower + LANES].astype(F32))
+        plus, minus = feature_pair(queries[:, lower : lower + LANES].astype(F32))
         features = jnp.concatenate([plus, minus], axis=1)
         folded = state_ref[pair, 0]
         none = jnp.zeros_like(folded)
@@ -134,12 +139,17 @@
         out_ref[0, i] = rows_ref[0, z ^ k, c].astype(F32) + row_out[i * depth : (i + 1) * depth]
 
 
-def column_kernel(head_dim, count, temper_ref, wq_ref, wk_ref, wv_ref, *refs):
+def column_kernel(head_dim, raw, temper_ref, gain_ref, wq_ref, wk_ref, wv_ref, *refs):
+    count = len(raw)
     blocks = refs[:count]
     outs = refs[-3 - count : -3]
     q_all, k_all, v_all = refs[-3:]
     _one, haps, depth, width = blocks[0].shape
-    rows = jnp.concatenate([block[0, r] for block in blocks for r in range(haps)], axis=0)
+    pieces = []
+    for block, is_raw in zip(blocks, raw):
+        piece = block[0].reshape(haps * depth, width)
+        pieces.append(normalise(piece, gain_ref[...]) if is_raw else piece)
+    rows = jnp.concatenate(pieces, axis=0)
     shape = q_all.shape
     ones = group_ones(2 * LANES, head_dim)
     q = plain(rows, wq_ref[...]).astype(BF16).astype(F32)
@@ -152,8 +162,8 @@
     all_haps = shape[0]
     many = all_haps * TILE
     same = (
-        lax.broadcasted_iota(jnp.int32, (many, many), 0) % TILE
-        == lax.broadcasted_iota(jnp.int32, (many, many), 1) % TILE
+        lax.broadcasted_iota(jnp.int32, (2 * many, many), 0) % TILE
+        == lax.broadcasted_iota(jnp.int32, (2 * many, many), 1) % TILE
     )
     first_head = lane_of((many, LANES)) < head_dim
     none = jnp.zeros((many, LANES), BF16)
@@ -164,14 +174,13 @@
             query = q_all[at].reshape(many, LANES)
             key = k_all[at].reshape(many, LANES)
             value = v_all[at].reshape(many, LANES)
-            score_a = last_dims(jnp.where(first_head, query, none), key)
-            score_b = last_dims(jnp.where(first_head, none, query), key)
-            weight_a = jnp.where(same, jnp.exp(score_a), 0.0).astype(BF16)
-            weight_b = jnp.where(same, jnp.exp(score_b), 0.0).astype(BF16)
-            sum_a = plain(weight_a, jnp.where(first_head, value, one))
-            sum_b = plain(weight_b, jnp.where(first_head, one, value))
-            summed = jnp.where(first_head, sum_a, sum_b)
-            total = pltpu.roll(jnp.where(first_head, sum_b, sum_a), head_dim, 1)
+            queries = jnp.concatenate(
+                [jnp.where(first_head, query, none), jnp.where(first_head, none, query)], axis=0
+            )
+            weight = jnp.where(same, jnp.exp(last_dims(queries, key)), 0.0).astype(BF16)
+            sums = plain(weight, jnp.concatenate([value, one], axis=1))
+            summed = jnp.where(first_head, sums[:many, :LANES], sums[many:, :LANES])
+            total = jnp.where(first_head, sums[:many, LANES:], sums[many:, LANES:])
             result = (summed / total).astype(BF16).reshape(all_haps, TILE, LANES)
             for k in range(count):
                 outs[k][0, :, start : start + TILE, lower : lower + LANES] = result[
@@ -274,16 +283,16 @@
         slot = places[c, k][1]
         return pl.BlockSpec((1, haps, depth, width), lambda *_: (slot, 0, 0, 0))
 
-    *normed, temper_flat = pl.pallas_call(
-        functools.partial(pack_kernel, head_dim, places),
+    normed = pl.pallas_call(
+        functools.partial(pack_kernel, places),
         grid=(haps,),
-        in_specs=[SCALARS, SCALARS, rows_spec, whole(gain_flat)],
-        out_specs=hap_specs + [whole(flat)],
-        out_shape=shapes + [flat],
+        in_specs=[SCALARS, rows_spec, whole(gain_flat)],
+        out_specs=hap_specs,
+        out_shape=shapes,
         compiler_params=PARAMS,
         cost_estimate=cost(PACK_COST),
         name="pack",
-    )(place, temper, rows5, gain_flat)
+    )(place, rows5, gain_flat)
 
     def send_all(arrays):
         got = {}
@@ -294,8 +303,6 @@
                 sent[index] = exchange(arrays[index], k)
         return sent
 
-    full_rows = jax.ShapeDtypeStruct((haps, length, width), BF16)
-    row_spec = pl.BlockSpec((1, length, width), lambda r: (r, 0, 0))
     state_spec = pl.BlockSpec((pairs, 1, head_dim, 2 * LANES), lambda r: (0, r, 0, 0))
     state_shape = (pairs, haps, head_dim, 2 * LANES)
     state = pl.pallas_call(
@@ -309,16 +316,16 @@
         name="row",
     )(*normed, key_row, value_row)
 
-    q_row = pl.pallas_call(
-        functools.partial(query_kernel, places),
-        grid=(haps,),
-        in_specs=hap_specs + [once(query_row)],
-        out_specs=row_spec,
-        out_shape=full_rows,
+    temper_flat = pl.pallas_call(
+        functools.partial(spread_kernel, head_dim),
+        grid=(1,),
+        in_specs=[SCALARS],
+        out_specs=whole(flat),
+        out_shape=flat,
         compiler_params=PARAMS,
-        cost_estimate=cost(QUERY_COST),
-        name="query",
-    )(*normed, query_row)
+        cost_estimate=cost(SPREAD_COST),
+        name="spread",
+    )(temper)
 
     waiting = [
         index for index in range(len(lengths)) if any(places[c, k][0] == index for c, k in order if c > 0 and k > 1)
@@ -327,6 +334,12 @@
     queue = list(normed)
     for index, array in zip(waiting, held):
         queue[index] = array
+    raw = [k > 1 and RAW for k in range(n)]
+    for k in range(n):
+        if raw[k]:
+            queue[places[0, k][0]] = lax.dynamic_index_in_dim(
+                rows5[:, :, 0], place[0] ^ k, 1, keepdims=False
+            )[None]
     arrived = send_all(queue)
 
     shares = state.reshape(m, -1, 2 * LANES)
@@ -351,8 +364,6 @@
     for c in range(chunks):
         blocks = [arrived[places[c, k][0]] for k in range(n)]
         extra = []
-        if c == 0:
-            blocks, q_row = lax.optimization_barrier((blocks, q_row))
         if c > 0:
             if TIE_C1 == "state":
                 state = add_up(shares)
@@ -362,20 +373,20 @@
             extra = [column_outs[places[0, 1][0]]] if n > 1 else []
         every = pltpu.VMEM((haps * n, depth, width), BF16)
         results = pl.pallas_call(
-            functools.partial(column_kernel, head_dim, n),
+            functools.partial(column_kernel, head_dim, raw if c == 0 else [False] * n),
             grid=(1,),
-            in_specs=[whole(temper_flat)]
+            in_specs=[whole(temper_flat), whole(gain_flat)]
             + [once(query_col)] * 3
             + [piece_spec(c, k) for k in range(n)]
             + [anywhere] * len(extra),
             out_specs=[piece_spec(c, k) for k in range(n)],
             out_shape=[shapes[places[c, k][0]] for k in range(n)],
             scratch_shapes=[every] * 3,
-            input_output_aliases={4 + n: 1} if extra else {},
+            input_output_aliases={5 + n: 1} if extra else {},
             compiler_params=PARAMS,
             cost_estimate=cost(COLUMN_COSTS[c]),
             name="column",
-        )(temper_flat, query_col, key_col, value_col, *blocks, *extra)
+        )(temper_flat, gain_flat, query_col, key_col, value_col, *blocks, *extra)
         if column_outs is None:
             column_outs = [None] * len(shapes)
         for k in range(n):
@@ -387,14 +398,14 @@
     acc = pl.pallas_call(
         functools.partial(along_kernel, head_dim, order),
         grid=(haps,),
-        in_specs=[SCALARS, rows_spec, row_spec, state_spec, whole(head_gain_flat), once(out_row)],
+        in_specs=[SCALARS, rows_spec, whole(gain_flat), once(query_row), state_spec, whole(head_gain_flat), once(out_row)],
         out_specs=pl.BlockSpec((1, len(order), depth, width), lambda r: (r, 0, 0, 0)),
         out_shape=jax.ShapeDtypeStruct((haps, len(order), depth, width), F32),
         scratch_shapes=[pltpu.VMEM((length, width), BF16)],
         compiler_params=PARAMS,
         cost_estimate=cost(ALONG_COST),
         name="along",
-    )(place, rows5, q_row, state, head_gain_flat, out_row)
+    )(place, rows5, gain_flat, query_row, state, head_gain_flat, out_row)
 
     early = [(0, k) for k in range(n) if k != 1] if chunks > 1 else []
     late = [piece for piece in order if piece not in early]

time: 86.6 us -> 81 us (0.935)
  Pallas kernels: 37.7 us -> 33.1 us
  starting transfers between devices: 20.1 us -> 24 us
  local copies, waits for them, and re-layouts: 5.09 us -> 2.14 us
  waiting for transfers between devices: 11.9 us -> 10.5 us
    pallas_call x4, Pallas kernels: 20.9 us -> 14.2 us  [the longest x2 11.9 us: local(): pl.pallas_call(functools.partial(column_kernel, head_dim, raw if c == 0 e...]
    unnamed x36 -> x34, local copies, waits for them, and re-layouts: 5.09 us -> 0.1 us
    ppermute x10, starting transfers between devices: 15.9 us -> 19.8 us  [exchange(): return lax.ppermute(array, 'hap', [(i, i ^ k) for i in range(n)])]
    pallas_call x1, Pallas kernels: 4.7 us -> 6.72 us  [local(): pl.pallas_call(functools.partial(along_kernel, head_dim, order), grid=(ha...]
    ppermute x10, waiting for transfers between devices: 11.9 us -> 10.5 us  [exchange(): return lax.ppermute(array, 'hap', [(i, i ^ k) for i in range(n)])]
    slice x0 -> x1, local copies, waits for them, and re-layouts: none -> 1.33 us  [local(): rows5[:, :, 0]]
  transfers between devices with their start and end apart: 11 -> 11, of which waited for: 2 -> 3; matrix products, arithmetic and copies ran while one was open for 0% -> 0% of each run, Pallas kernels for 38% -> 38%
where the time goes in v3:
time: 81 us; the launch traced here: 80.7 us
  Pallas kernels  33.1 us (41%)
  starting transfers between devices  24 us (30%)
  blocking collectives  10.6 us (13%)
  waiting for transfers between devices  10.5 us (13%)
  local copies, waits for them, and re-layouts  2.14 us (3%)
    ppermute x10, starting transfers between devices, exchange(): return lax.ppermute(array, 'hap', [(i, i ^ k) for i in range(n)])  19.8 us
    pallas_call x2, Pallas kernels, local(): pl.pallas_call(functools.partial(column_kernel, head_dim, raw if c == 0 e...  11.9 us
    all_gather x1, blocking collectives, add_up(): return lax.all_gather(share, 'pos', axis=0, tiled=True).reshape(state_shape)  10.6 us
    ppermute x10, waiting for transfers between devices, exchange(): return lax.ppermute(array, 'hap', [(i, i ^ k) for i in range(n)])  10.5 us
    pallas_call x1, Pallas kernels, local(): pl.pallas_call(functools.partial(along_kernel, head_dim, order), grid=(ha...  6.72 us
    pallas_call x1, Pallas kernels, local(): pl.pallas_call(functools.partial(row_kernel, head_dim, places), grid=(hap...  6.36 us
    pallas_call x2, Pallas kernels, local(): pl.pallas_call(functools.partial(finish_kernel, pieces, order), grid=(1,)...  4.4 us
    all_to_all x1, starting transfers between devices, local(): lax.all_to_all(shares, 'pos', split_axis=0, concat_axis=0, tiled=True)  4.22 us
  transfers between devices with their start and end apart: 11, of which 3 were waited for; matrix products, arithmetic and copies ran while one was open for 0% of the time, Pallas kernels for 38%

profile of v3, /device:TPU:0, one launch (start us, length us, event | category | flops | bytes accessed | tf_op | source)
XLA Modules:
  0.0 80.7 jit_solution(15330546146084856364)
XLA Ops:
  0.0 1.3 %slice.5 = bf16[3,4,1,32,1024]{4,3,2,1,0:T(8,128)(2,1)S(1)} slice(bf16[3,4,2,32,1024]{4,3,2,1,0:T(8,128)(2,1)} %bitcast.11), slice={[0:3], [0:4], [0:1], [0:32], [0:1024]} | slice | bytes 1572864 | tf_op jit(solution)/shard_map/slice | solution.py:341
  1.3 0.7 dynamic-slice_bitcast_fusion
  2.1 5.0 %collective-permute-start.4 = (bf16[1,3,32,1024]{3,2,1,0:T(8,128)(2,1)}, bf16[1,3,32,1024]{3,2,1,0:T(8,128)(2,1)S(1)}, u32[]{:S(2)}, u32[]{:S(2)}) collective-permute-start(bf16[1,3,32,1024]{3,2,1,0:T(8,128)(2,1)} %get-tuple-element.51), channel_id=1, source_target_pairs={{0,24},{8,16},{16,8},{24,0},{1,25},{9,17},{17,9},{25,1},{2,26},{10... | collective-permute-start | bytes 589832 | tf_op jit(solution)/shard_map/ppermute | solution.py:266
  7.1 0.0 collective-permute-start.3
  7.1 0.0 copy-done
  7.1 0.0 copy-done.4
  7.1 0.0 copy-start.6
  7.1 0.0 copy-start.7
  7.2 1.8 %pack.1 = (bf16[1,3,32,1024]{3,2,1,0:T(8,128)(2,1)S(1)}, bf16[2,3,32,1024]{3,2,1,0:T(8,128)(2,1)S(1)}, bf16[1,3,32,1024]{3,2,1,0:T(8,128)(2,1)S(1)}, bf16[1,3,32...) custom-call(s32[1]{0:T(128)} %bitcast.place_ref, ...), custom_call_target="tpu_custom_call" | custom-call | flops 10000000000 | bytes 1 | tf_op jit(solution)/shard_map/pack/pallas_call | solution.py:286
  8.9 0.5 collective-permute-start
  9.5 0.0 copy-done.6
  9.5 0.0 copy-done.7
  9.5 6.4 %row.1 = bf16[8,3,64,256]{3,2,1,0:T(8,128)(2,1)} custom-call(bf16[1,3,32,1024]{3,2,1,0:T(8,128)(2,1)S(1)} %get-tuple-element.32.refs_0_, bf16[2,3,32,1024]{3,2,1,0:T(8,128)(2,1)S(1)} %get-tuple-element.29.refs_1_, bf16[1,3,32,1024]{3,2,1,0:T(8,128)(2,1)S(1)} %get-tuple-element.33.refs_2_, bf16[1,3,32,1024]{3,2,1,0:T(8,128)(2,1)S(1)} %get-tuple-element.34.refs_3_, ...), custom_call_target="tpu_custom_call" | custom-call | flops 20000000000 | bytes 1 | tf_op jit(solution)/shard_map/row/pallas_call | solution.py:308
  15.9 0.0 copy-done.15
  15.9 4.2 %all-to-all-start = ((bf16[8,192,256]{2,1,0:T(8,128)(2,1)}), bf16[8,192,256]{2,1,0:T(8,128)(2,1)}, u32[]{:S(2)}, u32[]{:S(2)}) async-start(bf16[8,192,256]{2,1,0:T(8,128)(2,1)} %bitcast.3), calls=%async_computation | async-start | bytes 1572864 | tf_op jit(solution)/shard_map/all_to_all | solution.py:346
  20.1 0.0 copy-start.8
  20.1 0.0 copy-start.10
  20.1 0.0 copy-start.12
  20.1 3.0 %collective-permute-start.1 = (bf16[1,3,32,1024]{3,2,1,0:T(8,128)(2,1)}, bf16[1,3,32,1024]{3,2,1,0:T(8,128)(2,1)}, u32[]{:S(2)}, u32[]{:S(2)}) collective-permute-start(bf16[1,3,32,1024]{3,2,1,0:T(8,128)(2,1)} %get-tuple-element.35.refs_5_), channel_id=1, source_target_pairs={{0,16},{8,24},{16,0},{24,8},{1,17},{9,25},{17,1},{25,9},{2,18},{10... | collective-permute-start | bytes 589832 | tf_op jit(solution)/shard_map/ppermute | solution.py:266
  23.1 1.0 %collective-permute-start.2 = (bf16[1,3,32,1024]{3,2,1,0:T(8,128)(2,1)}, bf16[1,3,32,1024]{3,2,1,0:T(8,128)(2,1)}, u32[]{:S(2)}, u32[]{:S(2)}) collective-permute-start(bf16[1,3,32,1024]{3,2,1,0:T(8,128)(2,1)} %get-tuple-element.36.refs_6_), channel_id=1, source_target_pairs={{0,24},{8,16},{16,8},{24,0},{1,25},{9,17},{17,9},{25,1},{2,26},{10... | collective-permute-start | bytes 589832 | tf_op jit(solution)/shard_map/ppermute | solution.py:266
  24.1 0.5 spread.1.temper_ref
  24.6 0.0 collective-permute-done.4.refs_3_
  24.6 0.0 collective-permute-done.3.refs_2_
  24.7 1.3 %collective-permute-done.refs_1_ = bf16[2,3,32,1024]{3,2,1,0:T(8,128)(2,1)S(1)} collective-permute-done((bf16[2,3,32,1024]{3,2,1,0:T(8,128)(2,1)S(1)}, bf16[2,3,32,1024]{3,2,1,0:T(8,128)(2,1)S(1)}, u32[]{:S(2)}, u32[]{:S(2)}) %collective-permute-start) | collective-permute-done | bytes 393248 | tf_op jit(solution)/shard_map/ppermute | solution.py:266
  26.0 5.4 %column.2 = (bf16[1,3,32,1024]{3,2,1,0:T(8,128)(2,1)S(1)}, bf16[2,3,32,1024]{3,2,1,0:T(8,128)(2,1)S(1)}, bf16[1,3,32,1024]{3,2,1,0:T(8,128)(2,1)S(1)}, bf16[1,3,32,1024]{3,2,1,0:T(8,128)(2,1)S(1)}) custom-call(f32[1,1024]{1,0:T(1,128)S(1)} %spread.1.temper_ref, f32[1,1024]{1,0:T(1,128)S(1)} %bitcast.16, bf16[1024,1024]{1,0:T(8,128)(2,1)S(1)} %copy-done.8, ...), custom_call_target="tpu_custom_call" | custom-call | flops 199999995904 | bytes 1 | tf_op jit(solution)/shard_map/column/pallas_call | solution.py:375
  31.4 1.1 %collective-permute-start.8 = (bf16[1,3,32,1024]{3,2,1,0:T(8,128)(2,1)S(1)}, bf16[1,3,32,1024]{3,2,1,0:T(8,128)(2,1)S(1)}, u32[]{:S(2)}, u32[]{:S(2)}) collective-permute-start(bf16[1,3,32,1024]{3,2,1,0:T(8,128)(2,1)S(1)} %get-tuple-element.49), channel_id=1, source_target_pairs={{0,16},{8,24},{16,0},{24,8},{1,17},{9,25},{17,1},{25,9},{2,18},{10... | collective-permute-start | bytes 589832 | tf_op jit(solution)/shard_map/ppermute | solution.py:266
  32.5 2.4 %collective-permute-start.9 = (bf16[1,3,32,1024]{3,2,1,0:T(8,128)(2,1)S(1)}, bf16[1,3,32,1024]{3,2,1,0:T(8,128)(2,1)S(1)}, u32[]{:S(2)}, u32[]{:S(2)}) collective-permute-start(bf16[1,3,32,1024]{3,2,1,0:T(8,128)(2,1)S(1)} %get-tuple-element.50), channel_id=1, source_target_pairs={{0,24},{8,16},{16,8},{24,0},{1,25},{9,17},{17,9},{25,1},{2,26},{10... | collective-permute-start | bytes 589832 | tf_op jit(solution)/shard_map/ppermute | solution.py:266
  34.8 0.0 all-to-all-done.shares_ref
  34.9 1.4 %share.1 = bf16[192,256]{1,0:T(8,128)(2,1)S(1)} custom-call(bf16[8,192,256]{2,1,0:T(8,128)(2,1)} %all-to-all-done.shares_ref), custom_call_target="tpu_custom_call" | custom-call | flops 5000000000 | bytes 1 | tf_op jit(solution)/shard_map/share/pallas_call | solution.py:351
  36.2 10.6 %all_gather.3 = bf16[1536,256]{1,0:T(8,128)(2,1)S(1)} all-gather(bf16[192,256]{1,0:T(8,128)(2,1)S(1)} %share.1), channel_id=1, replica_groups=mesh['hap'=4,'pos'=8] {'pos'}, dimensions={0}, use_global_device_ids=true | all-gather | bytes 884736 | tf_op jit(solution)/shard_map/all_gather | solution.py:361
  46.8 0.0 collective-permute-done.1.refs_2_
  46.8 0.0 collective-permute-done.2.refs_3_
  46.8 0.0 copy-start.2
  46.9 0.0 copy-start.3
  46.9 0.0 copy-start.5
  46.9 6.5 %column.3 = (bf16[1,3,32,1024]{3,2,1,0:T(8,128)(2,1)S(1)}, bf16[2,3,32,1024]{3,2,1,0:T(8,128)(2,1)S(1)}, bf16[1,3,32,1024]{3,2,1,0:T(8,128)(2,1)S(1)}, bf16[1,3,32,1024]{3,2,1,0:T(8,128)(2,1)S(1)}) custom-call(f32[1,1024]{1,0:T(1,128)S(1)} %spread.1.temper_ref, f32[1,1024]{1,0:T(1,128)S(1)} %bitcast.17, ...), custom_call_target="tpu_custom_call", output_to_operand_aliasing={{1}: (9, {})} | custom-call | flops 30000001024 | bytes 1 | tf_op jit(solution)/shard_map/column/pallas_call | solution.py:375
  53.4 6.1 %collective-permute-start.6 = (bf16[1,3,32,1024]{3,2,1,0:T(8,128)(2,1)S(1)}, bf16[1,3,32,1024]{3,2,1,0:T(8,128)(2,1)S(1)}, u32[]{:S(2)}, u32[]{:S(2)}) collective-permute-start(bf16[1,3,32,1024]{3,2,1,0:T(8,128)(2,1)S(1)} %get-tuple-element.46), channel_id=1, source_target_pairs={{0,16},{8,24},{16,0},{24,8},{1,17},{9,25},{17,1},{25,9},{2,18},{10... | collective-permute-start | bytes 589832 | tf_op jit(solution)/shard_map/ppermute | solution.py:266
  59.5 0.4 collective-permute-start.7
  59.9 0.2 collective-permute-start.5
  60.1 6.7 %along.1.acc_ref = f32[3,8,32,1024]{3,2,1,0:T(8,128)S(1)} custom-call(s32[1]{0:T(128)} %bitcast.place_ref, bf16[3,4,2,32,1024]{4,3,2,1,0:T(8,128)(2,1)S(1)} %bitcast.13, f32[1,1024]{1,0:T(1,128)S(1)} %bitcast.18, bf16[1024,1024]{1,0:T(8,128)(2,1)S(1)} %copy-done.2, bf16[8,3,64,256]{3,2,1,0:T(8,128)(2,1)S(1)} %bitcast.14, f32[1,1024]{1,0:T(1,128)S(1)} %bitcast.19, ...), custom_call_target="tpu_custom_call" | custom-call | bytes 1 | tf_op jit(solution)/shard_map/along/pallas_call | solution.py:398
  66.9 0.0 collective-permute-done.8.refs_1_
  66.9 0.0 collective-permute-done.9.refs_2_
  66.9 0.0 copy-done.1
  66.9 1.9 %finish.2.refs_5_ = bf16[3,4,2,32,1024]{4,3,2,1,0:T(8,128)(2,1)} custom-call(s32[1]{0:T(128)} %bitcast.place_ref, f32[3,8,32,1024]{3,2,1,0:T(8,128)S(1)} %along.1.acc_ref, bf16[1024,1024]{1,0:T(8,128)(2,1)S(1)} %copy-done.1, bf16[1,3,32,1024]{3,2,1,0:T(8,128)(2,1)S(1)} %get-tuple-element.48.refs_0_, ...), custom_call_target="tpu_custom_call" | custom-call | flops 30000001024 | bytes 1 | tf_op jit(solution)/shard_map/finish/pallas_call | solution.py:416
  68.8 3.9 %collective-permute-done.6.refs_3_ = bf16[1,3,32,1024]{3,2,1,0:T(8,128)(2,1)S(1)} collective-permute-done((bf16[1,3,32,1024]{3,2,1,0:T(8,128)(2,1)S(1)}, bf16[1,3,32,1024]{3,2,1,0:T(8,128)(2,1)S(1)}, u32[]{:S(2)}, u32[]{:S(2)}) %collective-permute-start.6) | collective-permute-done | bytes 196640 | tf_op jit(solution)/shard_map/ppermute | solution.py:266
  72.7 0.0 collective-permute-done.7.refs_4_
  72.7 5.3 %collective-permute-done.5.refs_0_.refs_2_ = bf16[2,3,32,1024]{3,2,1,0:T(8,128)(2,1)S(1)} collective-permute-done((bf16[2,3,32,1024]{3,2,1,0:T(8,128)(2,1)S(1)}, bf16[2,3,32,1024]{3,2,1,0:T(8,128)(2,1)S(1)}, u32[]{:S(2)}, u32[]{:S(2)}) %collective-permute-start.5) | collective-permute-done | bytes 393248 | tf_op jit(solution)/shard_map/ppermute | solution.py:266
  78.0 2.5 %finish.3 = bf16[3,4,2,32,1024]{4,3,2,1,0:T(8,128)(2,1)} custom-call(s32[1]{0:T(128)} %bitcast.place_ref, f32[3,8,32,1024]{3,2,1,0:T(8,128)S(1)} %along.1.acc_ref, bf16[1024,1024]{1,0:T(8,128)(2,1)S(1)} %copy-done.1, bf16[2,3,32,1024]{3,2,1,0:T(8,128)(2,1)S(1)} %collective-permute-done.5.refs_0_.refs_2_, ...), custom_call_target="tpu_custom_call", output_to_operand_aliasing={{}: (8, {})} | custom-call | bytes 1 | tf_op jit(solution)/shard_map/finish/pallas_call | solution.py:416
  (20 shorter events, 0.0 us)
Async XLA Ops:
  0.0 7.1 %copy-start = (bf16[3,256,1024]{2,1,0:T(8,128)(2,1)S(1)}, bf16[3,256,1024]{2,1,0:T(8,128)(2,1)}, u32[]{:S(2)}) copy-start(bf16[3,256,1024]{2,1,0:T(8,128)(2,1)} %param.12) | copy-start | bytes 4718596
  0.0 7.1 %copy-start.4 = (f32[1024]{0:T(1024)S(1)}, f32[1024]{0:T(1024)}, u32[]{:S(2)}) copy-start(f32[1024]{0:T(1024)} %param.13) | copy-start | bytes 12292
  2.1 22.6 %collective-permute-start.4 = (bf16[1,3,32,1024]{3,2,1,0:T(8,128)(2,1)}, bf16[1,3,32,1024]{3,2,1,0:T(8,128)(2,1)S(1)}, u32[]{:S(2)}, u32[]{:S(2)}) collective-permute-start(bf16[1,3,32,1024]{3,2,1,0:T(8,128)(2,1)} %get-tuple-element.51), channel_id=1, source_target_pairs={{0,24},{8,16},{16,8},{24,0},{1,25},{9,17},{17,9},{25,1},{2,26},{10... | collective-permute-start | bytes 589832 | tf_op jit(solution)/shard_map/ppermute | solution.py:266
  7.1 17.5 %collective-permute-start.3 = (bf16[1,3,32,1024]{3,2,1,0:T(8,128)(2,1)S(1)}, bf16[1,3,32,1024]{3,2,1,0:T(8,128)(2,1)S(1)}, u32[]{:S(2)}, u32[]{:S(2)}) collective-permute-start(bf16[1,3,32,1024]{3,2,1,0:T(8,128)(2,1)S(1)} %get-tuple-element.52), channel_id=1, source_target_pairs={{0,16},{8,24},{16,0},{24,8},{1,17},{9,25},{17,1},{25,9},{2,18},{10... | collective-permute-start | bytes 589832 | tf_op jit(solution)/shard_map/ppermute | solution.py:266
  7.1 2.3 %copy-start.6 = (bf16[1024,1024]{1,0:T(8,128)(2,1)S(1)}, bf16[1024,1024]{1,0:T(8,128)(2,1)}, u32[]{:S(2)}) copy-start(bf16[1024,1024]{1,0:T(8,128)(2,1)} %refs_7_.1) | copy-start | bytes 6291460
  7.1 2.4 %copy-start.7 = (bf16[1024,1024]{1,0:T(8,128)(2,1)S(1)}, bf16[1024,1024]{1,0:T(8,128)(2,1)}, u32[]{:S(2)}) copy-start(bf16[1024,1024]{1,0:T(8,128)(2,1)} %refs_8_.1) | copy-start | bytes 6291460
  8.9 6.9 %copy-start.15 = (bf16[1,3,32,1024]{3,2,1,0:T(8,128)(2,1)}, bf16[1,3,32,1024]{3,2,1,0:T(8,128)(2,1)S(1)}, u32[]{:S(2)}) copy-start(bf16[1,3,32,1024]{3,2,1,0:T(8,128)(2,1)S(1)} %get-tuple-element.39.refs_4_.refs_0_) | copy-start | bytes 589828
  8.9 17.0 %collective-permute-start = (bf16[2,3,32,1024]{3,2,1,0:T(8,128)(2,1)S(1)}, bf16[2,3,32,1024]{3,2,1,0:T(8,128)(2,1)S(1)}, u32[]{:S(2)}, u32[]{:S(2)}) collective-permute-start(bf16[2,3,32,1024]{3,2,1,0:T(8,128)(2,1)S(1)} %get-tuple-element.29.refs_1_), channel_id=1, source_target_pairs={{0,8},{8,0},{16,24},{24,16},{1,9},{9,1},{17,25},{25,17},{2,10},{10... | collective-permute-start | bytes 1179656 | tf_op jit(solution)/shard_map/ppermute | solution.py:266
  9.5 14.6 %copy-start.14 = (f32[16]{0:T(128)S(1)}, f32[16]{0:T(128)}, u32[]{:S(2)}) copy-start(f32[16]{0:T(128)} %temper_ref.1) | copy-start | bytes 196
  15.9 19.0 %all-to-all-start = ((bf16[8,192,256]{2,1,0:T(8,128)(2,1)}), bf16[8,192,256]{2,1,0:T(8,128)(2,1)}, u32[]{:S(2)}, u32[]{:S(2)}) async-start(bf16[8,192,256]{2,1,0:T(8,128)(2,1)} %bitcast.3), calls=%async_computation | async-start | bytes 1572864 | tf_op jit(solution)/shard_map/all_to_all | solution.py:346
  20.1 5.9 %copy-start.8 = (bf16[1024,1024]{1,0:T(8,128)(2,1)S(1)}, bf16[1024,1024]{1,0:T(8,128)(2,1)}, u32[]{:S(2)}) copy-start(bf16[1024,1024]{1,0:T(8,128)(2,1)} %wq_ref.5) | copy-start | bytes 6291460
  20.1 5.9 %copy-start.10 = (bf16[1024,1024]{1,0:T(8,128)(2,1)S(1)}, bf16[1024,1024]{1,0:T(8,128)(2,1)}, u32[]{:S(2)}) copy-start(bf16[1024,1024]{1,0:T(8,128)(2,1)} %wk_ref.3) | copy-start | bytes 6291460
  20.1 5.9 %copy-start.12 = (bf16[1024,1024]{1,0:T(8,128)(2,1)S(1)}, bf16[1024,1024]{1,0:T(8,128)(2,1)}, u32[]{:S(2)}) copy-start(bf16[1024,1024]{1,0:T(8,128)(2,1)} %wv_ref.3) | copy-start | bytes 6291460
  20.1 26.7 %collective-permute-start.1 = (bf16[1,3,32,1024]{3,2,1,0:T(8,128)(2,1)}, bf16[1,3,32,1024]{3,2,1,0:T(8,128)(2,1)}, u32[]{:S(2)}, u32[]{:S(2)}) collective-permute-start(bf16[1,3,32,1024]{3,2,1,0:T(8,128)(2,1)} %get-tuple-element.35.refs_5_), channel_id=1, source_target_pairs={{0,16},{8,24},{16,0},{24,8},{1,17},{9,25},{17,1},{25,9},{2,18},{10... | collective-permute-start | bytes 589832 | tf_op jit(solution)/shard_map/ppermute | solution.py:266
  23.1 23.7 %collective-permute-start.2 = (bf16[1,3,32,1024]{3,2,1,0:T(8,128)(2,1)}, bf16[1,3,32,1024]{3,2,1,0:T(8,128)(2,1)}, u32[]{:S(2)}, u32[]{:S(2)}) collective-permute-start(bf16[1,3,32,1024]{3,2,1,0:T(8,128)(2,1)} %get-tuple-element.36.refs_6_), channel_id=1, source_target_pairs={{0,24},{8,16},{16,8},{24,0},{1,25},{9,17},{17,9},{25,1},{2,26},{10... | collective-permute-start | bytes 589832 | tf_op jit(solution)/shard_map/ppermute | solution.py:266
  31.4 35.5 %collective-permute-start.8 = (bf16[1,3,32,1024]{3,2,1,0:T(8,128)(2,1)S(1)}, bf16[1,3,32,1024]{3,2,1,0:T(8,128)(2,1)S(1)}, u32[]{:S(2)}, u32[]{:S(2)}) collective-permute-start(bf16[1,3,32,1024]{3,2,1,0:T(8,128)(2,1)S(1)} %get-tuple-element.49), channel_id=1, source_target_pairs={{0,16},{8,24},{16,0},{24,8},{1,17},{9,25},{17,1},{25,9},{2,18},{10... | collective-permute-start | bytes 589832 | tf_op jit(solution)/shard_map/ppermute | solution.py:266
  32.5 14.4 %copy-start.16 = (bf16[1,3,32,1024]{3,2,1,0:T(8,128)(2,1)S(1)}, bf16[1,3,32,1024]{3,2,1,0:T(8,128)(2,1)}, u32[]{:S(2)}) copy-start(bf16[1,3,32,1024]{3,2,1,0:T(8,128)(2,1)} %copy-done.15) | copy-start | bytes 589828
  32.5 34.4 %collective-permute-start.9 = (bf16[1,3,32,1024]{3,2,1,0:T(8,128)(2,1)S(1)}, bf16[1,3,32,1024]{3,2,1,0:T(8,128)(2,1)S(1)}, u32[]{:S(2)}, u32[]{:S(2)}) collective-permute-start(bf16[1,3,32,1024]{3,2,1,0:T(8,128)(2,1)S(1)} %get-tuple-element.50), channel_id=1, source_target_pairs={{0,24},{8,16},{16,8},{24,0},{1,25},{9,17},{17,9},{25,1},{2,26},{10... | collective-permute-start | bytes 589832 | tf_op jit(solution)/shard_map/ppermute | solution.py:266
  34.8 12.0 %copy-start.9 = (bf16[1024,1024]{1,0:T(8,128)(2,1)S(1)}, bf16[1024,1024]{1,0:T(8,128)(2,1)}, u32[]{:S(2)}) copy-start(bf16[1024,1024]{1,0:T(8,128)(2,1)} %wq_ref.5) | copy-start | bytes 6291460
  34.8 12.0 %copy-start.11 = (bf16[1024,1024]{1,0:T(8,128)(2,1)S(1)}, bf16[1024,1024]{1,0:T(8,128)(2,1)}, u32[]{:S(2)}) copy-start(bf16[1024,1024]{1,0:T(8,128)(2,1)} %wk_ref.3) | copy-start | bytes 6291460
  34.8 12.0 %copy-start.13 = (bf16[1024,1024]{1,0:T(8,128)(2,1)S(1)}, bf16[1024,1024]{1,0:T(8,128)(2,1)}, u32[]{:S(2)}) copy-start(bf16[1024,1024]{1,0:T(8,128)(2,1)} %wv_ref.3) | copy-start | bytes 6291460
  46.8 13.3 %copy-start.2 = (bf16[1024,1024]{1,0:T(8,128)(2,1)S(1)}, bf16[1024,1024]{1,0:T(8,128)(2,1)}, u32[]{:S(2)}) copy-start(bf16[1024,1024]{1,0:T(8,128)(2,1)} %wq_ref.3) | copy-start | bytes 6291460
  46.9 13.3 %copy-start.3 = (bf16[1024,1024]{1,0:T(8,128)(2,1)S(1)}, bf16[1024,1024]{1,0:T(8,128)(2,1)}, u32[]{:S(2)}) copy-start(bf16[1024,1024]{1,0:T(8,128)(2,1)} %wo_ref.3) | copy-start | bytes 6291460
  46.9 13.3 %copy-start.5 = (f32[1024]{0:T(1024)S(1)}, f32[1024]{0:T(1024)}, u32[]{:S(2)}) copy-start(f32[1024]{0:T(1024)} %param.18) | copy-start | bytes 12292
  53.4 19.3 %collective-permute-start.6 = (bf16[1,3,32,1024]{3,2,1,0:T(8,128)(2,1)S(1)}, bf16[1,3,32,1024]{3,2,1,0:T(8,128)(2,1)S(1)}, u32[]{:S(2)}, u32[]{:S(2)}) collective-permute-start(bf16[1,3,32,1024]{3,2,1,0:T(8,128)(2,1)S(1)} %get-tuple-element.46), channel_id=1, source_target_pairs={{0,16},{8,24},{16,0},{24,8},{1,17},{9,25},{17,1},{25,9},{2,18},{10... | collective-permute-start | bytes 589832 | tf_op jit(solution)/shard_map/ppermute | solution.py:266
  59.5 13.2 %collective-permute-start.7 = (bf16[1,3,32,1024]{3,2,1,0:T(8,128)(2,1)S(1)}, bf16[1,3,32,1024]{3,2,1,0:T(8,128)(2,1)S(1)}, u32[]{:S(2)}, u32[]{:S(2)}) collective-permute-start(bf16[1,3,32,1024]{3,2,1,0:T(8,128)(2,1)S(1)} %get-tuple-element.47), channel_id=1, source_target_pairs={{0,24},{8,16},{16,8},{24,0},{1,25},{9,17},{17,9},{25,1},{2,26},{10... | collective-permute-start | bytes 589832 | tf_op jit(solution)/shard_map/ppermute | solution.py:266
  59.9 18.1 %collective-permute-start.5 = (bf16[2,3,32,1024]{3,2,1,0:T(8,128)(2,1)S(1)}, bf16[2,3,32,1024]{3,2,1,0:T(8,128)(2,1)S(1)}, u32[]{:S(2)}, u32[]{:S(2)}) collective-permute-start(bf16[2,3,32,1024]{3,2,1,0:T(8,128)(2,1)S(1)} %get-tuple-element.44), channel_id=1, source_target_pairs={{0,8},{8,0},{16,24},{24,16},{1,9},{9,1},{17,25},{25,17},{2,10},{10... | collective-permute-start | bytes 1179656 | tf_op jit(solution)/shard_map/ppermute | solution.py:266
  60.1 6.8 %copy-start.1 = (bf16[1024,1024]{1,0:T(8,128)(2,1)S(1)}, bf16[1024,1024]{1,0:T(8,128)(2,1)}, u32[]{:S(2)}) copy-start(bf16[1024,1024]{1,0:T(8,128)(2,1)} %wo_ref.5) | copy-start | bytes 6291460

commit v4 on v3

--- a/solution.py
+++ b/solution.py
@@ -19,9 +19,10 @@
 RAW = True
 SHARE_COST = 5
 TIE_C1 = 'state'
+TIE_BACK = True
 ALONG_COST = 0
 COLUMN_COSTS = (200, 30)
-FINISH_COSTS = (30, 0)
+FINISH_COSTS = (30, 0, 0)
 
 
 def last_dims(left, right):
@@ -360,38 +361,35 @@
         )(shares)
         return lax.all_gather(share, "pos", axis=0, tiled=True).reshape(state_shape)
 
-    column_outs = None
+    one_piece = jax.ShapeDtypeStruct((1, haps, depth, width), BF16)
+    one_spec = pl.BlockSpec(one_piece.shape, lambda *_: (0, 0, 0, 0))
+    returned = {}
     for c in range(chunks):
         blocks = [arrived[places[c, k][0]] for k in range(n)]
-        extra = []
         if c > 0:
             if TIE_C1 == "state":
                 state = add_up(shares)
                 blocks, state = lax.optimization_barrier((blocks, state))
             elif TIE_C1 == "shares":
                 blocks, shares = lax.optimization_barrier((blocks, shares))
-            extra = [column_outs[places[0, 1][0]]] if n > 1 else []
         every = pltpu.VMEM((haps * n, depth, width), BF16)
         results = pl.pallas_call(
             functools.partial(column_kernel, head_dim, raw if c == 0 else [False] * n),
             grid=(1,),
             in_specs=[whole(temper_flat), whole(gain_flat)]
             + [once(query_col)] * 3
-            + [piece_spec(c, k) for k in range(n)]
-            + [anywhere] * len(extra),
-            out_specs=[piece_spec(c, k) for k in range(n)],
-            out_shape=[shapes[places[c, k][0]] for k in range(n)],
+            + [piece_spec(c, k) for k in range(n)],
+            out_specs=[one_spec] * n,
+            out_shape=[one_piece] * n,
             scratch_shapes=[every] * 3,
-            input_output_aliases={5 + n: 1} if extra else {},
             compiler_params=PARAMS,
             cost_estimate=cost(COLUMN_COSTS[c]),
             name="column",
-        )(temper_flat, gain_flat, query_col, key_col, value_col, *blocks, *extra)
-        if column_outs is None:
-            column_outs = [None] * len(shapes)
+        )(temper_flat, gain_flat, query_col, key_col, value_col, *blocks)
+        if TIE_BACK and c > 0 and n > 1:
+            results, returned[0, 1] = lax.optimization_barrier((results, returned[0, 1]))
         for k in range(n):
-            column_outs[places[c, k][0]] = results[k]
-    returned = send_all(column_outs)
+            returned[c, k] = exchange(results[k], k) if k > 0 else results[k]
 
     if state is None:
         state = add_up(shares)
@@ -407,17 +405,20 @@
         name="along",
     )(place, rows5, gain_flat, query_row, state, head_gain_flat, out_row)
 
-    early = [(0, k) for k in range(n) if k != 1] if chunks > 1 else []
-    late = [piece for piece in order if piece not in early]
+    groups = [[], [], []]
+    for c, k in order:
+        groups[2 if c == chunks - 1 and k > 1 else 0 if c == 0 and chunks > 1 else 1].append((c, k))
     updated = None
-    for pieces in [early, late] if early else [late]:
+    for pieces, weight in zip(groups, FINISH_COSTS):
+        if not pieces:
+            continue
         extra = [] if updated is None else [updated]
         count = len(pieces)
         updated = pl.pallas_call(
             functools.partial(finish_kernel, pieces, order),
             grid=(1,),
             in_specs=[SCALARS, anywhere, once(out_col)]
-            + [piece_spec(c, k) for c, k in pieces]
+            + [one_spec] * count
             + [anywhere] * len(extra),
             out_specs=anywhere,
             out_shape=jax.ShapeDtypeStruct(rows5.shape, BF16),
@@ -429,9 +430,9 @@
             ],
             input_output_aliases={3 + count: 0} if extra else {},
             compiler_params=PARAMS,
-            cost_estimate=cost(FINISH_COSTS[0 if pieces is early else 1]),
+            cost_estimate=cost(weight),
             name="finish",
-        )(place, acc, out_col, *[returned[places[c, k][0]] for c, k in pieces], *extra)
+        )(place, acc, out_col, *[returned[piece] for piece in pieces], *extra)
     return updated.reshape(haps, length, width)
 
 

time: 81 us -> 77.3 us (0.954)
  waiting for transfers between devices: 10.5 us -> 5.98 us
    ppermute x10 -> x11, waiting for transfers between devices: 10.5 us -> 5.98 us  [exchange(): return lax.ppermute(array, 'hap', [(i, i ^ k) for i in range(n)])]
    pallas_call x2 -> x3, Pallas kernels: 4.4 us -> 5.25 us  [local(): pl.pallas_call(functools.partial(finish_kernel, pieces, order), grid=(1,)...]
    ppermute x10 -> x11, starting transfers between devices: 19.8 us -> 19.6 us  [exchange(): return lax.ppermute(array, 'hap', [(i, i ^ k) for i in range(n)])]
  transfers between devices with their start and end apart: 11 -> 12, of which waited for: 3 -> 2; matrix products, arithmetic and copies ran while one was open for 0% -> 0% of each run, Pallas kernels for 38% -> 42%
where the time goes in v4:
time: 77.3 us; the launch traced here: 77.1 us
  Pallas kernels  33.9 us (44%)
  starting transfers between devices  23.8 us (31%)
  blocking collectives  10.7 us (14%)
  waiting for transfers between devices  5.98 us (8%)
  local copies, waits for them, and re-layouts  2.14 us (3%)
    ppermute x11, starting transfers between devices, exchange(): return lax.ppermute(array, 'hap', [(i, i ^ k) for i in range(n)])  19.6 us
    pallas_call x2, Pallas kernels, local(): pl.pallas_call(functools.partial(column_kernel, head_dim, raw if c == 0 e...  11.9 us
    all_gather x1, blocking collectives, add_up(): return lax.all_gather(share, 'pos', axis=0, tiled=True).reshape(state_shape)  10.7 us
    pallas_call x1, Pallas kernels, local(): pl.pallas_call(functools.partial(along_kernel, head_dim, order), grid=(ha...  6.73 us
    pallas_call x1, Pallas kernels, local(): pl.pallas_call(functools.partial(row_kernel, head_dim, places), grid=(hap...  6.36 us
    ppermute x11, waiting for transfers between devices, exchange(): return lax.ppermute(array, 'hap', [(i, i ^ k) for i in range(n)])  5.98 us
    pallas_call x3, Pallas kernels, local(): pl.pallas_call(functools.partial(finish_kernel, pieces, order), grid=(1,)...  5.25 us
    all_to_all x1, starting transfers between devices, local(): lax.all_to_all(shares, 'pos', split_axis=0, concat_axis=0, tiled=True)  4.21 us
  transfers between devices with their start and end apart: 12, of which 2 were waited for; matrix products, arithmetic and copies ran while one was open for 0% of the time, Pallas kernels for 42%

profile of v4, /device:TPU:0, one launch (start us, length us, event | category | flops | bytes accessed | tf_op | source)
XLA Modules:
  0.0 77.1 jit_solution(16521527376502275663)
XLA Ops:
  0.0 1.3 %slice.5 = bf16[3,4,1,32,1024]{4,3,2,1,0:T(8,128)(2,1)S(1)} slice(bf16[3,4,2,32,1024]{4,3,2,1,0:T(8,128)(2,1)} %bitcast.11), slice={[0:3], [0:4], [0:1], [0:32], [0:1024]} | slice | bytes 1572864 | tf_op jit(solution)/shard_map/slice | solution.py:342
  1.3 0.7 dynamic-slice_bitcast_fusion
  2.1 5.0 %collective-permute-start.4 = (bf16[1,3,32,1024]{3,2,1,0:T(8,128)(2,1)}, bf16[1,3,32,1024]{3,2,1,0:T(8,128)(2,1)S(1)}, u32[]{:S(2)}, u32[]{:S(2)}) collective-permute-start(bf16[1,3,32,1024]{3,2,1,0:T(8,128)(2,1)} %get-tuple-element.61), channel_id=1, source_target_pairs={{0,24},{8,16},{16,8},{24,0},{1,25},{9,17},{17,9},{25,1},{2,26},{10... | collective-permute-start | bytes 589832 | tf_op jit(solution)/shard_map/ppermute | solution.py:267
  7.1 0.0 collective-permute-start.3
  7.1 0.0 copy-done.4
  7.1 0.0 copy-start.6
  7.1 0.0 copy-start.7
  7.1 1.8 %pack.1 = (bf16[1,3,32,1024]{3,2,1,0:T(8,128)(2,1)S(1)}, bf16[2,3,32,1024]{3,2,1,0:T(8,128)(2,1)S(1)}, bf16[1,3,32,1024]{3,2,1,0:T(8,128)(2,1)S(1)}, bf16[1,3,32...) custom-call(s32[1]{0:T(128)} %bitcast.place_ref, ...), custom_call_target="tpu_custom_call" | custom-call | flops 10000000000 | bytes 1 | tf_op jit(solution)/shard_map/pack/pallas_call | solution.py:287
  8.9 0.5 collective-permute-start
  9.5 0.0 copy-done.7
  9.5 6.4 %row.1 = bf16[8,3,64,256]{3,2,1,0:T(8,128)(2,1)} custom-call(bf16[1,3,32,1024]{3,2,1,0:T(8,128)(2,1)S(1)} %get-tuple-element.37.refs_0_, bf16[2,3,32,1024]{3,2,1,0:T(8,128)(2,1)S(1)} %get-tuple-element.34.refs_1_, bf16[1,3,32,1024]{3,2,1,0:T(8,128)(2,1)S(1)} %get-tuple-element.38.refs_2_, bf16[1,3,32,1024]{3,2,1,0:T(8,128)(2,1)S(1)} %get-tuple-element.39.refs_3_, ...), custom_call_target="tpu_custom_call" | custom-call | flops 20000000000 | bytes 1 | tf_op jit(solution)/shard_map/row/pallas_call | solution.py:309
  15.9 0.0 copy-done.15
  15.9 4.2 %all-to-all-start = ((bf16[8,192,256]{2,1,0:T(8,128)(2,1)}), bf16[8,192,256]{2,1,0:T(8,128)(2,1)}, u32[]{:S(2)}, u32[]{:S(2)}) async-start(bf16[8,192,256]{2,1,0:T(8,128)(2,1)} %bitcast.3), calls=%async_computation | async-start | bytes 1572864 | tf_op jit(solution)/shard_map/all_to_all | solution.py:347
  20.1 0.0 copy-start.8
  20.1 0.0 copy-start.10
  20.1 0.0 copy-start.12
  20.1 3.0 %collective-permute-start.1 = (bf16[1,3,32,1024]{3,2,1,0:T(8,128)(2,1)}, bf16[1,3,32,1024]{3,2,1,0:T(8,128)(2,1)}, u32[]{:S(2)}, u32[]{:S(2)}) collective-permute-start(bf16[1,3,32,1024]{3,2,1,0:T(8,128)(2,1)} %get-tuple-element.40.refs_5_), channel_id=1, source_target_pairs={{0,16},{8,24},{16,0},{24,8},{1,17},{9,25},{17,1},{25,9},{2,18},{10... | collective-permute-start | bytes 589832 | tf_op jit(solution)/shard_map/ppermute | solution.py:267
  23.1 1.0 %collective-permute-start.2 = (bf16[1,3,32,1024]{3,2,1,0:T(8,128)(2,1)}, bf16[1,3,32,1024]{3,2,1,0:T(8,128)(2,1)}, u32[]{:S(2)}, u32[]{:S(2)}) collective-permute-start(bf16[1,3,32,1024]{3,2,1,0:T(8,128)(2,1)} %get-tuple-element.41.refs_6_), channel_id=1, source_target_pairs={{0,24},{8,16},{16,8},{24,0},{1,25},{9,17},{17,9},{25,1},{2,26},{10... | collective-permute-start | bytes 589832 | tf_op jit(solution)/shard_map/ppermute | solution.py:267
  24.1 0.5 spread.1.temper_ref
  24.6 0.0 collective-permute-done.4.refs_3_
  24.6 0.0 collective-permute-done.3.refs_2_
  24.6 1.3 %collective-permute-done.refs_1_ = bf16[2,3,32,1024]{3,2,1,0:T(8,128)(2,1)S(1)} collective-permute-done((bf16[2,3,32,1024]{3,2,1,0:T(8,128)(2,1)S(1)}, bf16[2,3,32,1024]{3,2,1,0:T(8,128)(2,1)S(1)}, u32[]{:S(2)}, u32[]{:S(2)}) %collective-permute-start) | collective-permute-done | bytes 393248 | tf_op jit(solution)/shard_map/ppermute | solution.py:267
  26.0 5.4 %column.3 = (bf16[1,3,32,1024]{3,2,1,0:T(8,128)(2,1)S(1)}, bf16[1,3,32,1024]{3,2,1,0:T(8,128)(2,1)S(1)}, bf16[1,3,32,1024]{3,2,1,0:T(8,128)(2,1)S(1)}, bf16[1,3,32,1024]{3,2,1,0:T(8,128)(2,1)S(1)}) custom-call(f32[1,1024]{1,0:T(1,128)S(1)} %spread.1.temper_ref, f32[1,1024]{1,0:T(1,128)S(1)} %bitcast.16, bf16[1024,1024]{1,0:T(8,128)(2,1)S(1)} %copy-done.8, ...), custom_call_target="tpu_custom_call" | custom-call | flops 199999995904 | bytes 1 | tf_op jit(solution)/shard_map/column/pallas_call | solution.py:376
  31.4 1.1 %collective-permute-start.5 = (bf16[1,3,32,1024]{3,2,1,0:T(8,128)(2,1)S(1)}, bf16[1,3,32,1024]{3,2,1,0:T(8,128)(2,1)S(1)}, u32[]{:S(2)}, u32[]{:S(2)}) collective-permute-start(bf16[1,3,32,1024]{3,2,1,0:T(8,128)(2,1)S(1)} %get-tuple-element.52), channel_id=1, source_target_pairs={{0,8},{8,0},{16,24},{24,16},{1,9},{9,1},{17,25},{25,17},{2,10},{10... | collective-permute-start | bytes 589832 | tf_op jit(solution)/shard_map/ppermute | solution.py:267
  32.5 2.6 %collective-permute-start.9 = (bf16[1,3,32,1024]{3,2,1,0:T(8,128)(2,1)S(1)}, bf16[1,3,32,1024]{3,2,1,0:T(8,128)(2,1)S(1)}, u32[]{:S(2)}, u32[]{:S(2)}) collective-permute-start(bf16[1,3,32,1024]{3,2,1,0:T(8,128)(2,1)S(1)} %get-tuple-element.59), channel_id=1, source_target_pairs={{0,16},{8,24},{16,0},{24,8},{1,17},{9,25},{17,1},{25,9},{2,18},{10... | collective-permute-start | bytes 589832 | tf_op jit(solution)/shard_map/ppermute | solution.py:267
  35.1 0.8 %collective-permute-start.10 = (bf16[1,3,32,1024]{3,2,1,0:T(8,128)(2,1)S(1)}, bf16[1,3,32,1024]{3,2,1,0:T(8,128)(2,1)S(1)}, u32[]{:S(2)}, u32[]{:S(2)}) collective-permute-start(bf16[1,3,32,1024]{3,2,1,0:T(8,128)(2,1)S(1)} %get-tuple-element.60), channel_id=1, source_target_pairs={{0,24},{8,16},{16,8},{24,0},{1,25},{9,17},{17,9},{25,1},{2,26},{10... | collective-permute-start | bytes 589832 | tf_op jit(solution)/shard_map/ppermute | solution.py:267
  35.8 0.0 all-to-all-done.shares_ref
  35.9 1.4 %share.1 = bf16[192,256]{1,0:T(8,128)(2,1)S(1)} custom-call(bf16[8,192,256]{2,1,0:T(8,128)(2,1)} %all-to-all-done.shares_ref), custom_call_target="tpu_custom_call" | custom-call | flops 5000000000 | bytes 1 | tf_op jit(solution)/shard_map/share/pallas_call | solution.py:352
  37.3 10.7 %all_gather.3 = bf16[1536,256]{1,0:T(8,128)(2,1)S(1)} all-gather(bf16[192,256]{1,0:T(8,128)(2,1)S(1)} %share.1), channel_id=1, replica_groups=mesh['hap'=4,'pos'=8] {'pos'}, dimensions={0}, use_global_device_ids=true | all-gather | bytes 884736 | tf_op jit(solution)/shard_map/all_gather | solution.py:362
  48.0 0.0 collective-permute-done.1.refs_2_
  48.0 0.0 collective-permute-done.2.refs_3_
  48.0 0.0 copy-start.2
  48.0 0.0 copy-start.3
  48.0 0.0 copy-start.5
  48.1 6.5 %column.2 = (bf16[1,3,32,1024]{3,2,1,0:T(8,128)(2,1)S(1)}, bf16[1,3,32,1024]{3,2,1,0:T(8,128)(2,1)S(1)}, bf16[1,3,32,1024]{3,2,1,0:T(8,128)(2,1)S(1)}, bf16[1,3,32,1024]{3,2,1,0:T(8,128)(2,1)S(1)}) custom-call(f32[1,1024]{1,0:T(1,128)S(1)} %spread.1.temper_ref, f32[1,1024]{1,0:T(1,128)S(1)} %bitcast.17, bf16[1024,1024]{1,0:T(8,128)(2,1)S(1)} %copy-done.9, ...), custom_call_target="tpu_custom_call" | custom-call | flops 30000001024 | bytes 1 | tf_op jit(solution)/shard_map/column/pallas_call | solution.py:376
  54.5 0.0 collective-permute-done.5.refs_1_
  54.6 5.0 %collective-permute-start.6 = (bf16[1,3,32,1024]{3,2,1,0:T(8,128)(2,1)S(1)}, bf16[1,3,32,1024]{3,2,1,0:T(8,128)(2,1)S(1)}, u32[]{:S(2)}, u32[]{:S(2)}) collective-permute-start(bf16[1,3,32,1024]{3,2,1,0:T(8,128)(2,1)S(1)} %get-tuple-element.53), channel_id=1, source_target_pairs={{0,16},{8,24},{16,0},{24,8},{1,17},{9,25},{17,1},{25,9},{2,18},{10... | collective-permute-start | bytes 589832 | tf_op jit(solution)/shard_map/ppermute | solution.py:267
  59.5 0.4 collective-permute-start.7
  60.0 0.2 collective-permute-start.8
  60.2 6.7 %along.1.acc_ref = f32[3,8,32,1024]{3,2,1,0:T(8,128)S(1)} custom-call(s32[1]{0:T(128)} %bitcast.place_ref, bf16[3,4,2,32,1024]{4,3,2,1,0:T(8,128)(2,1)S(1)} %bitcast.13, f32[1,1024]{1,0:T(1,128)S(1)} %bitcast.18, bf16[1024,1024]{1,0:T(8,128)(2,1)S(1)} %copy-done.2, bf16[8,3,64,256]{3,2,1,0:T(8,128)(2,1)S(1)} %bitcast.14, f32[1,1024]{1,0:T(1,128)S(1)} %bitcast.19, ...), custom_call_target="tpu_custom_call" | custom-call | bytes 1 | tf_op jit(solution)/shard_map/along/pallas_call | solution.py:396
  66.9 0.0 collective-permute-done.9.refs_2_
  66.9 0.0 collective-permute-done.10.refs_3_
  67.0 2.2 %finish.3.refs_2_ = bf16[3,4,2,32,1024]{4,3,2,1,0:T(8,128)(2,1)} custom-call(s32[1]{0:T(128)} %bitcast.place_ref, f32[3,8,32,1024]{3,2,1,0:T(8,128)S(1)} %along.1.acc_ref, bf16[1024,1024]{1,0:T(8,128)(2,1)S(1)} %copy-done, bf16[1,3,32,1024]{3,2,1,0:T(8,128)(2,1)S(1)} %get-tuple-element.57.refs_0_, ...), custom_call_target="tpu_custom_call" | custom-call | flops 30000001024 | bytes 1 | tf_op jit(solution)/shard_map/finish/pallas_call | solution.py:417
  69.2 4.7 %collective-permute-done.8.refs_1_ = bf16[1,3,32,1024]{3,2,1,0:T(8,128)(2,1)S(1)} collective-permute-done((bf16[1,3,32,1024]{3,2,1,0:T(8,128)(2,1)S(1)}, bf16[1,3,32,1024]{3,2,1,0:T(8,128)(2,1)S(1)}, u32[]{:S(2)}, u32[]{:S(2)}) %collective-permute-start.8) | collective-permute-done | bytes 196640 | tf_op jit(solution)/shard_map/ppermute | solution.py:267
  73.8 1.5 %finish.4.refs_2_ = bf16[3,4,2,32,1024]{4,3,2,1,0:T(8,128)(2,1)} custom-call(s32[1]{0:T(128)} %bitcast.place_ref, f32[3,8,32,1024]{3,2,1,0:T(8,128)S(1)} %along.1.acc_ref, bf16[1024,1024]{1,0:T(8,128)(2,1)S(1)} %copy-done, bf16[1,3,32,1024]{3,2,1,0:T(8,128)(2,1)S(1)} %get-tuple-element.55.refs_0_, ...), custom_call_target="tpu_custom_call", output_to_operand_aliasing={{}: (5, {})} | custom-call | bytes 1 | tf_op jit(solution)/shard_map/finish/pallas_call | solution.py:417
  75.4 0.0 collective-permute-done.6.refs_0_
  75.4 0.0 collective-permute-done.7.refs_1_
  75.4 1.5 %finish.5 = bf16[3,4,2,32,1024]{4,3,2,1,0:T(8,128)(2,1)} custom-call(s32[1]{0:T(128)} %bitcast.place_ref, f32[3,8,32,1024]{3,2,1,0:T(8,128)S(1)} %along.1.acc_ref, bf16[1024,1024]{1,0:T(8,128)(2,1)S(1)} %copy-done, bf16[1,3,32,1024]{3,2,1,0:T(8,128)(2,1)S(1)} %collective-permute-done.6.refs_0_, ...), custom_call_target="tpu_custom_call", output_to_operand_aliasing={{}: (5, {})} | custom-call | bytes 1 | tf_op jit(solution)/shard_map/finish/pallas_call | solution.py:417
  (23 shorter events, 0.0 us)
Async XLA Ops:
  0.0 7.1 %copy-start.1 = (bf16[3,256,1024]{2,1,0:T(8,128)(2,1)S(1)}, bf16[3,256,1024]{2,1,0:T(8,128)(2,1)}, u32[]{:S(2)}) copy-start(bf16[3,256,1024]{2,1,0:T(8,128)(2,1)} %param.12) | copy-start | bytes 4718596
  0.0 7.1 %copy-start.4 = (f32[1024]{0:T(1024)S(1)}, f32[1024]{0:T(1024)}, u32[]{:S(2)}) copy-start(f32[1024]{0:T(1024)} %param.13) | copy-start | bytes 12292
  2.1 22.6 %collective-permute-start.4 = (bf16[1,3,32,1024]{3,2,1,0:T(8,128)(2,1)}, bf16[1,3,32,1024]{3,2,1,0:T(8,128)(2,1)S(1)}, u32[]{:S(2)}, u32[]{:S(2)}) collective-permute-start(bf16[1,3,32,1024]{3,2,1,0:T(8,128)(2,1)} %get-tuple-element.61), channel_id=1, source_target_pairs={{0,24},{8,16},{16,8},{24,0},{1,25},{9,17},{17,9},{25,1},{2,26},{10... | collective-permute-start | bytes 589832 | tf_op jit(solution)/shard_map/ppermute | solution.py:267
  7.1 17.5 %collective-permute-start.3 = (bf16[1,3,32,1024]{3,2,1,0:T(8,128)(2,1)S(1)}, bf16[1,3,32,1024]{3,2,1,0:T(8,128)(2,1)S(1)}, u32[]{:S(2)}, u32[]{:S(2)}) collective-permute-start(bf16[1,3,32,1024]{3,2,1,0:T(8,128)(2,1)S(1)} %get-tuple-element.62), channel_id=1, source_target_pairs={{0,16},{8,24},{16,0},{24,8},{1,17},{9,25},{17,1},{25,9},{2,18},{10... | collective-permute-start | bytes 589832 | tf_op jit(solution)/shard_map/ppermute | solution.py:267
  7.1 2.3 %copy-start.6 = (bf16[1024,1024]{1,0:T(8,128)(2,1)S(1)}, bf16[1024,1024]{1,0:T(8,128)(2,1)}, u32[]{:S(2)}) copy-start(bf16[1024,1024]{1,0:T(8,128)(2,1)} %refs_7_.1) | copy-start | bytes 6291460
  7.1 2.4 %copy-start.7 = (bf16[1024,1024]{1,0:T(8,128)(2,1)S(1)}, bf16[1024,1024]{1,0:T(8,128)(2,1)}, u32[]{:S(2)}) copy-start(bf16[1024,1024]{1,0:T(8,128)(2,1)} %refs_8_.1) | copy-start | bytes 6291460
  8.9 6.9 %copy-start.15 = (bf16[1,3,32,1024]{3,2,1,0:T(8,128)(2,1)}, bf16[1,3,32,1024]{3,2,1,0:T(8,128)(2,1)S(1)}, u32[]{:S(2)}) copy-start(bf16[1,3,32,1024]{3,2,1,0:T(8,128)(2,1)S(1)} %get-tuple-element.44.refs_4_.refs_0_) | copy-start | bytes 589828
  8.9 17.0 %collective-permute-start = (bf16[2,3,32,1024]{3,2,1,0:T(8,128)(2,1)S(1)}, bf16[2,3,32,1024]{3,2,1,0:T(8,128)(2,1)S(1)}, u32[]{:S(2)}, u32[]{:S(2)}) collective-permute-start(bf16[2,3,32,1024]{3,2,1,0:T(8,128)(2,1)S(1)} %get-tuple-element.34.refs_1_), channel_id=1, source_target_pairs={{0,8},{8,0},{16,24},{24,16},{1,9},{9,1},{17,25},{25,17},{2,10},{10... | collective-permute-start | bytes 1179656 | tf_op jit(solution)/shard_map/ppermute | solution.py:267
  9.5 14.6 %copy-start.14 = (f32[16]{0:T(128)S(1)}, f32[16]{0:T(128)}, u32[]{:S(2)}) copy-start(f32[16]{0:T(128)} %temper_ref.1) | copy-start | bytes 196
  15.9 20.0 %all-to-all-start = ((bf16[8,192,256]{2,1,0:T(8,128)(2,1)}), bf16[8,192,256]{2,1,0:T(8,128)(2,1)}, u32[]{:S(2)}, u32[]{:S(2)}) async-start(bf16[8,192,256]{2,1,0:T(8,128)(2,1)} %bitcast.3), calls=%async_computation | async-start | bytes 1572864 | tf_op jit(solution)/shard_map/all_to_all | solution.py:347
  20.1 5.9 %copy-start.8 = (bf16[1024,1024]{1,0:T(8,128)(2,1)S(1)}, bf16[1024,1024]{1,0:T(8,128)(2,1)}, u32[]{:S(2)}) copy-start(bf16[1024,1024]{1,0:T(8,128)(2,1)} %wq_ref.5) | copy-start | bytes 6291460
  20.1 5.9 %copy-start.10 = (bf16[1024,1024]{1,0:T(8,128)(2,1)S(1)}, bf16[1024,1024]{1,0:T(8,128)(2,1)}, u32[]{:S(2)}) copy-start(bf16[1024,1024]{1,0:T(8,128)(2,1)} %wk_ref.3) | copy-start | bytes 6291460
  20.1 5.9 %copy-start.12 = (bf16[1024,1024]{1,0:T(8,128)(2,1)S(1)}, bf16[1024,1024]{1,0:T(8,128)(2,1)}, u32[]{:S(2)}) copy-start(bf16[1024,1024]{1,0:T(8,128)(2,1)} %wv_ref.3) | copy-start | bytes 6291460
  20.1 27.9 %collective-permute-start.1 = (bf16[1,3,32,1024]{3,2,1,0:T(8,128)(2,1)}, bf16[1,3,32,1024]{3,2,1,0:T(8,128)(2,1)}, u32[]{:S(2)}, u32[]{:S(2)}) collective-permute-start(bf16[1,3,32,1024]{3,2,1,0:T(8,128)(2,1)} %get-tuple-element.40.refs_5_), channel_id=1, source_target_pairs={{0,16},{8,24},{16,0},{24,8},{1,17},{9,25},{17,1},{25,9},{2,18},{10... | collective-permute-start | bytes 589832 | tf_op jit(solution)/shard_map/ppermute | solution.py:267
  23.1 24.9 %collective-permute-start.2 = (bf16[1,3,32,1024]{3,2,1,0:T(8,128)(2,1)}, bf16[1,3,32,1024]{3,2,1,0:T(8,128)(2,1)}, u32[]{:S(2)}, u32[]{:S(2)}) collective-permute-start(bf16[1,3,32,1024]{3,2,1,0:T(8,128)(2,1)} %get-tuple-element.41.refs_6_), channel_id=1, source_target_pairs={{0,24},{8,16},{16,8},{24,0},{1,25},{9,17},{17,9},{25,1},{2,26},{10... | collective-permute-start | bytes 589832 | tf_op jit(solution)/shard_map/ppermute | solution.py:267
  31.4 23.2 %collective-permute-start.5 = (bf16[1,3,32,1024]{3,2,1,0:T(8,128)(2,1)S(1)}, bf16[1,3,32,1024]{3,2,1,0:T(8,128)(2,1)S(1)}, u32[]{:S(2)}, u32[]{:S(2)}) collective-permute-start(bf16[1,3,32,1024]{3,2,1,0:T(8,128)(2,1)S(1)} %get-tuple-element.52), channel_id=1, source_target_pairs={{0,8},{8,0},{16,24},{24,16},{1,9},{9,1},{17,25},{25,17},{2,10},{10... | collective-permute-start | bytes 589832 | tf_op jit(solution)/shard_map/ppermute | solution.py:267
  32.5 34.5 %collective-permute-start.9 = (bf16[1,3,32,1024]{3,2,1,0:T(8,128)(2,1)S(1)}, bf16[1,3,32,1024]{3,2,1,0:T(8,128)(2,1)S(1)}, u32[]{:S(2)}, u32[]{:S(2)}) collective-permute-start(bf16[1,3,32,1024]{3,2,1,0:T(8,128)(2,1)S(1)} %get-tuple-element.59), channel_id=1, source_target_pairs={{0,16},{8,24},{16,0},{24,8},{1,17},{9,25},{17,1},{25,9},{2,18},{10... | collective-permute-start | bytes 589832 | tf_op jit(solution)/shard_map/ppermute | solution.py:267
  35.1 12.9 %copy-start.16 = (bf16[1,3,32,1024]{3,2,1,0:T(8,128)(2,1)S(1)}, bf16[1,3,32,1024]{3,2,1,0:T(8,128)(2,1)}, u32[]{:S(2)}) copy-start(bf16[1,3,32,1024]{3,2,1,0:T(8,128)(2,1)} %copy-done.15) | copy-start | bytes 589828
  35.1 31.9 %collective-permute-start.10 = (bf16[1,3,32,1024]{3,2,1,0:T(8,128)(2,1)S(1)}, bf16[1,3,32,1024]{3,2,1,0:T(8,128)(2,1)S(1)}, u32[]{:S(2)}, u32[]{:S(2)}) collective-permute-start(bf16[1,3,32,1024]{3,2,1,0:T(8,128)(2,1)S(1)} %get-tuple-element.60), channel_id=1, source_target_pairs={{0,24},{8,16},{16,8},{24,0},{1,25},{9,17},{17,9},{25,1},{2,26},{10... | collective-permute-start | bytes 589832 | tf_op jit(solution)/shard_map/ppermute | solution.py:267
  35.9 12.1 %copy-start.9 = (bf16[1024,1024]{1,0:T(8,128)(2,1)S(1)}, bf16[1024,1024]{1,0:T(8,128)(2,1)}, u32[]{:S(2)}) copy-start(bf16[1024,1024]{1,0:T(8,128)(2,1)} %wq_ref.5) | copy-start | bytes 6291460
  35.9 12.2 %copy-start.11 = (bf16[1024,1024]{1,0:T(8,128)(2,1)S(1)}, bf16[1024,1024]{1,0:T(8,128)(2,1)}, u32[]{:S(2)}) copy-start(bf16[1024,1024]{1,0:T(8,128)(2,1)} %wk_ref.3) | copy-start | bytes 6291460
  35.9 12.2 %copy-start.13 = (bf16[1024,1024]{1,0:T(8,128)(2,1)S(1)}, bf16[1024,1024]{1,0:T(8,128)(2,1)}, u32[]{:S(2)}) copy-start(bf16[1024,1024]{1,0:T(8,128)(2,1)} %wv_ref.3) | copy-start | bytes 6291460
  48.0 12.2 %copy-start.2 = (bf16[1024,1024]{1,0:T(8,128)(2,1)S(1)}, bf16[1024,1024]{1,0:T(8,128)(2,1)}, u32[]{:S(2)}) copy-start(bf16[1024,1024]{1,0:T(8,128)(2,1)} %wq_ref.3) | copy-start | bytes 6291460
  48.0 12.2 %copy-start.3 = (bf16[1024,1024]{1,0:T(8,128)(2,1)S(1)}, bf16[1024,1024]{1,0:T(8,128)(2,1)}, u32[]{:S(2)}) copy-start(bf16[1024,1024]{1,0:T(8,128)(2,1)} %wo_ref.4) | copy-start | bytes 6291460
  48.0 12.1 %copy-start.5 = (f32[1024]{0:T(1024)S(1)}, f32[1024]{0:T(1024)}, u32[]{:S(2)}) copy-start(f32[1024]{0:T(1024)} %param.18) | copy-start | bytes 12292
  54.6 20.8 %collective-permute-start.6 = (bf16[1,3,32,1024]{3,2,1,0:T(8,128)(2,1)S(1)}, bf16[1,3,32,1024]{3,2,1,0:T(8,128)(2,1)S(1)}, u32[]{:S(2)}, u32[]{:S(2)}) collective-permute-start(bf16[1,3,32,1024]{3,2,1,0:T(8,128)(2,1)S(1)} %get-tuple-element.53), channel_id=1, source_target_pairs={{0,16},{8,24},{16,0},{24,8},{1,17},{9,25},{17,1},{25,9},{2,18},{10... | collective-permute-start | bytes 589832 | tf_op jit(solution)/shard_map/ppermute | solution.py:267
  59.5 15.8 %collective-permute-start.7 = (bf16[1,3,32,1024]{3,2,1,0:T(8,128)(2,1)S(1)}, bf16[1,3,32,1024]{3,2,1,0:T(8,128)(2,1)S(1)}, u32[]{:S(2)}, u32[]{:S(2)}) collective-permute-start(bf16[1,3,32,1024]{3,2,1,0:T(8,128)(2,1)S(1)} %get-tuple-element.54), channel_id=1, source_target_pairs={{0,24},{8,16},{16,8},{24,0},{1,25},{9,17},{17,9},{25,1},{2,26},{10... | collective-permute-start | bytes 589832 | tf_op jit(solution)/shard_map/ppermute | solution.py:267
  60.0 13.9 %collective-permute-start.8 = (bf16[1,3,32,1024]{3,2,1,0:T(8,128)(2,1)S(1)}, bf16[1,3,32,1024]{3,2,1,0:T(8,128)(2,1)S(1)}, u32[]{:S(2)}, u32[]{:S(2)}) collective-permute-start(bf16[1,3,32,1024]{3,2,1,0:T(8,128)(2,1)S(1)} %get-tuple-element.56), channel_id=1, source_target_pairs={{0,8},{8,0},{16,24},{24,16},{1,9},{9,1},{17,25},{25,17},{2,10},{10... | collective-permute-start | bytes 589832 | tf_op jit(solution)/shard_map/ppermute | solution.py:267
  60.2 6.8 %copy-start = (bf16[1024,1024]{1,0:T(8,128)(2,1)S(1)}, bf16[1024,1024]{1,0:T(8,128)(2,1)}, u32[]{:S(2)}) copy-start(bf16[1024,1024]{1,0:T(8,128)(2,1)} %wo_ref.7) | copy-start | bytes 6291460

commit v5 on v4

--- a/solution.py
+++ b/solution.py
@@ -16,10 +16,7 @@
 PACK_COST = 10
 ROW_COST = 20
 SPREAD_COST = 5
-RAW = True
 SHARE_COST = 5
-TIE_C1 = 'state'
-TIE_BACK = True
 ALONG_COST = 0
 COLUMN_COSTS = (200, 30)
 FINISH_COSTS = (30, 0, 0)
@@ -84,7 +81,8 @@
     z = place_ref[0]
     gain = gain_ref[...]
     for (c, k), (index, slot) in places.items():
-        outs[index][slot, 0] = normalise(rows_ref[0, z ^ k, c], gain)
+        for r in range(rows_ref.shape[0]):
+            outs[index][slot, r] = normalise(rows_ref[r, z ^ k, c], gain)
 
 
 def share_kernel(shares_ref, out_ref):
@@ -96,17 +94,23 @@
 
 def row_kernel(head_dim, places, *refs):
     wk_ref, wv_ref, state_ref = refs[-3:]
-    rows = jnp.concatenate([refs[index][slot, 0] for index, slot in places.values()], axis=0)
+    haps = state_ref.shape[1]
+    rows = jnp.concatenate(
+        [refs[index][slot, r] for r in range(haps) for index, slot in places.values()], axis=0
+    )
+    length = rows.shape[0] // haps
     keys = plain(rows, wk_ref[...]).astype(BF16)
     values = plain(rows, wv_ref[...]).astype(BF16)
     first_head = lane_of((head_dim, 2 * LANES)) % LANES < head_dim
-    for pair in range(keys.shape[1] // LANES):
-        lower = pair * LANES
-        plus, minus = feature_pair(keys[:, lower : lower + LANES].astype(F32))
-        features = jnp.concatenate([plus, minus], axis=1)
-        state = first_dims(values[:, lower : lower + LANES], features)
-        folded = jnp.where(first_head, state[:head_dim], state[head_dim:])
-        state_ref[pair, 0] = folded.astype(BF16)
+    for r in range(haps):
+        here = slice(r * length, (r + 1) * length)
+        for pair in range(keys.shape[1] // LANES):
+            lanes = slice(pair * LANES, (pair + 1) * LANES)
+            plus, minus = feature_pair(keys[here, lanes].astype(F32))
+            features = jnp.concatenate([plus, minus], axis=1)
+            state = first_dims(values[here, lanes], features)
+            folded = jnp.where(first_head, state[:head_dim], state[head_dim:])
+            state_ref[pair, r] = folded.astype(BF16)
 
 
 def along_kernel(
@@ -275,9 +279,6 @@
             places[c, k] = (len(lengths), 0)
             lengths.append(chunks if k == 1 else 1)
     shapes = [jax.ShapeDtypeStruct((many, haps, depth, width), BF16) for many in lengths]
-    hap_specs = [
-        pl.BlockSpec((many, 1, depth, width), lambda r: (0, r, 0, 0)) for many in lengths
-    ]
     rows_spec = pl.BlockSpec((1, n, chunks, depth, width), lambda r: (r, 0, 0, 0, 0))
 
     def piece_spec(c, k):
@@ -286,9 +287,9 @@
 
     normed = pl.pallas_call(
         functools.partial(pack_kernel, places),
-        grid=(haps,),
-        in_specs=[SCALARS, rows_spec, whole(gain_flat)],
-        out_specs=hap_specs,
+        grid=(1,),
+        in_specs=[SCALARS, whole(rows5), whole(gain_flat)],
+        out_specs=[whole(shape) for shape in shapes],
         out_shape=shapes,
         compiler_params=PARAMS,
         cost_estimate=cost(PACK_COST),
@@ -296,9 +297,8 @@
     )(place, rows5, gain_flat)
 
     def send_all(arrays):
-        got = {}
         sent = list(arrays)
-        for c, k in order[1:] if n > 1 else []:
+        for c, k in order:
             index, slot = places[c, k]
             if k > 0 and slot == 0:
                 sent[index] = exchange(arrays[index], k)
@@ -308,9 +308,9 @@
     state_shape = (pairs, haps, head_dim, 2 * LANES)
     state = pl.pallas_call(
         functools.partial(row_kernel, head_dim, places),
-        grid=(haps,),
-        in_specs=hap_specs + [once(key_row)] * 2,
-        out_specs=state_spec,
+        grid=(1,),
+        in_specs=[whole(array) for array in normed] + [once(key_row)] * 2,
+        out_specs=pl.BlockSpec(state_shape, lambda *_: (0, 0, 0, 0)),
         out_shape=jax.ShapeDtypeStruct(state_shape, BF16),
         compiler_params=PARAMS,
         cost_estimate=cost(ROW_COST),
@@ -328,14 +328,12 @@
         name="spread",
     )(temper)
 
-    waiting = [
-        index for index in range(len(lengths)) if any(places[c, k][0] == index for c, k in order if c > 0 and k > 1)
-    ]
+    waiting = [places[c, k][0] for c, k in order if c > 0 and k > 1]
     held, state = lax.optimization_barrier(([normed[index] for index in waiting], state))
     queue = list(normed)
     for index, array in zip(waiting, held):
         queue[index] = array
-    raw = [k > 1 and RAW for k in range(n)]
+    raw = [k > 1 for k in range(n)]
     for k in range(n):
         if raw[k]:
             queue[places[0, k][0]] = lax.dynamic_index_in_dim(
@@ -365,20 +363,18 @@
     one_spec = pl.BlockSpec(one_piece.shape, lambda *_: (0, 0, 0, 0))
     returned = {}
     for c in range(chunks):
-        blocks = [arrived[places[c, k][0]] for k in range(n)]
+        ks = [0, 1][:n] + list(range(2, n))[:: -1 if c > 0 else 1]
+        blocks = [arrived[places[c, k][0]] for k in ks]
         if c > 0:
-            if TIE_C1 == "state":
-                state = add_up(shares)
-                blocks, state = lax.optimization_barrier((blocks, state))
-            elif TIE_C1 == "shares":
-                blocks, shares = lax.optimization_barrier((blocks, shares))
+            state = add_up(shares)
+            blocks, state = lax.optimization_barrier((blocks, state))
         every = pltpu.VMEM((haps * n, depth, width), BF16)
         results = pl.pallas_call(
-            functools.partial(column_kernel, head_dim, raw if c == 0 else [False] * n),
+            functools.partial(column_kernel, head_dim, [raw[k] and c == 0 for k in ks]),
             grid=(1,),
             in_specs=[whole(temper_flat), whole(gain_flat)]
             + [once(query_col)] * 3
-            + [piece_spec(c, k) for k in range(n)],
+            + [piece_spec(c, k) for k in ks],
             out_specs=[one_spec] * n,
             out_shape=[one_piece] * n,
             scratch_shapes=[every] * 3,
@@ -386,10 +382,10 @@
             cost_estimate=cost(COLUMN_COSTS[c]),
             name="column",
         )(temper_flat, gain_flat, query_col, key_col, value_col, *blocks)
-        if TIE_BACK and c > 0 and n > 1:
+        if c > 0 and n > 1:
             results, returned[0, 1] = lax.optimization_barrier((results, returned[0, 1]))
-        for k in range(n):
-            returned[c, k] = exchange(results[k], k) if k > 0 else results[k]
+        for k, result in zip(ks, results):
+            returned[c, k] = exchange(result, k) if k > 0 else result
 
     if state is None:
         state = add_up(shares)
@@ -412,6 +408,7 @@
     for pieces, weight in zip(groups, FINISH_COSTS):
         if not pieces:
             continue
+        pieces = pieces[::-1]
         extra = [] if updated is None else [updated]
         count = len(pieces)
         updated = pl.pallas_call(

time: 77.3 us -> 77 us (level)
  starting transfers between devices: 23.8 us -> 21.8 us
  waiting for transfers between devices: 5.98 us -> 7.85 us
    ppermute x11, starting transfers between devices: 19.6 us -> 17.6 us  [exchange(): return lax.ppermute(array, 'hap', [(i, i ^ k) for i in range(n)])]
    ppermute x11, waiting for transfers between devices: 5.98 us -> 7.85 us  [exchange(): return lax.ppermute(array, 'hap', [(i, i ^ k) for i in range(n)])]
  transfers between devices with their start and end apart: 12 -> 12, of which waited for: 2 -> 5; matrix products, arithmetic and copies ran while one was open for 0% -> 0% of each run, Pallas kernels for 42% -> 41%
where the time goes in v5:
time: 77 us; the launch traced here: 76.8 us
  Pallas kernels  33.3 us (43%)
  starting transfers between devices  21.8 us (28%)
  blocking collectives  10.6 us (14%)
  waiting for transfers between devices  7.85 us (10%)
  local copies, waits for them, and re-layouts  2.72 us (4%)
    ppermute x11, starting transfers between devices, exchange(): return lax.ppermute(array, 'hap', [(i, i ^ k) for i in range(n)])  17.6 us
    pallas_call x2, Pallas kernels, local(): pl.pallas_call(functools.partial(column_kernel, head_dim, [raw[k] and c =...  11.9 us
    all_gather x1, blocking collectives, add_up(): return lax.all_gather(share, 'pos', axis=0, tiled=True).reshape(state_shape)  10.6 us
    ppermute x11, waiting for transfers between devices, exchange(): return lax.ppermute(array, 'hap', [(i, i ^ k) for i in range(n)])  7.85 us
    pallas_call x1, Pallas kernels, local(): pl.pallas_call(functools.partial(along_kernel, head_dim, order), grid=(ha...  6.73 us
    pallas_call x1, Pallas kernels, local(): pl.pallas_call(functools.partial(row_kernel, head_dim, places), grid=(1,)...  6.25 us
    pallas_call x3, Pallas kernels, local(): pl.pallas_call(functools.partial(finish_kernel, pieces, order), grid=(1,)...  5.25 us
    all_to_all x1, starting transfers between devices, local(): lax.all_to_all(shares, 'pos', split_axis=0, concat_axis=0, tiled=True)  4.21 us
  transfers between devices with their start and end apart: 12, of which 5 were waited for; matrix products, arithmetic and copies ran while one was open for 0% of the time, Pallas kernels for 41%

profile of v5, /device:TPU:0, one launch (start us, length us, event | category | flops | bytes accessed | tf_op | source)
XLA Modules:
  0.0 76.8 jit_solution(6168860618086119117)
XLA Ops:
  0.0 1.3 %slice.5 = bf16[3,4,1,32,1024]{4,3,2,1,0:T(8,128)(2,1)S(1)} slice(bf16[3,4,2,32,1024]{4,3,2,1,0:T(8,128)(2,1)} %bitcast.11), slice={[0:3], [0:4], [0:1], [0:32], [0:1024]} | slice | bytes 1572864 | tf_op jit(solution)/shard_map/slice | solution.py:340
  1.3 0.7 dynamic-slice_bitcast_fusion
  2.1 5.0 %collective-permute-start.4 = (bf16[1,3,32,1024]{3,2,1,0:T(8,128)(2,1)}, bf16[1,3,32,1024]{3,2,1,0:T(8,128)(2,1)S(1)}, u32[]{:S(2)}, u32[]{:S(2)}) collective-permute-start(bf16[1,3,32,1024]{3,2,1,0:T(8,128)(2,1)} %get-tuple-element.61), channel_id=1, source_target_pairs={{0,24},{8,16},{16,8},{24,0},{1,25},{9,17},{17,9},{25,1},{2,26},{10... | collective-permute-start | bytes 589832 | tf_op jit(solution)/shard_map/ppermute | solution.py:271
  7.1 0.0 collective-permute-start.3
  7.1 0.0 copy-start.6
  7.1 0.0 copy-start.7
  7.1 1.3 %pack.1 = (bf16[1,3,32,1024]{3,2,1,0:T(8,128)(2,1)S(1)}, bf16[2,3,32,1024]{3,2,1,0:T(8,128)(2,1)S(1)}, bf16[1,3,32,1024]{3,2,1,0:T(8,128)(2,1)S(1)}, bf16[1,3,32...) custom-call(s32[1]{0:T(128)} %bitcast.place_ref, ...), custom_call_target="tpu_custom_call" | custom-call | flops 10000000000 | bytes 1 | tf_op jit(solution)/shard_map/pack/pallas_call | solution.py:288
  8.4 0.5 collective-permute-start
  9.0 0.6 copy-done.7
  9.6 6.2 %row.1 = bf16[8,3,64,256]{3,2,1,0:T(8,128)(2,1)} custom-call(bf16[1,3,32,1024]{3,2,1,0:T(8,128)(2,1)S(1)} %get-tuple-element.37.refs_0_, bf16[2,3,32,1024]{3,2,1,0:T(8,128)(2,1)S(1)} %get-tuple-element.34.refs_1_, bf16[1,3,32,1024]{3,2,1,0:T(8,128)(2,1)S(1)} %get-tuple-element.38.refs_2_, bf16[1,3,32,1024]{3,2,1,0:T(8,128)(2,1)S(1)} %get-tuple-element.39.refs_3_, ...), custom_call_target="tpu_custom_call" | custom-call | flops 20000000000 | bytes 1 | tf_op jit(solution)/shard_map/row/pallas_call | solution.py:309
  15.8 0.0 copy-done.15
  15.8 4.2 %all-to-all-start = ((bf16[8,192,256]{2,1,0:T(8,128)(2,1)}), bf16[8,192,256]{2,1,0:T(8,128)(2,1)}, u32[]{:S(2)}, u32[]{:S(2)}) async-start(bf16[8,192,256]{2,1,0:T(8,128)(2,1)} %bitcast.3), calls=%async_computation | async-start | bytes 1572864 | tf_op jit(solution)/shard_map/all_to_all | solution.py:345
  20.0 0.0 copy-start.8
  20.0 0.0 copy-start.10
  20.1 0.0 copy-start.12
  20.1 3.3 %collective-permute-start.1 = (bf16[1,3,32,1024]{3,2,1,0:T(8,128)(2,1)}, bf16[1,3,32,1024]{3,2,1,0:T(8,128)(2,1)}, u32[]{:S(2)}, u32[]{:S(2)}) collective-permute-start(bf16[1,3,32,1024]{3,2,1,0:T(8,128)(2,1)} %get-tuple-element.40.refs_6_), channel_id=1, source_target_pairs={{0,24},{8,16},{16,8},{24,0},{1,25},{9,17},{17,9},{25,1},{2,26},{10... | collective-permute-start | bytes 589832 | tf_op jit(solution)/shard_map/ppermute | solution.py:271
  23.4 0.0 collective-permute-start.2
  23.4 0.5 spread.1.temper_ref
  23.9 0.0 collective-permute-done.4.refs_3_
  23.9 0.2 collective-permute-done.3.refs_2_
  24.1 0.8 %collective-permute-done.refs_1_ = bf16[2,3,32,1024]{3,2,1,0:T(8,128)(2,1)S(1)} collective-permute-done((bf16[2,3,32,1024]{3,2,1,0:T(8,128)(2,1)S(1)}, bf16[2,3,32,1024]{3,2,1,0:T(8,128)(2,1)S(1)}, u32[]{:S(2)}, u32[]{:S(2)}) %collective-permute-start) | collective-permute-done | bytes 393248 | tf_op jit(solution)/shard_map/ppermute | solution.py:271
  25.0 5.4 %column.3 = (bf16[1,3,32,1024]{3,2,1,0:T(8,128)(2,1)S(1)}, bf16[1,3,32,1024]{3,2,1,0:T(8,128)(2,1)S(1)}, bf16[1,3,32,1024]{3,2,1,0:T(8,128)(2,1)S(1)}, bf16[1,3,32,1024]{3,2,1,0:T(8,128)(2,1)S(1)}) custom-call(f32[1,1024]{1,0:T(1,128)S(1)} %spread.1.temper_ref, f32[1,1024]{1,0:T(1,128)S(1)} %bitcast.16, bf16[1024,1024]{1,0:T(8,128)(2,1)S(1)} %copy-done.8, ...), custom_call_target="tpu_custom_call" | custom-call | flops 199999995904 | bytes 1 | tf_op jit(solution)/shard_map/column/pallas_call | solution.py:372
  30.4 1.9 %collective-permute-start.5 = (bf16[1,3,32,1024]{3,2,1,0:T(8,128)(2,1)S(1)}, bf16[1,3,32,1024]{3,2,1,0:T(8,128)(2,1)S(1)}, u32[]{:S(2)}, u32[]{:S(2)}) collective-permute-start(bf16[1,3,32,1024]{3,2,1,0:T(8,128)(2,1)S(1)} %get-tuple-element.52), channel_id=1, source_target_pairs={{0,8},{8,0},{16,24},{24,16},{1,9},{9,1},{17,25},{25,17},{2,10},{10... | collective-permute-start | bytes 589832 | tf_op jit(solution)/shard_map/ppermute | solution.py:271
  32.3 1.9 %collective-permute-start.9 = (bf16[1,3,32,1024]{3,2,1,0:T(8,128)(2,1)S(1)}, bf16[1,3,32,1024]{3,2,1,0:T(8,128)(2,1)S(1)}, u32[]{:S(2)}, u32[]{:S(2)}) collective-permute-start(bf16[1,3,32,1024]{3,2,1,0:T(8,128)(2,1)S(1)} %get-tuple-element.57), channel_id=1, source_target_pairs={{0,24},{8,16},{16,8},{24,0},{1,25},{9,17},{17,9},{25,1},{2,26},{10... | collective-permute-start | bytes 589832 | tf_op jit(solution)/shard_map/ppermute | solution.py:271
  34.2 0.5 collective-permute-start.10
  34.7 0.0 all-to-all-done.shares_ref
  34.7 1.4 %share.1 = bf16[192,256]{1,0:T(8,128)(2,1)S(1)} custom-call(bf16[8,192,256]{2,1,0:T(8,128)(2,1)} %all-to-all-done.shares_ref), custom_call_target="tpu_custom_call" | custom-call | flops 5000000000 | bytes 1 | tf_op jit(solution)/shard_map/share/pallas_call | solution.py:350
  36.1 10.6 %all_gather.3 = bf16[1536,256]{1,0:T(8,128)(2,1)S(1)} all-gather(bf16[192,256]{1,0:T(8,128)(2,1)S(1)} %share.1), channel_id=1, replica_groups=mesh['hap'=4,'pos'=8] {'pos'}, dimensions={0}, use_global_device_ids=true | all-gather | bytes 884736 | tf_op jit(solution)/shard_map/all_gather | solution.py:360
  46.7 0.0 collective-permute-done.1.refs_2_
  46.7 3.5 %collective-permute-done.2.refs_3_ = bf16[1,3,32,1024]{3,2,1,0:T(8,128)(2,1)} collective-permute-done((bf16[1,3,32,1024]{3,2,1,0:T(8,128)(2,1)}, bf16[1,3,32,1024]{3,2,1,0:T(8,128)(2,1)}, u32[]{:S(2)}, u32[]{:S(2)}) %collective-permute-start.2) | collective-permute-done | bytes 196640 | tf_op jit(solution)/shard_map/ppermute | solution.py:271
  50.2 0.0 copy-done.16
  50.3 0.0 copy-start.2
  50.3 0.0 copy-start.3
  50.3 0.0 copy-start.5
  50.3 6.5 %column.2 = (bf16[1,3,32,1024]{3,2,1,0:T(8,128)(2,1)S(1)}, bf16[1,3,32,1024]{3,2,1,0:T(8,128)(2,1)S(1)}, bf16[1,3,32,1024]{3,2,1,0:T(8,128)(2,1)S(1)}, bf16[1,3,32,1024]{3,2,1,0:T(8,128)(2,1)S(1)}) custom-call(f32[1,1024]{1,0:T(1,128)S(1)} %spread.1.temper_ref, f32[1,1024]{1,0:T(1,128)S(1)} %bitcast.17, bf16[1024,1024]{1,0:T(8,128)(2,1)S(1)} %copy-done.9, ...), custom_call_target="tpu_custom_call" | custom-call | flops 30000001024 | bytes 1 | tf_op jit(solution)/shard_map/column/pallas_call | solution.py:372
  56.8 0.0 collective-permute-done.5.refs_2_
  56.8 2.9 %collective-permute-start.6 = (bf16[1,3,32,1024]{3,2,1,0:T(8,128)(2,1)S(1)}, bf16[1,3,32,1024]{3,2,1,0:T(8,128)(2,1)S(1)}, u32[]{:S(2)}, u32[]{:S(2)}) collective-permute-start(bf16[1,3,32,1024]{3,2,1,0:T(8,128)(2,1)S(1)} %get-tuple-element.53), channel_id=1, source_target_pairs={{0,24},{8,16},{16,8},{24,0},{1,25},{9,17},{17,9},{25,1},{2,26},{10... | collective-permute-start | bytes 589832 | tf_op jit(solution)/shard_map/ppermute | solution.py:271
  59.7 0.0 collective-permute-start.7
  59.7 1.5 %collective-permute-start.8 = (bf16[1,3,32,1024]{3,2,1,0:T(8,128)(2,1)S(1)}, bf16[1,3,32,1024]{3,2,1,0:T(8,128)(2,1)S(1)}, u32[]{:S(2)}, u32[]{:S(2)}) collective-permute-start(bf16[1,3,32,1024]{3,2,1,0:T(8,128)(2,1)S(1)} %get-tuple-element.55), channel_id=1, source_target_pairs={{0,8},{8,0},{16,24},{24,16},{1,9},{9,1},{17,25},{25,17},{2,10},{10... | collective-permute-start | bytes 589832 | tf_op jit(solution)/shard_map/ppermute | solution.py:271
  61.3 6.7 %along.1.acc_ref = f32[3,8,32,1024]{3,2,1,0:T(8,128)S(1)} custom-call(s32[1]{0:T(128)} %bitcast.place_ref, bf16[3,4,2,32,1024]{4,3,2,1,0:T(8,128)(2,1)S(1)} %bitcast.13, f32[1,1024]{1,0:T(1,128)S(1)} %bitcast.18, bf16[1024,1024]{1,0:T(8,128)(2,1)S(1)} %copy-done.2, bf16[8,3,64,256]{3,2,1,0:T(8,128)(2,1)S(1)} %bitcast.14, f32[1,1024]{1,0:T(1,128)S(1)} %bitcast.19, ...), custom_call_target="tpu_custom_call" | custom-call | bytes 1 | tf_op jit(solution)/shard_map/along/pallas_call | solution.py:392
  68.0 0.0 collective-permute-done.9.refs_0_
  68.0 0.0 collective-permute-done.10.refs_1_
  68.0 2.2 %finish.3.refs_2_ = bf16[3,4,2,32,1024]{4,3,2,1,0:T(8,128)(2,1)} custom-call(s32[1]{0:T(128)} %bitcast.place_ref, f32[3,8,32,1024]{3,2,1,0:T(8,128)S(1)} %along.1.acc_ref, bf16[1024,1024]{1,0:T(8,128)(2,1)S(1)} %copy-done, bf16[1,3,32,1024]{3,2,1,0:T(8,128)(2,1)S(1)} %collective-permute-done.9.refs_0_, ...), custom_call_target="tpu_custom_call" | custom-call | flops 30000001024 | bytes 1 | tf_op jit(solution)/shard_map/finish/pallas_call | solution.py:414
  70.2 1.3 %collective-permute-done.8.refs_0_ = bf16[1,3,32,1024]{3,2,1,0:T(8,128)(2,1)S(1)} collective-permute-done((bf16[1,3,32,1024]{3,2,1,0:T(8,128)(2,1)S(1)}, bf16[1,3,32,1024]{3,2,1,0:T(8,128)(2,1)S(1)}, u32[]{:S(2)}, u32[]{:S(2)}) %collective-permute-start.8) | collective-permute-done | bytes 196640 | tf_op jit(solution)/shard_map/ppermute | solution.py:271
  71.6 1.5 %finish.4.refs_2_ = bf16[3,4,2,32,1024]{4,3,2,1,0:T(8,128)(2,1)} custom-call(s32[1]{0:T(128)} %bitcast.place_ref, f32[3,8,32,1024]{3,2,1,0:T(8,128)S(1)} %along.1.acc_ref, bf16[1024,1024]{1,0:T(8,128)(2,1)S(1)} %copy-done, bf16[1,3,32,1024]{3,2,1,0:T(8,128)(2,1)S(1)} %collective-permute-done.8.refs_0_, ...), custom_call_target="tpu_custom_call", output_to_operand_aliasing={{}: (5, {})} | custom-call | bytes 1 | tf_op jit(solution)/shard_map/finish/pallas_call | solution.py:414
  73.1 0.0 collective-permute-done.6.refs_0_
  73.1 2.0 %collective-permute-done.7.refs_1_ = bf16[1,3,32,1024]{3,2,1,0:T(8,128)(2,1)S(1)} collective-permute-done((bf16[1,3,32,1024]{3,2,1,0:T(8,128)(2,1)S(1)}, bf16[1,3,32,1024]{3,2,1,0:T(8,128)(2,1)S(1)}, u32[]{:S(2)}, u32[]{:S(2)}) %collective-permute-start.7) | collective-permute-done | bytes 196640 | tf_op jit(solution)/shard_map/ppermute | solution.py:271
  75.1 1.5 %finish.5 = bf16[3,4,2,32,1024]{4,3,2,1,0:T(8,128)(2,1)} custom-call(s32[1]{0:T(128)} %bitcast.place_ref, f32[3,8,32,1024]{3,2,1,0:T(8,128)S(1)} %along.1.acc_ref, bf16[1024,1024]{1,0:T(8,128)(2,1)S(1)} %copy-done, bf16[1,3,32,1024]{3,2,1,0:T(8,128)(2,1)S(1)} %collective-permute-done.6.refs_0_, ...), custom_call_target="tpu_custom_call", output_to_operand_aliasing={{}: (5, {})} | custom-call | bytes 1 | tf_op jit(solution)/shard_map/finish/pallas_call | solution.py:414
  (23 shorter events, 0.0 us)
Async XLA Ops:
  0.0 7.1 %copy-start.1 = (bf16[3,256,1024]{2,1,0:T(8,128)(2,1)S(1)}, bf16[3,256,1024]{2,1,0:T(8,128)(2,1)}, u32[]{:S(2)}) copy-start(bf16[3,256,1024]{2,1,0:T(8,128)(2,1)} %param.12) | copy-start | bytes 4718596
  0.0 7.1 %copy-start.4 = (f32[1024]{0:T(1024)S(1)}, f32[1024]{0:T(1024)}, u32[]{:S(2)}) copy-start(f32[1024]{0:T(1024)} %param.13) | copy-start | bytes 12292
  2.1 21.9 %collective-permute-start.4 = (bf16[1,3,32,1024]{3,2,1,0:T(8,128)(2,1)}, bf16[1,3,32,1024]{3,2,1,0:T(8,128)(2,1)S(1)}, u32[]{:S(2)}, u32[]{:S(2)}) collective-permute-start(bf16[1,3,32,1024]{3,2,1,0:T(8,128)(2,1)} %get-tuple-element.61), channel_id=1, source_target_pairs={{0,24},{8,16},{16,8},{24,0},{1,25},{9,17},{17,9},{25,1},{2,26},{10... | collective-permute-start | bytes 589832 | tf_op jit(solution)/shard_map/ppermute | solution.py:271
  7.1 17.0 %collective-permute-start.3 = (bf16[1,3,32,1024]{3,2,1,0:T(8,128)(2,1)S(1)}, bf16[1,3,32,1024]{3,2,1,0:T(8,128)(2,1)S(1)}, u32[]{:S(2)}, u32[]{:S(2)}) collective-permute-start(bf16[1,3,32,1024]{3,2,1,0:T(8,128)(2,1)S(1)} %get-tuple-element.62), channel_id=1, source_target_pairs={{0,16},{8,24},{16,0},{24,8},{1,17},{9,25},{17,1},{25,9},{2,18},{10... | collective-permute-start | bytes 589832 | tf_op jit(solution)/shard_map/ppermute | solution.py:271
  7.1 1.8 %copy-start.6 = (bf16[1024,1024]{1,0:T(8,128)(2,1)S(1)}, bf16[1024,1024]{1,0:T(8,128)(2,1)}, u32[]{:S(2)}) copy-start(bf16[1024,1024]{1,0:T(8,128)(2,1)} %refs_7_.1) | copy-start | bytes 6291460
  7.1 2.4 %copy-start.7 = (bf16[1024,1024]{1,0:T(8,128)(2,1)S(1)}, bf16[1024,1024]{1,0:T(8,128)(2,1)}, u32[]{:S(2)}) copy-start(bf16[1024,1024]{1,0:T(8,128)(2,1)} %refs_8_.1) | copy-start | bytes 6291460
  8.4 7.4 %copy-start.15 = (bf16[1,3,32,1024]{3,2,1,0:T(8,128)(2,1)}, bf16[1,3,32,1024]{3,2,1,0:T(8,128)(2,1)S(1)}, u32[]{:S(2)}) copy-start(bf16[1,3,32,1024]{3,2,1,0:T(8,128)(2,1)S(1)} %get-tuple-element.44.refs_4_.refs_0_) | copy-start | bytes 589828
  8.4 16.5 %collective-permute-start = (bf16[2,3,32,1024]{3,2,1,0:T(8,128)(2,1)S(1)}, bf16[2,3,32,1024]{3,2,1,0:T(8,128)(2,1)S(1)}, u32[]{:S(2)}, u32[]{:S(2)}) collective-permute-start(bf16[2,3,32,1024]{3,2,1,0:T(8,128)(2,1)S(1)} %get-tuple-element.34.refs_1_), channel_id=1, source_target_pairs={{0,8},{8,0},{16,24},{24,16},{1,9},{9,1},{17,25},{25,17},{2,10},{10... | collective-permute-start | bytes 1179656 | tf_op jit(solution)/shard_map/ppermute | solution.py:271
  9.6 13.8 %copy-start.14 = (f32[16]{0:T(128)S(1)}, f32[16]{0:T(128)}, u32[]{:S(2)}) copy-start(f32[16]{0:T(128)} %temper_ref.1) | copy-start | bytes 196
  15.8 18.9 %all-to-all-start = ((bf16[8,192,256]{2,1,0:T(8,128)(2,1)}), bf16[8,192,256]{2,1,0:T(8,128)(2,1)}, u32[]{:S(2)}, u32[]{:S(2)}) async-start(bf16[8,192,256]{2,1,0:T(8,128)(2,1)} %bitcast.3), calls=%async_computation | async-start | bytes 1572864 | tf_op jit(solution)/shard_map/all_to_all | solution.py:345
  20.0 4.9 %copy-start.8 = (bf16[1024,1024]{1,0:T(8,128)(2,1)S(1)}, bf16[1024,1024]{1,0:T(8,128)(2,1)}, u32[]{:S(2)}) copy-start(bf16[1024,1024]{1,0:T(8,128)(2,1)} %wq_ref.5) | copy-start | bytes 6291460
  20.0 4.9 %copy-start.10 = (bf16[1024,1024]{1,0:T(8,128)(2,1)S(1)}, bf16[1024,1024]{1,0:T(8,128)(2,1)}, u32[]{:S(2)}) copy-start(bf16[1024,1024]{1,0:T(8,128)(2,1)} %wk_ref.3) | copy-start | bytes 6291460
  20.1 4.9 %copy-start.12 = (bf16[1024,1024]{1,0:T(8,128)(2,1)S(1)}, bf16[1024,1024]{1,0:T(8,128)(2,1)}, u32[]{:S(2)}) copy-start(bf16[1024,1024]{1,0:T(8,128)(2,1)} %wv_ref.3) | copy-start | bytes 6291460
  20.1 26.6 %collective-permute-start.1 = (bf16[1,3,32,1024]{3,2,1,0:T(8,128)(2,1)}, bf16[1,3,32,1024]{3,2,1,0:T(8,128)(2,1)}, u32[]{:S(2)}, u32[]{:S(2)}) collective-permute-start(bf16[1,3,32,1024]{3,2,1,0:T(8,128)(2,1)} %get-tuple-element.40.refs_6_), channel_id=1, source_target_pairs={{0,24},{8,16},{16,8},{24,0},{1,25},{9,17},{17,9},{25,1},{2,26},{10... | collective-permute-start | bytes 589832 | tf_op jit(solution)/shard_map/ppermute | solution.py:271
  23.4 26.9 %collective-permute-start.2 = (bf16[1,3,32,1024]{3,2,1,0:T(8,128)(2,1)}, bf16[1,3,32,1024]{3,2,1,0:T(8,128)(2,1)}, u32[]{:S(2)}, u32[]{:S(2)}) collective-permute-start(bf16[1,3,32,1024]{3,2,1,0:T(8,128)(2,1)} %get-tuple-element.41.refs_5_), channel_id=1, source_target_pairs={{0,16},{8,24},{16,0},{24,8},{1,17},{9,25},{17,1},{25,9},{2,18},{10... | collective-permute-start | bytes 589832 | tf_op jit(solution)/shard_map/ppermute | solution.py:271
  30.4 26.4 %collective-permute-start.5 = (bf16[1,3,32,1024]{3,2,1,0:T(8,128)(2,1)S(1)}, bf16[1,3,32,1024]{3,2,1,0:T(8,128)(2,1)S(1)}, u32[]{:S(2)}, u32[]{:S(2)}) collective-permute-start(bf16[1,3,32,1024]{3,2,1,0:T(8,128)(2,1)S(1)} %get-tuple-element.52), channel_id=1, source_target_pairs={{0,8},{8,0},{16,24},{24,16},{1,9},{9,1},{17,25},{25,17},{2,10},{10... | collective-permute-start | bytes 589832 | tf_op jit(solution)/shard_map/ppermute | solution.py:271
  32.3 35.7 %collective-permute-start.9 = (bf16[1,3,32,1024]{3,2,1,0:T(8,128)(2,1)S(1)}, bf16[1,3,32,1024]{3,2,1,0:T(8,128)(2,1)S(1)}, u32[]{:S(2)}, u32[]{:S(2)}) collective-permute-start(bf16[1,3,32,1024]{3,2,1,0:T(8,128)(2,1)S(1)} %get-tuple-element.57), channel_id=1, source_target_pairs={{0,24},{8,16},{16,8},{24,0},{1,25},{9,17},{17,9},{25,1},{2,26},{10... | collective-permute-start | bytes 589832 | tf_op jit(solution)/shard_map/ppermute | solution.py:271
  34.2 16.1 %copy-start.16 = (bf16[1,3,32,1024]{3,2,1,0:T(8,128)(2,1)S(1)}, bf16[1,3,32,1024]{3,2,1,0:T(8,128)(2,1)}, u32[]{:S(2)}) copy-start(bf16[1,3,32,1024]{3,2,1,0:T(8,128)(2,1)} %copy-done.15) | copy-start | bytes 589828
  34.2 33.8 %collective-permute-start.10 = (bf16[1,3,32,1024]{3,2,1,0:T(8,128)(2,1)S(1)}, bf16[1,3,32,1024]{3,2,1,0:T(8,128)(2,1)S(1)}, u32[]{:S(2)}, u32[]{:S(2)}) collective-permute-start(bf16[1,3,32,1024]{3,2,1,0:T(8,128)(2,1)S(1)} %get-tuple-element.58), channel_id=1, source_target_pairs={{0,16},{8,24},{16,0},{24,8},{1,17},{9,25},{17,1},{25,9},{2,18},{10... | collective-permute-start | bytes 589832 | tf_op jit(solution)/shard_map/ppermute | solution.py:271
  34.7 15.6 %copy-start.9 = (bf16[1024,1024]{1,0:T(8,128)(2,1)S(1)}, bf16[1024,1024]{1,0:T(8,128)(2,1)}, u32[]{:S(2)}) copy-start(bf16[1024,1024]{1,0:T(8,128)(2,1)} %wq_ref.5) | copy-start | bytes 6291460
  34.7 15.6 %copy-start.11 = (bf16[1024,1024]{1,0:T(8,128)(2,1)S(1)}, bf16[1024,1024]{1,0:T(8,128)(2,1)}, u32[]{:S(2)}) copy-start(bf16[1024,1024]{1,0:T(8,128)(2,1)} %wk_ref.3) | copy-start | bytes 6291460
  34.7 15.6 %copy-start.13 = (bf16[1024,1024]{1,0:T(8,128)(2,1)S(1)}, bf16[1024,1024]{1,0:T(8,128)(2,1)}, u32[]{:S(2)}) copy-start(bf16[1024,1024]{1,0:T(8,128)(2,1)} %wv_ref.3) | copy-start | bytes 6291460
  50.3 11.0 %copy-start.2 = (bf16[1024,1024]{1,0:T(8,128)(2,1)S(1)}, bf16[1024,1024]{1,0:T(8,128)(2,1)}, u32[]{:S(2)}) copy-start(bf16[1024,1024]{1,0:T(8,128)(2,1)} %wq_ref.3) | copy-start | bytes 6291460
  50.3 11.0 %copy-start.3 = (bf16[1024,1024]{1,0:T(8,128)(2,1)S(1)}, bf16[1024,1024]{1,0:T(8,128)(2,1)}, u32[]{:S(2)}) copy-start(bf16[1024,1024]{1,0:T(8,128)(2,1)} %wo_ref.4) | copy-start | bytes 6291460
  50.3 11.0 %copy-start.5 = (f32[1024]{0:T(1024)S(1)}, f32[1024]{0:T(1024)}, u32[]{:S(2)}) copy-start(f32[1024]{0:T(1024)} %param.18) | copy-start | bytes 12292
  56.8 16.3 %collective-permute-start.6 = (bf16[1,3,32,1024]{3,2,1,0:T(8,128)(2,1)S(1)}, bf16[1,3,32,1024]{3,2,1,0:T(8,128)(2,1)S(1)}, u32[]{:S(2)}, u32[]{:S(2)}) collective-permute-start(bf16[1,3,32,1024]{3,2,1,0:T(8,128)(2,1)S(1)} %get-tuple-element.53), channel_id=1, source_target_pairs={{0,24},{8,16},{16,8},{24,0},{1,25},{9,17},{17,9},{25,1},{2,26},{10... | collective-permute-start | bytes 589832 | tf_op jit(solution)/shard_map/ppermute | solution.py:271
  59.7 15.4 %collective-permute-start.7 = (bf16[1,3,32,1024]{3,2,1,0:T(8,128)(2,1)S(1)}, bf16[1,3,32,1024]{3,2,1,0:T(8,128)(2,1)S(1)}, u32[]{:S(2)}, u32[]{:S(2)}) collective-permute-start(bf16[1,3,32,1024]{3,2,1,0:T(8,128)(2,1)S(1)} %get-tuple-element.54), channel_id=1, source_target_pairs={{0,16},{8,24},{16,0},{24,8},{1,17},{9,25},{17,1},{25,9},{2,18},{10... | collective-permute-start | bytes 589832 | tf_op jit(solution)/shard_map/ppermute | solution.py:271
  59.7 11.8 %collective-permute-start.8 = (bf16[1,3,32,1024]{3,2,1,0:T(8,128)(2,1)S(1)}, bf16[1,3,32,1024]{3,2,1,0:T(8,128)(2,1)S(1)}, u32[]{:S(2)}, u32[]{:S(2)}) collective-permute-start(bf16[1,3,32,1024]{3,2,1,0:T(8,128)(2,1)S(1)} %get-tuple-element.55), channel_id=1, source_target_pairs={{0,8},{8,0},{16,24},{24,16},{1,9},{9,1},{17,25},{25,17},{2,10},{10... | collective-permute-start | bytes 589832 | tf_op jit(solution)/shard_map/ppermute | solution.py:271
  61.3 6.8 %copy-start = (bf16[1024,1024]{1,0:T(8,128)(2,1)S(1)}, bf16[1024,1024]{1,0:T(8,128)(2,1)}, u32[]{:S(2)}) copy-start(bf16[1024,1024]{1,0:T(8,128)(2,1)} %wo_ref.7) | copy-start | bytes 6291460

commit v6 on v5

--- a/solution.py
+++ b/solution.py
@@ -195,23 +195,16 @@
 
 def finish_kernel(pieces, order, place_ref, acc_ref, wo_ref, *refs):
     mixed = refs[: len(pieces)]
-    out_ref, acc, result, acc_sems, out_sems = refs[-5:]
+    out_ref, result, out_sems = refs[-3:]
     z = place_ref[0]
     _one, haps, depth, _width = mixed[0].shape
-    loads = [
-        pltpu.make_async_copy(acc_ref.at[:, order.index(piece)], acc.at[i], acc_sems.at[i])
-        for i, piece in enumerate(pieces)
-    ]
-    for load in loads:
-        load.start()
     flat = jnp.concatenate([block[0, r] for block in mixed for r in range(haps)], axis=0)
     col_out = plain(flat, wo_ref[...])
     stores = []
     for i, (c, k) in enumerate(pieces):
-        loads[i].wait()
         for r in range(haps):
             lower = (i * haps + r) * depth
-            result[i, r] = (acc[i, r] + col_out[lower : lower + depth]).astype(BF16)
+            result[i, r] = (acc_ref[r, order.index((c, k))] + col_out[lower : lower + depth]).astype(BF16)
         store = pltpu.make_async_copy(result.at[i], out_ref.at[:, z ^ k, c], out_sems.at[i])
         store.start()
         stores.append(store)
@@ -414,15 +407,13 @@
         updated = pl.pallas_call(
             functools.partial(finish_kernel, pieces, order),
             grid=(1,),
-            in_specs=[SCALARS, anywhere, once(out_col)]
+            in_specs=[SCALARS, once(acc), once(out_col)]
             + [one_spec] * count
             + [anywhere] * len(extra),
             out_specs=anywhere,
             out_shape=jax.ShapeDtypeStruct(rows5.shape, BF16),
             scratch_shapes=[
-                pltpu.VMEM((count, haps, depth, width), F32),
                 pltpu.VMEM((count, haps, depth, width), BF16),
-                pltpu.SemaphoreType.DMA((count,)),
                 pltpu.SemaphoreType.DMA((count,)),
             ],
             input_output_aliases={3 + count: 0} if extra else {},

time: 77 us -> 76.8 us (level)
    pallas_call x3, Pallas kernels: 5.25 us -> 4.47 us  [local(): pl.pallas_call(functools.partial(finish_kernel, pieces, order), grid=(1,)...]
where the time goes in v6:
time: 76.8 us; the launch traced here: 76.6 us
  Pallas kernels  32.6 us (42%)
  starting transfers between devices  21.8 us (28%)
  blocking collectives  10.6 us (14%)
  waiting for transfers between devices  8.43 us (11%)
  local copies, waits for them, and re-layouts  2.72 us (4%)
    ppermute x11, starting transfers between devices, exchange(): return lax.ppermute(array, 'hap', [(i, i ^ k) for i in range(n)])  17.6 us
    pallas_call x2, Pallas kernels, local(): pl.pallas_call(functools.partial(column_kernel, head_dim, [raw[k] and c =...  11.9 us
    all_gather x1, blocking collectives, add_up(): return lax.all_gather(share, 'pos', axis=0, tiled=True).reshape(state_shape)  10.6 us
    ppermute x11, waiting for transfers between devices, exchange(): return lax.ppermute(array, 'hap', [(i, i ^ k) for i in range(n)])  8.43 us
    pallas_call x1, Pallas kernels, local(): pl.pallas_call(functools.partial(along_kernel, head_dim, order), grid=(ha...  6.73 us
    pallas_call x1, Pallas kernels, local(): pl.pallas_call(functools.partial(row_kernel, head_dim, places), grid=(1,)...  6.25 us
    pallas_call x3, Pallas kernels, local(): pl.pallas_call(functools.partial(finish_kernel, pieces, order), grid=(1,)...  4.47 us
    all_to_all x1, starting transfers between devices, local(): lax.all_to_all(shares, 'pos', split_axis=0, concat_axis=0, tiled=True)  4.21 us
  transfers between devices with their start and end apart: 12, of which 5 were waited for; matrix products, arithmetic and copies ran while one was open for 0% of the time, Pallas kernels for 41%

profile of v6, /device:TPU:0, one launch (start us, length us, event | category | flops | bytes accessed | tf_op | source)
XLA Modules:
  0.0 76.6 jit_solution(1650628946251930950)
XLA Ops:
  0.0 1.3 %slice.5 = bf16[3,4,1,32,1024]{4,3,2,1,0:T(8,128)(2,1)S(1)} slice(bf16[3,4,2,32,1024]{4,3,2,1,0:T(8,128)(2,1)} %bitcast.11), slice={[0:3], [0:4], [0:1], [0:32], [0:1024]} | slice | bytes 1572864 | tf_op jit(solution)/shard_map/slice | solution.py:333
  1.3 0.7 dynamic-slice_bitcast_fusion
  2.1 5.0 %collective-permute-start.4 = (bf16[1,3,32,1024]{3,2,1,0:T(8,128)(2,1)}, bf16[1,3,32,1024]{3,2,1,0:T(8,128)(2,1)S(1)}, u32[]{:S(2)}, u32[]{:S(2)}) collective-permute-start(bf16[1,3,32,1024]{3,2,1,0:T(8,128)(2,1)} %get-tuple-element.61), channel_id=1, source_target_pairs={{0,24},{8,16},{16,8},{24,0},{1,25},{9,17},{17,9},{25,1},{2,26},{10... | collective-permute-start | bytes 589832 | tf_op jit(solution)/shard_map/ppermute | solution.py:264
  7.1 0.0 collective-permute-start.3
  7.1 0.0 copy-done.1
  7.1 0.0 copy-start.6
  7.1 0.0 copy-start.7
  7.1 1.3 %pack.1 = (bf16[1,3,32,1024]{3,2,1,0:T(8,128)(2,1)S(1)}, bf16[2,3,32,1024]{3,2,1,0:T(8,128)(2,1)S(1)}, bf16[1,3,32,1024]{3,2,1,0:T(8,128)(2,1)S(1)}, bf16[1,3,32...) custom-call(s32[1]{0:T(128)} %bitcast.place_ref, ...), custom_call_target="tpu_custom_call" | custom-call | flops 10000000000 | bytes 1 | tf_op jit(solution)/shard_map/pack/pallas_call | solution.py:281
  8.4 0.5 collective-permute-start
  9.0 0.6 copy-done.7
  9.6 6.2 %row.1 = bf16[8,3,64,256]{3,2,1,0:T(8,128)(2,1)} custom-call(bf16[1,3,32,1024]{3,2,1,0:T(8,128)(2,1)S(1)} %get-tuple-element.37.refs_0_, bf16[2,3,32,1024]{3,2,1,0:T(8,128)(2,1)S(1)} %get-tuple-element.34.refs_1_, bf16[1,3,32,1024]{3,2,1,0:T(8,128)(2,1)S(1)} %get-tuple-element.38.refs_2_, bf16[1,3,32,1024]{3,2,1,0:T(8,128)(2,1)S(1)} %get-tuple-element.39.refs_3_, ...), custom_call_target="tpu_custom_call" | custom-call | flops 20000000000 | bytes 1 | tf_op jit(solution)/shard_map/row/pallas_call | solution.py:302
  15.8 0.0 copy-done.15
  15.8 4.2 %all-to-all-start = ((bf16[8,192,256]{2,1,0:T(8,128)(2,1)}), bf16[8,192,256]{2,1,0:T(8,128)(2,1)}, u32[]{:S(2)}, u32[]{:S(2)}) async-start(bf16[8,192,256]{2,1,0:T(8,128)(2,1)} %bitcast.3), calls=%async_computation | async-start | bytes 1572864 | tf_op jit(solution)/shard_map/all_to_all | solution.py:338
  20.0 0.0 copy-start.8
  20.0 0.0 copy-start.10
  20.1 0.0 copy-start.12
  20.1 3.3 %collective-permute-start.1 = (bf16[1,3,32,1024]{3,2,1,0:T(8,128)(2,1)}, bf16[1,3,32,1024]{3,2,1,0:T(8,128)(2,1)}, u32[]{:S(2)}, u32[]{:S(2)}) collective-permute-start(bf16[1,3,32,1024]{3,2,1,0:T(8,128)(2,1)} %get-tuple-element.40.refs_6_), channel_id=1, source_target_pairs={{0,24},{8,16},{16,8},{24,0},{1,25},{9,17},{17,9},{25,1},{2,26},{10... | collective-permute-start | bytes 589832 | tf_op jit(solution)/shard_map/ppermute | solution.py:264
  23.4 0.0 collective-permute-start.2
  23.4 0.5 spread.1.temper_ref
  23.9 0.0 collective-permute-done.4.refs_3_
  23.9 0.2 collective-permute-done.3.refs_2_
  24.1 0.8 %collective-permute-done.refs_1_ = bf16[2,3,32,1024]{3,2,1,0:T(8,128)(2,1)S(1)} collective-permute-done((bf16[2,3,32,1024]{3,2,1,0:T(8,128)(2,1)S(1)}, bf16[2,3,32,1024]{3,2,1,0:T(8,128)(2,1)S(1)}, u32[]{:S(2)}, u32[]{:S(2)}) %collective-permute-start) | collective-permute-done | bytes 393248 | tf_op jit(solution)/shard_map/ppermute | solution.py:264
  25.0 5.4 %column.3 = (bf16[1,3,32,1024]{3,2,1,0:T(8,128)(2,1)S(1)}, bf16[1,3,32,1024]{3,2,1,0:T(8,128)(2,1)S(1)}, bf16[1,3,32,1024]{3,2,1,0:T(8,128)(2,1)S(1)}, bf16[1,3,32,1024]{3,2,1,0:T(8,128)(2,1)S(1)}) custom-call(f32[1,1024]{1,0:T(1,128)S(1)} %spread.1.temper_ref, f32[1,1024]{1,0:T(1,128)S(1)} %bitcast.16, bf16[1024,1024]{1,0:T(8,128)(2,1)S(1)} %copy-done.8, ...), custom_call_target="tpu_custom_call" | custom-call | flops 199999995904 | bytes 1 | tf_op jit(solution)/shard_map/column/pallas_call | solution.py:365
  30.4 1.9 %collective-permute-start.5 = (bf16[1,3,32,1024]{3,2,1,0:T(8,128)(2,1)S(1)}, bf16[1,3,32,1024]{3,2,1,0:T(8,128)(2,1)S(1)}, u32[]{:S(2)}, u32[]{:S(2)}) collective-permute-start(bf16[1,3,32,1024]{3,2,1,0:T(8,128)(2,1)S(1)} %get-tuple-element.52), channel_id=1, source_target_pairs={{0,8},{8,0},{16,24},{24,16},{1,9},{9,1},{17,25},{25,17},{2,10},{10... | collective-permute-start | bytes 589832 | tf_op jit(solution)/shard_map/ppermute | solution.py:264
  32.3 1.9 %collective-permute-start.9 = (bf16[1,3,32,1024]{3,2,1,0:T(8,128)(2,1)S(1)}, bf16[1,3,32,1024]{3,2,1,0:T(8,128)(2,1)S(1)}, u32[]{:S(2)}, u32[]{:S(2)}) collective-permute-start(bf16[1,3,32,1024]{3,2,1,0:T(8,128)(2,1)S(1)} %get-tuple-element.57), channel_id=1, source_target_pairs={{0,24},{8,16},{16,8},{24,0},{1,25},{9,17},{17,9},{25,1},{2,26},{10... | collective-permute-start | bytes 589832 | tf_op jit(solution)/shard_map/ppermute | solution.py:264
  34.2 0.5 collective-permute-start.10
  34.7 0.0 all-to-all-done.shares_ref
  34.7 1.4 %share.1 = bf16[192,256]{1,0:T(8,128)(2,1)S(1)} custom-call(bf16[8,192,256]{2,1,0:T(8,128)(2,1)} %all-to-all-done.shares_ref), custom_call_target="tpu_custom_call" | custom-call | flops 5000000000 | bytes 1 | tf_op jit(solution)/shard_map/share/pallas_call | solution.py:343
  36.1 10.6 %all_gather.3 = bf16[1536,256]{1,0:T(8,128)(2,1)S(1)} all-gather(bf16[192,256]{1,0:T(8,128)(2,1)S(1)} %share.1), channel_id=1, replica_groups=mesh['hap'=4,'pos'=8] {'pos'}, dimensions={0}, use_global_device_ids=true | all-gather | bytes 884736 | tf_op jit(solution)/shard_map/all_gather | solution.py:353
  46.7 0.0 collective-permute-done.1.refs_2_
  46.7 3.5 %collective-permute-done.2.refs_3_ = bf16[1,3,32,1024]{3,2,1,0:T(8,128)(2,1)} collective-permute-done((bf16[1,3,32,1024]{3,2,1,0:T(8,128)(2,1)}, bf16[1,3,32,1024]{3,2,1,0:T(8,128)(2,1)}, u32[]{:S(2)}, u32[]{:S(2)}) %collective-permute-start.2) | collective-permute-done | bytes 196640 | tf_op jit(solution)/shard_map/ppermute | solution.py:264
  50.3 0.0 copy-start.2
  50.3 0.0 copy-start.3
  50.3 0.0 copy-start.5
  50.3 6.5 %column.2 = (bf16[1,3,32,1024]{3,2,1,0:T(8,128)(2,1)S(1)}, bf16[1,3,32,1024]{3,2,1,0:T(8,128)(2,1)S(1)}, bf16[1,3,32,1024]{3,2,1,0:T(8,128)(2,1)S(1)}, bf16[1,3,32,1024]{3,2,1,0:T(8,128)(2,1)S(1)}) custom-call(f32[1,1024]{1,0:T(1,128)S(1)} %spread.1.temper_ref, f32[1,1024]{1,0:T(1,128)S(1)} %bitcast.17, bf16[1024,1024]{1,0:T(8,128)(2,1)S(1)} %copy-done.9, ...), custom_call_target="tpu_custom_call" | custom-call | flops 30000001024 | bytes 1 | tf_op jit(solution)/shard_map/column/pallas_call | solution.py:365
  56.8 0.0 collective-permute-done.5.refs_2_
  56.8 2.9 %collective-permute-start.6 = (bf16[1,3,32,1024]{3,2,1,0:T(8,128)(2,1)S(1)}, bf16[1,3,32,1024]{3,2,1,0:T(8,128)(2,1)S(1)}, u32[]{:S(2)}, u32[]{:S(2)}) collective-permute-start(bf16[1,3,32,1024]{3,2,1,0:T(8,128)(2,1)S(1)} %get-tuple-element.53), channel_id=1, source_target_pairs={{0,24},{8,16},{16,8},{24,0},{1,25},{9,17},{17,9},{25,1},{2,26},{10... | collective-permute-start | bytes 589832 | tf_op jit(solution)/shard_map/ppermute | solution.py:264
  59.7 0.0 collective-permute-start.7
  59.7 1.5 %collective-permute-start.8 = (bf16[1,3,32,1024]{3,2,1,0:T(8,128)(2,1)S(1)}, bf16[1,3,32,1024]{3,2,1,0:T(8,128)(2,1)S(1)}, u32[]{:S(2)}, u32[]{:S(2)}) collective-permute-start(bf16[1,3,32,1024]{3,2,1,0:T(8,128)(2,1)S(1)} %get-tuple-element.55), channel_id=1, source_target_pairs={{0,8},{8,0},{16,24},{24,16},{1,9},{9,1},{17,25},{25,17},{2,10},{10... | collective-permute-start | bytes 589832 | tf_op jit(solution)/shard_map/ppermute | solution.py:264
  61.3 6.7 %along.1.acc_ref = f32[3,8,32,1024]{3,2,1,0:T(8,128)S(1)} custom-call(s32[1]{0:T(128)} %bitcast.place_ref, bf16[3,4,2,32,1024]{4,3,2,1,0:T(8,128)(2,1)S(1)} %bitcast.13, f32[1,1024]{1,0:T(1,128)S(1)} %bitcast.18, bf16[1024,1024]{1,0:T(8,128)(2,1)S(1)} %copy-done.2, bf16[8,3,64,256]{3,2,1,0:T(8,128)(2,1)S(1)} %bitcast.14, f32[1,1024]{1,0:T(1,128)S(1)} %bitcast.19, ...), custom_call_target="tpu_custom_call" | custom-call | bytes 1 | tf_op jit(solution)/shard_map/along/pallas_call | solution.py:385
  68.0 0.0 collective-permute-done.9.refs_0_
  68.0 0.0 collective-permute-done.10.refs_1_
  68.0 1.8 %finish.3.refs_2_ = bf16[3,4,2,32,1024]{4,3,2,1,0:T(8,128)(2,1)} custom-call(s32[1]{0:T(128)} %bitcast.place_ref, f32[3,8,32,1024]{3,2,1,0:T(8,128)S(1)} %along.1.acc_ref, bf16[1024,1024]{1,0:T(8,128)(2,1)S(1)} %copy-done, bf16[1,3,32,1024]{3,2,1,0:T(8,128)(2,1)S(1)} %collective-permute-done.9.refs_0_, ...), custom_call_target="tpu_custom_call" | custom-call | flops 30000001024 | bytes 1 | tf_op jit(solution)/shard_map/finish/pallas_call | solution.py:407
  69.9 1.7 %collective-permute-done.8.refs_0_ = bf16[1,3,32,1024]{3,2,1,0:T(8,128)(2,1)S(1)} collective-permute-done((bf16[1,3,32,1024]{3,2,1,0:T(8,128)(2,1)S(1)}, bf16[1,3,32,1024]{3,2,1,0:T(8,128)(2,1)S(1)}, u32[]{:S(2)}, u32[]{:S(2)}) %collective-permute-start.8) | collective-permute-done | bytes 196640 | tf_op jit(solution)/shard_map/ppermute | solution.py:264
  71.6 1.3 %finish.4.refs_2_ = bf16[3,4,2,32,1024]{4,3,2,1,0:T(8,128)(2,1)} custom-call(s32[1]{0:T(128)} %bitcast.place_ref, f32[3,8,32,1024]{3,2,1,0:T(8,128)S(1)} %along.1.acc_ref, bf16[1024,1024]{1,0:T(8,128)(2,1)S(1)} %copy-done, bf16[1,3,32,1024]{3,2,1,0:T(8,128)(2,1)S(1)} %collective-permute-done.8.refs_0_, ...), custom_call_target="tpu_custom_call", output_to_operand_aliasing={{}: (5, {})} | custom-call | bytes 1 | tf_op jit(solution)/shard_map/finish/pallas_call | solution.py:407
  72.9 0.0 collective-permute-done.6.refs_0_
  72.9 2.2 %collective-permute-done.7.refs_1_ = bf16[1,3,32,1024]{3,2,1,0:T(8,128)(2,1)S(1)} collective-permute-done((bf16[1,3,32,1024]{3,2,1,0:T(8,128)(2,1)S(1)}, bf16[1,3,32,1024]{3,2,1,0:T(8,128)(2,1)S(1)}, u32[]{:S(2)}, u32[]{:S(2)}) %collective-permute-start.7) | collective-permute-done | bytes 196640 | tf_op jit(solution)/shard_map/ppermute | solution.py:264
  75.1 1.3 %finish.5 = bf16[3,4,2,32,1024]{4,3,2,1,0:T(8,128)(2,1)} custom-call(s32[1]{0:T(128)} %bitcast.place_ref, f32[3,8,32,1024]{3,2,1,0:T(8,128)S(1)} %along.1.acc_ref, bf16[1024,1024]{1,0:T(8,128)(2,1)S(1)} %copy-done, bf16[1,3,32,1024]{3,2,1,0:T(8,128)(2,1)S(1)} %collective-permute-done.6.refs_0_, ...), custom_call_target="tpu_custom_call", output_to_operand_aliasing={{}: (5, {})} | custom-call | bytes 1 | tf_op jit(solution)/shard_map/finish/pallas_call | solution.py:407
  (23 shorter events, 0.0 us)
Async XLA Ops:
  0.0 7.1 %copy-start.1 = (bf16[3,256,1024]{2,1,0:T(8,128)(2,1)S(1)}, bf16[3,256,1024]{2,1,0:T(8,128)(2,1)}, u32[]{:S(2)}) copy-start(bf16[3,256,1024]{2,1,0:T(8,128)(2,1)} %param.12) | copy-start | bytes 4718596
  0.0 7.1 %copy-start.4 = (f32[1024]{0:T(1024)S(1)}, f32[1024]{0:T(1024)}, u32[]{:S(2)}) copy-start(f32[1024]{0:T(1024)} %param.13) | copy-start | bytes 12292
  2.1 21.9 %collective-permute-start.4 = (bf16[1,3,32,1024]{3,2,1,0:T(8,128)(2,1)}, bf16[1,3,32,1024]{3,2,1,0:T(8,128)(2,1)S(1)}, u32[]{:S(2)}, u32[]{:S(2)}) collective-permute-start(bf16[1,3,32,1024]{3,2,1,0:T(8,128)(2,1)} %get-tuple-element.61), channel_id=1, source_target_pairs={{0,24},{8,16},{16,8},{24,0},{1,25},{9,17},{17,9},{25,1},{2,26},{10... | collective-permute-start | bytes 589832 | tf_op jit(solution)/shard_map/ppermute | solution.py:264
  7.1 17.0 %collective-permute-start.3 = (bf16[1,3,32,1024]{3,2,1,0:T(8,128)(2,1)S(1)}, bf16[1,3,32,1024]{3,2,1,0:T(8,128)(2,1)S(1)}, u32[]{:S(2)}, u32[]{:S(2)}) collective-permute-start(bf16[1,3,32,1024]{3,2,1,0:T(8,128)(2,1)S(1)} %get-tuple-element.62), channel_id=1, source_target_pairs={{0,16},{8,24},{16,0},{24,8},{1,17},{9,25},{17,1},{25,9},{2,18},{10... | collective-permute-start | bytes 589832 | tf_op jit(solution)/shard_map/ppermute | solution.py:264
  7.1 1.8 %copy-start.6 = (bf16[1024,1024]{1,0:T(8,128)(2,1)S(1)}, bf16[1024,1024]{1,0:T(8,128)(2,1)}, u32[]{:S(2)}) copy-start(bf16[1024,1024]{1,0:T(8,128)(2,1)} %refs_7_.1) | copy-start | bytes 6291460
  7.1 2.4 %copy-start.7 = (bf16[1024,1024]{1,0:T(8,128)(2,1)S(1)}, bf16[1024,1024]{1,0:T(8,128)(2,1)}, u32[]{:S(2)}) copy-start(bf16[1024,1024]{1,0:T(8,128)(2,1)} %refs_8_.1) | copy-start | bytes 6291460
  8.4 7.4 %copy-start.15 = (bf16[1,3,32,1024]{3,2,1,0:T(8,128)(2,1)}, bf16[1,3,32,1024]{3,2,1,0:T(8,128)(2,1)S(1)}, u32[]{:S(2)}) copy-start(bf16[1,3,32,1024]{3,2,1,0:T(8,128)(2,1)S(1)} %get-tuple-element.44.refs_4_.refs_0_) | copy-start | bytes 589828
  8.4 16.5 %collective-permute-start = (bf16[2,3,32,1024]{3,2,1,0:T(8,128)(2,1)S(1)}, bf16[2,3,32,1024]{3,2,1,0:T(8,128)(2,1)S(1)}, u32[]{:S(2)}, u32[]{:S(2)}) collective-permute-start(bf16[2,3,32,1024]{3,2,1,0:T(8,128)(2,1)S(1)} %get-tuple-element.34.refs_1_), channel_id=1, source_target_pairs={{0,8},{8,0},{16,24},{24,16},{1,9},{9,1},{17,25},{25,17},{2,10},{10... | collective-permute-start | bytes 1179656 | tf_op jit(solution)/shard_map/ppermute | solution.py:264
  9.6 13.8 %copy-start.14 = (f32[16]{0:T(128)S(1)}, f32[16]{0:T(128)}, u32[]{:S(2)}) copy-start(f32[16]{0:T(128)} %temper_ref.1) | copy-start | bytes 196
  15.8 18.9 %all-to-all-start = ((bf16[8,192,256]{2,1,0:T(8,128)(2,1)}), bf16[8,192,256]{2,1,0:T(8,128)(2,1)}, u32[]{:S(2)}, u32[]{:S(2)}) async-start(bf16[8,192,256]{2,1,0:T(8,128)(2,1)} %bitcast.3), calls=%async_computation | async-start | bytes 1572864 | tf_op jit(solution)/shard_map/all_to_all | solution.py:338
  20.0 4.9 %copy-start.8 = (bf16[1024,1024]{1,0:T(8,128)(2,1)S(1)}, bf16[1024,1024]{1,0:T(8,128)(2,1)}, u32[]{:S(2)}) copy-start(bf16[1024,1024]{1,0:T(8,128)(2,1)} %wq_ref.5) | copy-start | bytes 6291460
  20.0 4.9 %copy-start.10 = (bf16[1024,1024]{1,0:T(8,128)(2,1)S(1)}, bf16[1024,1024]{1,0:T(8,128)(2,1)}, u32[]{:S(2)}) copy-start(bf16[1024,1024]{1,0:T(8,128)(2,1)} %wk_ref.3) | copy-start | bytes 6291460
  20.1 4.9 %copy-start.12 = (bf16[1024,1024]{1,0:T(8,128)(2,1)S(1)}, bf16[1024,1024]{1,0:T(8,128)(2,1)}, u32[]{:S(2)}) copy-start(bf16[1024,1024]{1,0:T(8,128)(2,1)} %wv_ref.3) | copy-start | bytes 6291460
  20.1 26.6 %collective-permute-start.1 = (bf16[1,3,32,1024]{3,2,1,0:T(8,128)(2,1)}, bf16[1,3,32,1024]{3,2,1,0:T(8,128)(2,1)}, u32[]{:S(2)}, u32[]{:S(2)}) collective-permute-start(bf16[1,3,32,1024]{3,2,1,0:T(8,128)(2,1)} %get-tuple-element.40.refs_6_), channel_id=1, source_target_pairs={{0,24},{8,16},{16,8},{24,0},{1,25},{9,17},{17,9},{25,1},{2,26},{10... | collective-permute-start | bytes 589832 | tf_op jit(solution)/shard_map/ppermute | solution.py:264
  23.4 26.9 %collective-permute-start.2 = (bf16[1,3,32,1024]{3,2,1,0:T(8,128)(2,1)}, bf16[1,3,32,1024]{3,2,1,0:T(8,128)(2,1)}, u32[]{:S(2)}, u32[]{:S(2)}) collective-permute-start(bf16[1,3,32,1024]{3,2,1,0:T(8,128)(2,1)} %get-tuple-element.41.refs_5_), channel_id=1, source_target_pairs={{0,16},{8,24},{16,0},{24,8},{1,17},{9,25},{17,1},{25,9},{2,18},{10... | collective-permute-start | bytes 589832 | tf_op jit(solution)/shard_map/ppermute | solution.py:264
  30.4 26.4 %collective-permute-start.5 = (bf16[1,3,32,1024]{3,2,1,0:T(8,128)(2,1)S(1)}, bf16[1,3,32,1024]{3,2,1,0:T(8,128)(2,1)S(1)}, u32[]{:S(2)}, u32[]{:S(2)}) collective-permute-start(bf16[1,3,32,1024]{3,2,1,0:T(8,128)(2,1)S(1)} %get-tuple-element.52), channel_id=1, source_target_pairs={{0,8},{8,0},{16,24},{24,16},{1,9},{9,1},{17,25},{25,17},{2,10},{10... | collective-permute-start | bytes 589832 | tf_op jit(solution)/shard_map/ppermute | solution.py:264
  32.3 35.7 %collective-permute-start.9 = (bf16[1,3,32,1024]{3,2,1,0:T(8,128)(2,1)S(1)}, bf16[1,3,32,1024]{3,2,1,0:T(8,128)(2,1)S(1)}, u32[]{:S(2)}, u32[]{:S(2)}) collective-permute-start(bf16[1,3,32,1024]{3,2,1,0:T(8,128)(2,1)S(1)} %get-tuple-element.57), channel_id=1, source_target_pairs={{0,24},{8,16},{16,8},{24,0},{1,25},{9,17},{17,9},{25,1},{2,26},{10... | collective-permute-start | bytes 589832 | tf_op jit(solution)/shard_map/ppermute | solution.py:264
  34.2 16.1 %copy-start.16 = (bf16[1,3,32,1024]{3,2,1,0:T(8,128)(2,1)S(1)}, bf16[1,3,32,1024]{3,2,1,0:T(8,128)(2,1)}, u32[]{:S(2)}) copy-start(bf16[1,3,32,1024]{3,2,1,0:T(8,128)(2,1)} %copy-done.15) | copy-start | bytes 589828
  34.2 33.8 %collective-permute-start.10 = (bf16[1,3,32,1024]{3,2,1,0:T(8,128)(2,1)S(1)}, bf16[1,3,32,1024]{3,2,1,0:T(8,128)(2,1)S(1)}, u32[]{:S(2)}, u32[]{:S(2)}) collective-permute-start(bf16[1,3,32,1024]{3,2,1,0:T(8,128)(2,1)S(1)} %get-tuple-element.58), channel_id=1, source_target_pairs={{0,16},{8,24},{16,0},{24,8},{1,17},{9,25},{17,1},{25,9},{2,18},{10... | collective-permute-start | bytes 589832 | tf_op jit(solution)/shard_map/ppermute | solution.py:264
  34.7 15.6 %copy-start.9 = (bf16[1024,1024]{1,0:T(8,128)(2,1)S(1)}, bf16[1024,1024]{1,0:T(8,128)(2,1)}, u32[]{:S(2)}) copy-start(bf16[1024,1024]{1,0:T(8,128)(2,1)} %wq_ref.5) | copy-start | bytes 6291460
  34.7 15.6 %copy-start.11 = (bf16[1024,1024]{1,0:T(8,128)(2,1)S(1)}, bf16[1024,1024]{1,0:T(8,128)(2,1)}, u32[]{:S(2)}) copy-start(bf16[1024,1024]{1,0:T(8,128)(2,1)} %wk_ref.3) | copy-start | bytes 6291460
  34.7 15.6 %copy-start.13 = (bf16[1024,1024]{1,0:T(8,128)(2,1)S(1)}, bf16[1024,1024]{1,0:T(8,128)(2,1)}, u32[]{:S(2)}) copy-start(bf16[1024,1024]{1,0:T(8,128)(2,1)} %wv_ref.3) | copy-start | bytes 6291460
  50.3 11.0 %copy-start.2 = (bf16[1024,1024]{1,0:T(8,128)(2,1)S(1)}, bf16[1024,1024]{1,0:T(8,128)(2,1)}, u32[]{:S(2)}) copy-start(bf16[1024,1024]{1,0:T(8,128)(2,1)} %wq_ref.3) | copy-start | bytes 6291460
  50.3 11.0 %copy-start.3 = (bf16[1024,1024]{1,0:T(8,128)(2,1)S(1)}, bf16[1024,1024]{1,0:T(8,128)(2,1)}, u32[]{:S(2)}) copy-start(bf16[1024,1024]{1,0:T(8,128)(2,1)} %wo_ref.4) | copy-start | bytes 6291460
  50.3 11.0 %copy-start.5 = (f32[1024]{0:T(1024)S(1)}, f32[1024]{0:T(1024)}, u32[]{:S(2)}) copy-start(f32[1024]{0:T(1024)} %param.18) | copy-start | bytes 12292
  56.8 16.1 %collective-permute-start.6 = (bf16[1,3,32,1024]{3,2,1,0:T(8,128)(2,1)S(1)}, bf16[1,3,32,1024]{3,2,1,0:T(8,128)(2,1)S(1)}, u32[]{:S(2)}, u32[]{:S(2)}) collective-permute-start(bf16[1,3,32,1024]{3,2,1,0:T(8,128)(2,1)S(1)} %get-tuple-element.53), channel_id=1, source_target_pairs={{0,24},{8,16},{16,8},{24,0},{1,25},{9,17},{17,9},{25,1},{2,26},{10... | collective-permute-start | bytes 589832 | tf_op jit(solution)/shard_map/ppermute | solution.py:264
  59.7 15.4 %collective-permute-start.7 = (bf16[1,3,32,1024]{3,2,1,0:T(8,128)(2,1)S(1)}, bf16[1,3,32,1024]{3,2,1,0:T(8,128)(2,1)S(1)}, u32[]{:S(2)}, u32[]{:S(2)}) collective-permute-start(bf16[1,3,32,1024]{3,2,1,0:T(8,128)(2,1)S(1)} %get-tuple-element.54), channel_id=1, source_target_pairs={{0,16},{8,24},{16,0},{24,8},{1,17},{9,25},{17,1},{25,9},{2,18},{10... | collective-permute-start | bytes 589832 | tf_op jit(solution)/shard_map/ppermute | solution.py:264
  59.7 11.8 %collective-permute-start.8 = (bf16[1,3,32,1024]{3,2,1,0:T(8,128)(2,1)S(1)}, bf16[1,3,32,1024]{3,2,1,0:T(8,128)(2,1)S(1)}, u32[]{:S(2)}, u32[]{:S(2)}) collective-permute-start(bf16[1,3,32,1024]{3,2,1,0:T(8,128)(2,1)S(1)} %get-tuple-element.55), channel_id=1, source_target_pairs={{0,8},{8,0},{16,24},{24,16},{1,9},{9,1},{17,25},{25,17},{2,10},{10... | collective-permute-start | bytes 589832 | tf_op jit(solution)/shard_map/ppermute | solution.py:264
  61.3 6.8 %copy-start = (bf16[1024,1024]{1,0:T(8,128)(2,1)S(1)}, bf16[1024,1024]{1,0:T(8,128)(2,1)}, u32[]{:S(2)}) copy-start(bf16[1024,1024]{1,0:T(8,128)(2,1)} %wo_ref.7) | copy-start | bytes 6291460
